TPU v7x, 32 devices: a whole 2x2x4 slice. The times are simulated.
32 devices in a mesh: batch: 4 (over y, core), tensor: 8 (over z, x).
Axes of the slice: x: 2, y: 2, z: 4, core: 2. Of those that a mesh axis runs over, the one named last changes fastest.
Arguments:
- tokens: bfloat16 [16384, 1024], P(('batch', 'tensor')), may hold values from -6 to 6
- gain_attn: float32 [1024], replicated, may hold values from 0.1 to 1.9
- w_qkv: bfloat16 [1024, 1536], P('batch', 'tensor'), may hold values from -0.1875 to 0.1875
- w_attn_out: bfloat16 [1024, 512], P('batch', 'tensor'), may hold values from -0.25 to 0.25
- kv_cache: bfloat16 [512, 128, 1024], P('batch', None, 'tensor'), may hold values from -192 to 192
- page_table: int32 [4, 128], P('batch'), may hold values from 0 to 127, each once within a row
- cached_lengths: int32 [16], P('batch'), may hold values from 1 to 4096, 16384 in all
- gain_moe: float32 [1024], replicated, may hold values from 0.1 to 1.9
- w_router: bfloat16 [1024, 8], replicated, may hold values from -0.1875 to 0.1875
- routes: int32 [16384, 2], P(('batch', 'tensor')), may hold values from 0 to 7, all different within a row; in each aligned block of 512 rows (0 to 511, 512 to 1023, ...) at most 160 rows name the same one
- w_in: bfloat16 [8, 1024, 5632], P('tensor'), may hold values from -0.1875 to 0.1875
- w_out: bfloat16 [8, 2816, 1024], P('tensor'), may hold values from -0.109375 to 0.109375
Outputs:
- mixed: bfloat16 [16384, 1024], P(('batch', 'tensor'))
Inputs may be any that keep to these rules, and one draw needn't show every extreme that they name: `page_table`: each row lists all 128 pages of one batch index's pool once; local request r of that batch index reads its cached tokens from entries r * 32 to (r + 1) * 32 - 1 in order. `cached_lengths`: they sum to 16384. `routes`: a token's 2 experts differ; in the rows of one device (512 aligned rows) no expert is named by more than 160 rows, a bound that some block reaches.
All inputs are finite; a program needn't handle non-finite values. No bound on the sum of `cached_lengths` on one device may be relied on, other than what follows from the above.
Results may differ from a plain program's by a relative error of at most 0.012.
Values may be sent and summed in bfloat16 or wider, within the bound.
No kernel may reach another device: no remote copies, remote signals or barrier semaphores. Data moves between devices by JAX's collectives and lax.ppermute only.
A program may use at most 128 MiB of HBM per device.

v0:
```python
import math

import jax
import jax.numpy as jnp
from jax import lax
from jax.sharding import PartitionSpec as P

HD = 64


EPSILON = 1e-06
NEGATIVE = -1e30
CONTRACT = (((1,), (1,)), ((), ()))


def rms_norm(values, gain):
    values = values.astype(jnp.float32)
    mean_square = jnp.mean(values * values, axis=-1, keepdims=True)
    return values * lax.rsqrt(mean_square + EPSILON) * gain


def head_attention(queries, cache_keys, cache_values, span_keys, span_values, length):
    span = queries.shape[0]
    cache_max = cache_keys.shape[0]
    scale = 1.0 / math.sqrt(queries.shape[1])
    keys = jnp.concatenate([cache_keys, span_keys], axis=0)
    values_all = jnp.concatenate([cache_values, span_values], axis=0)
    height = min(512, span)
    column = jnp.arange(cache_max + span, dtype=jnp.int32)

    def one_block(first):
        query_block = lax.dynamic_slice_in_dim(queries, first, height, 0)
        scores = (
            lax.dot_general(query_block, keys, CONTRACT, preferred_element_type=jnp.float32) * scale
        )
        line = first + jnp.arange(height, dtype=jnp.int32)
        visible = jnp.where(
            column[None, :] < cache_max,
            column[None, :] < length,
            column[None, :] - cache_max <= line[:, None],
        )
        scores = jnp.where(visible, scores, NEGATIVE)
        top_score = jnp.max(scores, axis=1, keepdims=True)
        weights = jnp.exp(scores - top_score)
        weights = (weights / jnp.sum(weights, axis=1, keepdims=True)).astype(jnp.bfloat16)
        return jnp.dot(weights, values_all, preferred_element_type=jnp.float32).astype(jnp.bfloat16)

    outcome = lax.map(one_block, jnp.arange(span // height, dtype=jnp.int32) * height)
    return outcome.reshape(span, queries.shape[1])


def body(
    tokens,
    gain_attn,
    w_qkv,
    w_attn_out,
    kv_cache,
    page_table,
    cached_lengths,
    gain_moe,
    w_router,
    routes,
    w_in,
    w_out,
):
    normed = rms_norm(tokens, gain_attn).astype(jnp.bfloat16)
    full_qkv, out_columns = (
        lax.all_gather(w_qkv, "batch", axis=0, tiled=True),
        lax.all_gather(w_attn_out, "batch", axis=0, tiled=True),
    )
    projected = jnp.dot(
        lax.all_gather(normed, "tensor", axis=0, tiled=True),
        full_qkv,
        preferred_element_type=jnp.float32,
    ).astype(jnp.bfloat16)
    requests = cached_lengths.shape[0]
    span = projected.shape[0] // requests
    local_heads = out_columns.shape[1] // HD
    per_request = kv_cache.shape[0] // requests

    def one_request(request):
        block = lax.dynamic_slice_in_dim(projected, request * span, span, 0)
        pages = lax.dynamic_slice_in_dim(page_table[0], request * per_request, per_request, 0)
        cached = kv_cache[pages].reshape(per_request * kv_cache.shape[1], kv_cache.shape[2])
        length = cached_lengths[request]
        outputs = [
            head_attention(
                block[:, 0:HD],
                cached[:, 0:HD],
                cached[:, HD : 2 * HD],
                block[:, HD : 2 * HD],
                block[:, 2 * HD : 3 * HD],
                length,
            )
        ]
        return jnp.concatenate(outputs, axis=1)

    attended = lax.map(one_request, jnp.arange(requests, dtype=jnp.int32)).reshape(
        projected.shape[0], local_heads * HD
    )
    rows_here = tokens.shape[0]
    portion = lax.slice_in_dim(attended, 0, rows_here * lax.axis_size("tensor"), axis=0)
    projection = lax.psum_scatter(
        lax.dot_general(portion, out_columns, CONTRACT, preferred_element_type=jnp.float32),
        "tensor",
        scatter_dimension=0,
        tiled=True,
    )
    state = tokens.astype(jnp.float32) + projection
    normed_moe = rms_norm(state, gain_moe).astype(jnp.bfloat16)
    logits = jnp.dot(normed_moe, w_router, preferred_element_type=jnp.float32)
    experts = w_router.shape[1]
    top_count = routes.shape[1]
    onehot = (routes[:, :, None] == jnp.arange(experts, dtype=jnp.int32)[None, None, :]).astype(
        jnp.int32
    )
    picked = jnp.sum(onehot.astype(jnp.float32) * logits[:, None, :], axis=2)
    squashed = jax.nn.sigmoid(picked)
    gates = squashed / jnp.sum(squashed, axis=1, keepdims=True)
    flat_hits = onehot.reshape(rows_here * top_count, experts)
    before = jnp.cumsum(flat_hits, axis=0) - flat_hits
    slots = jnp.sum(before * flat_hits, axis=1).reshape(rows_here, top_count)
    capacity = max(2, (5 * rows_here * top_count + 4 * experts - 1) // (4 * experts))
    position = routes * capacity + slots
    slot_ids = jnp.arange(experts * capacity, dtype=jnp.int32)
    placing = jnp.any(slot_ids[:, None, None] == position[None, :, :], axis=2).astype(jnp.bfloat16)
    buffer = jnp.dot(placing, normed_moe, preferred_element_type=jnp.float32).astype(jnp.bfloat16)
    lanes = lax.axis_size("tensor")
    buffer = buffer.reshape(lanes, w_in.shape[0], capacity, normed_moe.shape[1])
    width_ff = w_out.shape[1]
    inner = jnp.einsum(
        "sekd,edf->sekf",
        lax.all_to_all(buffer, "tensor", split_axis=0, concat_axis=0, tiled=True),
        w_in,
        preferred_element_type=jnp.float32,
    )
    active = (jax.nn.gelu(inner[..., :width_ff], approximate=True) * inner[..., width_ff:]).astype(
        jnp.bfloat16
    )
    results = jnp.einsum(
        "sekf,efd->sekd", active, w_out, preferred_element_type=jnp.float32
    ).astype(jnp.bfloat16)
    returned = lax.all_to_all(results, "tensor", split_axis=0, concat_axis=0, tiled=True).reshape(
        experts * capacity, normed_moe.shape[1]
    )
    mixed = state
    for rank in range(top_count):
        pick = (position[:, rank : rank + 1] == slot_ids[None, :]).astype(jnp.bfloat16)
        mixed = mixed + gates[:, rank : rank + 1] * jnp.dot(
            pick, returned, preferred_element_type=jnp.float32
        )
    return mixed.astype(jnp.bfloat16)


def solution(mesh):
    in_specs = (
        P(("batch", "tensor"), None),
        P(),
        P("batch", "tensor"),
        P("batch", "tensor"),
        P("batch", None, "tensor"),
        P("batch", None),
        P("batch"),
        P(),
        P(),
        P(("batch", "tensor"), None),
        P("tensor", None, None),
        P("tensor", None, None),
    )
    out_specs = P(("batch", "tensor"), None)
    return jax.shard_map(body, mesh=mesh, in_specs=in_specs, out_specs=out_specs, check_vma=False)
```

profile of v0, /device:TPU:9, one launch (start us, length us, event | category | flops | bytes accessed | tf_op | source)
XLA Modules:
  0.0 762.9 jit_solution(7300272450513381690)
XLA Ops:
  6.5 1.5 fusion.27
  8.1 2.6 fusion.29
  10.8 6.4 all_gather.11
  17.2 6.6 all_gather.10
  23.8 110.9 %all-gather.2.cloned.1.call-done = bf16[4096,1024]{1,0:T(8,128)(2,1)} async-done(((bf16[512,1024]{1,0:T(8,128)(2,1)}), bf16[4096,1024]{1,0:T(8,128)(2,1)}) %all-gather.2.cloned.1.call-update) | async-done | bytes 8388624 | tf_op jit(solution)/shard_map/all_gather | solution.py:72
  134.7 7.5 convolution_convert_fusion
  142.8 144.1 %while.34 = (s32[]{:T(128)}, bf16[4,1024,64]{2,1,0:T(8,128)(2,1)}, s32[4]{0:T(128)}, bf16[4096,192]{0,1:T(8,128)(2,1)}, s32[1,128]{1,0:T(1,128)}, /*index=5*/bf1...) while((s32[]{:T(128)}, bf16[4,1024,64]{2,1,0:T(8,128)(2,1)}, ...), condition=%wide.region_6.7_spmd, body=%wide.region_1.6_spmd.sunk | while | flops 699973248 | bytes 42679420 | solution.py:98
  142.8 1.3 dynamic_slice.55
  150.9 2.9 gather_fusion
  154.7 23.3 %while.35 = (s32[]{:T(128)}, bf16[2,512,64]{1,2,0:T(8,128)(2,1)S(1)}, s32[]{:T(128)}, s32[2]{0:T(128)}, bf16[1024,64]{0,1:T(8,128)(2,1)S(1)}, /*index=5*/bf16[51...) while((s32[]{:T(128)}, ...), condition=%wide.region_5.5_spmd.clone.clone, body=%wide.region_2.4_spmd.clone.clone.sunk | while | flops 697350656 | bytes 33892520 | solution.py:48
  154.7 1.2 dynamic_slice.58
  159.2 2.9 fusion.79
  162.1 1.6 fusion.80
  163.7 2.6 fusion.81
  166.3 1.2 dynamic_slice.58
  170.9 2.9 fusion.79
  173.7 1.6 fusion.80
  175.3 2.6 fusion.81
  178.9 1.3 dynamic_slice.55
  186.9 2.9 gather_fusion
  190.7 23.3 %while.35 = (s32[]{:T(128)}, bf16[2,512,64]{1,2,0:T(8,128)(2,1)S(1)}, s32[]{:T(128)}, s32[2]{0:T(128)}, bf16[1024,64]{0,1:T(8,128)(2,1)S(1)}, /*index=5*/bf16[51...) while((s32[]{:T(128)}, ...), condition=%wide.region_5.5_spmd.clone.clone, body=%wide.region_2.4_spmd.clone.clone.sunk | while | flops 697350656 | bytes 33892520 | solution.py:48
  190.7 1.2 dynamic_slice.58
  195.2 2.9 fusion.79
  198.1 1.6 fusion.80
  199.7 2.6 fusion.81
  202.4 1.2 dynamic_slice.58
  206.9 2.9 fusion.79
  209.7 1.6 fusion.80
  211.3 2.6 fusion.81
  214.9 1.3 dynamic_slice.55
  222.9 2.9 gather_fusion
  226.7 23.3 %while.35 = (s32[]{:T(128)}, bf16[2,512,64]{1,2,0:T(8,128)(2,1)S(1)}, s32[]{:T(128)}, s32[2]{0:T(128)}, bf16[1024,64]{0,1:T(8,128)(2,1)S(1)}, /*index=5*/bf16[51...) while((s32[]{:T(128)}, ...), condition=%wide.region_5.5_spmd.clone.clone, body=%wide.region_2.4_spmd.clone.clone.sunk | while | flops 697350656 | bytes 33892520 | solution.py:48
  226.7 1.2 dynamic_slice.58
  231.2 2.9 fusion.79
  234.1 1.6 fusion.80
  235.7 2.6 fusion.81
  238.4 1.2 dynamic_slice.58
  242.9 2.9 fusion.79
  245.7 1.6 fusion.80
  247.3 2.6 fusion.81
  250.9 1.3 dynamic_slice.55
  258.9 2.9 gather_fusion
  262.7 23.3 %while.35 = (s32[]{:T(128)}, bf16[2,512,64]{1,2,0:T(8,128)(2,1)S(1)}, s32[]{:T(128)}, s32[2]{0:T(128)}, bf16[1024,64]{0,1:T(8,128)(2,1)S(1)}, /*index=5*/bf16[51...) while((s32[]{:T(128)}, ...), condition=%wide.region_5.5_spmd.clone.clone, body=%wide.region_2.4_spmd.clone.clone.sunk | while | flops 697350656 | bytes 33892520 | solution.py:48
  262.7 1.2 dynamic_slice.58
  267.2 2.9 fusion.79
  270.1 1.6 fusion.80
  271.7 2.6 fusion.81
  278.9 2.9 fusion.79
  281.7 1.6 fusion.80
  283.3 2.6 fusion.81
  286.9 9.3 %fusion.49 = f32[4096,1024]{1,0:T(8,128)} fusion(bf16[4096,64]{1,0:T(8,128)(2,1)} %bitcast.117, bf16[1024,64]{0,1:T(8,128)(2,1)S(1)} %copy-done.5), kind=kOutput, calls=%fused_computation.87 | convolution fusion | flops 536870912 | bytes 17432576 | tf_op jit(solution)/shard_map/dot_general | solution.py:104
  297.4 2.5 reduce-window.6
  300.7 2.4 fusion.23
  303.1 274.4 %reduce-scatter.2.cloned.1.call-done = f32[512,1024]{1,0:T(8,128)} async-done(((f32[4096,1024]{1,0:T(8,128)}), f32[512,1024]{1,0:T(8,128)}) %reduce-scatter.2.cloned.1.call-update) | async-done | bytes 2097168 | tf_op jit(solution)/shard_map/reduce_scatter | solution.py:103
  577.5 2.1 multiply_reduce_fusion
  580.7 1.5 convolution_convert_fusion.1
  582.3 62.7 %all_to_all.10 = bf16[8,1,160,1024]{3,2,1,0:T(8,128)(2,1)S(1)} all-to-all(bf16[8,1,160,1024]{3,2,1,0:T(8,128)(2,1)S(1)} %bitcast.116), channel_id=1, replica_groups=mesh['batch'=4,'tensor'=8] {'tensor'}, dimensions={0} | all-to-all | bytes 5242880 | tf_op jit(solution)/shard_map/all_to_all | solution.py:133
  645.0 23.2 %convolution_bitcast_fusion = f32[8,1,160,5632]{3,2,0,1:T(8,128)} fusion(bf16[1,1024,5632]{2,1,0:T(8,128)(2,1)} %param.26, bf16[8,1,160,1024]{3,2,1,0:T(8,128)(2,1)S(1)} %all_to_all.10), kind=kOutput, calls=%fused_computation.26 | convolution fusion | flops 14763950080 | bytes 42991616 | tf_op jit(solution)/shard_map/sekd,edf->sekf/dot_general | solution.py:131
  668.2 17.2 %convert_bitcast_fusion = bf16[8,1,160,1024]{3,2,1,0:T(8,128)(2,1)} fusion(bf16[1,2816,1024]{2,1,0:T(8,128)(2,1)} %param.27, f32[8,1,160,5632]{3,2,0,1:T(8,128)} %convolution_bitcast_fusion), kind=kOutput, calls=%fused_computation.49 | convolution fusion | flops 7419330560 | bytes 37224448 | tf_op jit(solution)/shard_map/sekf,efd->sekd/dot_general | solution.py:140
  685.4 5.1 all-to-all-start.1
  690.6 1.6 fusion.50
  692.3 56.0 %all-to-all-done.1 = bf16[8,1,160,1024]{3,2,1,0:T(8,128)(2,1)} async-done(((bf16[8,1,160,1024]{3,2,1,0:T(8,128)(2,1)}), bf16[8,1,160,1024]{3,2,1,0:T(8,128)(2,1)}, u32[]{:S(2)}, u32[]{:S(2)}) %all-to-all-start.1) | async-done | bytes 2621472 | tf_op jit(solution)/shard_map/all_to_all | solution.py:143
  748.3 3.3 fusion.25
  751.6 4.5 add_convert_fusion
  (134 shorter events, 39.1 us)
Async XLA Ops:
  6.5 684.0 %copy-start = (bf16[1024,8]{0,1:T(8,128)(2,1)S(1)}, bf16[1024,8]{0,1:T(8,128)(2,1)}, u32[]{:S(2)}) copy-start(bf16[1024,8]{0,1:T(8,128)(2,1)} %param.24) | copy-start | bytes 49156
  6.5 4.3 copy-start.8
  6.5 10.7 %copy-start.6 = (bf16[256,192]{0,1:T(8,128)(2,1)S(1)}, bf16[256,192]{0,1:T(8,128)(2,1)}, u32[]{:S(2)}) copy-start(bf16[256,192]{0,1:T(8,128)(2,1)} %param.18) | copy-start | bytes 294916
  6.5 128.2 %all-gather.2.cloned.1.call-start = ((), (), s32[]{:S(2)}) async-start(), calls=%async_computation.3 | async-start | bytes 9437184 | tf_op jit(solution)/shard_map/all_gather | solution.py:72
  10.7 566.8 %reduce-scatter.2.cloned.1.call-start = ((), (), s32[]{:S(2)}) async-start(), calls=%async_computation.4 | async-start | bytes 18874368 | tf_op jit(solution)/shard_map/reduce_scatter | solution.py:103
  142.8 144.1 %copy-start.5 = (bf16[1024,64]{0,1:T(8,128)(2,1)S(1)}, bf16[1024,64]{0,1:T(8,128)(2,1)}, u32[]{:S(2)}) copy-start(bf16[1024,64]{0,1:T(8,128)(2,1)} %all_gather.11) | copy-start | bytes 393220
  296.2 0.7 copy-start.7
  296.8 280.7 %copy-start.1 = (bf16[512,1024]{1,0:T(8,128)(2,1)S(1)}, bf16[512,1024]{1,0:T(8,128)(2,1)}, u32[]{:S(2)}) copy-start(bf16[512,1024]{1,0:T(8,128)(2,1)} %param.16) | copy-start | bytes 3145732
  297.0 282.6 %copy-start.9 = (f32[1024]{0:T(1024)S(1)}, f32[1024]{0:T(1024)}, u32[]{:S(2)}) copy-start(f32[1024]{0:T(1024)} %param.23) | copy-start | bytes 12292
  577.5 2.2 copy-start.2
  579.6 1.1 copy-start.4
  580.7 1.5 copy-start.3
  685.4 62.8 %all-to-all-start.1 = ((bf16[8,1,160,1024]{3,2,1,0:T(8,128)(2,1)}), bf16[8,1,160,1024]{3,2,1,0:T(8,128)(2,1)}, u32[]{:S(2)}, u32[]{:S(2)}) async-start(bf16[8,1,160,1024]{3,2,1,0:T(8,128)(2,1)} %convert_bitcast_fusion), calls=%async_computation.2 | async-start | bytes 5242880 | tf_op jit(solution)/shard_map/all_to_all | solution.py:143
Sparse Core Ops, SparseCore 0:
  10.8 123.8 all-gather.1
  296.3 281.1 reduce-scatter.1
where the time goes:
time: 768 us; the launch traced here: 763 us
  waiting for transfers between devices  441 us (57%)
  matrix products  112 us (15%)
  blocking collectives  75.7 us (10%)
  local copies, waits for them, and re-layouts  47.3 us (6%)
  other arithmetic  41.1 us (5%)
  loops' own time  26.6 us (3%)
  between operations  13.6 us (2%)
    reduce_scatter x1, waiting for transfers between devices, body(): lax.psum_scatter(lax.dot_general(portion, out_columns, CONTRACT, preferre...  274 us
    all_gather x1, waiting for transfers between devices, body(): lax.all_gather(normed, 'tensor', axis=0, tiled=True)  111 us
    all_to_all x1, blocking collectives, body(): lax.all_to_all(buffer, 'tensor', split_axis=0, concat_axis=0, tiled=True)  62.7 us
    all_to_all x1, waiting for transfers between devices, body(): lax.all_to_all(results, 'tensor', split_axis=0, concat_axis=0, tiled=True)  56 us
    dot_general x1, matrix products, body(): jnp.einsum('sekd,edf->sekf', lax.all_to_all(buffer, 'tensor', split_axis=...  23.2 us
    dot_general x8, matrix products, one_block(): lax.dot_general(query_block, keys, CONTRACT, preferred_element_type=jnp.f...  22.9 us
    dot_general x8, matrix products, one_block(): jnp.dot(weights, values_all, preferred_element_type=jnp.float32)  21.2 us
    dot_general x1, matrix products, body(): jnp.einsum('sekf,efd->sekd', active, w_out, preferred_element_type=jnp.fl...  17.2 us
  transfers between devices with their start and end apart: 3, of which 3 were waited for; matrix products, arithmetic and copies ran while one was open for 1% of the time, Pallas kernels for 0%

commit v1 on v0

v1 whole, which is shorter than its diff:
```python
import functools
import math

import jax
import jax.numpy as jnp
from jax import lax
from jax.experimental import pallas as pl
from jax.experimental.pallas import tpu as pltpu
from jax.sharding import PartitionSpec as P

HD = 64
EXT = 16
EPSILON = 1e-06
NEGATIVE = -1e30
F32, BF16 = jnp.float32, jnp.bfloat16
NT = (((1,), (1,)), ((), ()))
VMEM_LIMIT = 52 * 1024 * 1024
AXES = ("batch", "tensor")


def dot(a, b, dims=(((1,), (0,)), ((), ()))):
    return lax.dot_general(a, b, dims, preferred_element_type=F32)


def vmem(count):
    return [pl.BlockSpec(memory_space=pltpu.VMEM)] * count


def smem(count):
    return [pl.BlockSpec(memory_space=pltpu.SMEM)] * count


def params():
    return pltpu.CompilerParams(vmem_limit_bytes=VMEM_LIMIT)


def send(value, mask, lanes, groups):
    total = lanes * groups
    return lax.ppermute(value, AXES, [(i, i ^ mask) for i in range(total)])


def gather_xor(piece, lanes, groups):
    low = max(1, lanes // 4)
    high = [piece] + [send(piece, s, lanes, groups) for s in range(low, lanes, low)]
    block = jnp.stack(high)
    plane = {}
    for j in range(0, groups, 2):
        for s in range(low):
            mask = j * lanes + s
            plane[(j, s)] = block if mask == 0 else send(block, mask, lanes, groups)
    rows = [jnp.stack([plane[(j, s)] for s in range(low)], axis=1) for j in range(0, groups, 2)]
    half = jnp.stack(rows).reshape((groups // 2, lanes) + piece.shape)
    other = send(half, lanes, lanes, groups)
    return jnp.stack([half, other], axis=1).reshape((groups, lanes) + piece.shape)


def softmax_step(scores, values_ext, m, acc):
    top = jnp.maximum(m, jnp.max(scores, axis=0, keepdims=True))
    weights = jnp.exp(scores - top).astype(BF16)
    return top, acc * jnp.exp(m - top) + dot(values_ext, weights)


def ones_rows(keys):
    return jnp.ones((EXT, keys), BF16)


def cached_kernel(lanes, requests, span_devs, block_pages, *refs):
    info, lengths, table = refs[:3]
    q_refs = refs[3 : 3 + lanes]
    kv_ref = refs[3 + lanes]
    out_refs = refs[4 + lanes : 4 + 2 * lanes]
    q_all, m_ref, acc_ref, out_all = refs[4 + 2 * lanes :]
    page = kv_ref.shape[1]
    pages = table.shape[1] // requests
    rows = q_refs[0].shape[1]
    queries = rows * span_devs
    keys = block_pages * page
    tile = min(256, queries)
    for k in range(requests):
        for i in range(span_devs):
            q_all[k, 0:HD, i * rows : (i + 1) * rows] = q_refs[k * span_devs + i][...]
        q_all[k, HD : 2 * HD, :] = jnp.zeros((HD, queries), BF16)
    first = info[0] // span_devs

    def one_request(k, carry):
        request = jnp.bitwise_xor(first, k)
        length = lengths[request]
        m_ref[...] = jnp.full((1, queries), NEGATIVE, F32)
        acc_ref[...] = jnp.zeros((HD + EXT, queries), F32)

        def block(j, masked):
            parts = [
                kv_ref[
                    table[0, request * pages + jnp.minimum(j * block_pages + n, pages - 1)]
                ]
                for n in range(block_pages)
            ]
            both = jnp.concatenate(parts, axis=0)
            values = jnp.concatenate([both.T[HD : 2 * HD], ones_rows(keys)], axis=0)
            for t in range(0, queries, tile):
                at = pl.ds(t, tile)
                scores = dot(both, q_all[k, :, at])
                if masked:
                    position = j * keys + lax.broadcasted_iota(jnp.int32, scores.shape, 0)
                    scores = jnp.where(position < length, scores, NEGATIVE)
                top, acc = softmax_step(scores, values, m_ref[:, at], acc_ref[:, at])
                m_ref[:, at] = top
                acc_ref[:, at] = acc

        whole = length // keys

        def step(j, c):
            block(j, False)
            return c

        lax.fori_loop(0, whole, step, 0)

        @pl.when(whole * keys < length)
        def _():
            block(whole, True)

        total = acc_ref[HD : HD + 1, :]
        lse = m_ref[...] + jnp.log(total)
        hi = lse.astype(BF16).astype(F32)
        mid = (lse - hi).astype(BF16).astype(F32)
        lo = lse - hi - mid
        at_row = lax.broadcasted_iota(jnp.int32, (EXT, queries), 0)
        stats = jnp.where(
            at_row == 0, hi, jnp.where(at_row == 1, mid, jnp.where(at_row == 2, lo, 0.0))
        )
        out_all[k, 0:HD, :] = (acc_ref[0:HD, :] / total).astype(BF16)
        out_all[k, HD : HD + EXT, :] = stats.astype(BF16)
        return carry

    lax.fori_loop(0, requests, one_request, 0)
    for k in range(requests):
        for i in range(span_devs):
            out_refs[k * span_devs + i][...] = out_all[k, :, i * rows : (i + 1) * rows]


def cached_attention(me, lengths, table, chunks, kv_cache):
    lanes = len(chunks)
    requests = lengths.shape[0]
    span_devs = lanes // requests
    rows = chunks[0].shape[1]
    queries = rows * span_devs
    block_pages = 4
    return pl.pallas_call(
        functools.partial(cached_kernel, lanes, requests, span_devs, block_pages),
        out_shape=[jax.ShapeDtypeStruct((HD + EXT, rows), BF16)] * lanes,
        in_specs=smem(3) + vmem(lanes + 1),
        out_specs=vmem(lanes),
        scratch_shapes=[
            pltpu.VMEM((requests, 2 * HD, queries), BF16),
            pltpu.VMEM((1, queries), F32),
            pltpu.VMEM((HD + EXT, queries), F32),
            pltpu.VMEM((requests, HD + EXT, queries), BF16),
        ],
        compiler_params=params(),
        cost_estimate=pl.CostEstimate(
            flops=8 * 10**9, bytes_accessed=6 * 10**6, transcendentals=8 * 10**6
        ),
        name="cached_attention",
    )(me, lengths, table, *chunks, kv_cache)


def self_kernel(lanes, span_devs, *refs):
    info, q_ref = refs[:2]
    key_refs = refs[2 : 2 + span_devs]
    value_refs = refs[2 + span_devs : 2 + 2 * span_devs]
    out_ref = refs[2 + 2 * span_devs]
    rows = q_ref.shape[1]
    at = info[0] % span_devs

    def pair(j, other, causal):
        block = jnp.bitwise_xor(2 * j, other & ~1) // 2
        keys = key_refs[other][:, pl.ds(pl.multiple_of(block * 2 * HD, 2 * HD), 2 * HD)]
        both_q = q_ref[pl.ds(pl.multiple_of(j * 2 * HD, 2 * HD), 2 * HD), :]
        both_v = value_refs[other][pl.ds(pl.multiple_of(block * 2 * HD, 2 * HD), 2 * HD), :]
        nothing = jnp.zeros((HD, rows), BF16)
        for h in range(2):
            there = h ^ (other & 1)
            q = both_q[h * HD : (h + 1) * HD]
            q = jnp.concatenate([nothing, q] if there else [q, nothing], axis=0)
            scores = dot(keys, q)
            if causal:
                position = lax.broadcasted_iota(jnp.int32, scores.shape, 0)
                line = lax.broadcasted_iota(jnp.int32, scores.shape, 1)
                scores = jnp.where(position <= line, scores, NEGATIVE)
            values = jnp.concatenate([both_v[there * HD : (there + 1) * HD], ones_rows(rows)], axis=0)
            s = 2 * j + h
            if causal:
                m = jnp.full((1, rows), NEGATIVE, F32)
                acc = jnp.zeros((HD + EXT, rows), F32)
            else:
                m = out_ref[s, HD + EXT : HD + EXT + 1, :]
                acc = out_ref[s, 0 : HD + EXT, :]
            top, acc = softmax_step(scores, values, m, acc)
            out_ref[s, 0 : HD + EXT, :] = acc
            out_ref[s, HD + EXT : HD + EXT + 8, :] = jnp.broadcast_to(top, (8, rows))

    def run(other, causal):
        def step(j, c):
            pair(j, other, causal)
            return c

        lax.fori_loop(0, lanes // 2, step, 0)

    run(0, True)
    for other in range(1, span_devs):

        @pl.when(jnp.bitwise_xor(at, other) < at)
        def _(other=other):
            run(other, False)


def self_attention(me, q_t, keys, values):
    span_devs = len(keys)
    lanes = q_t.shape[0] // HD
    rows = q_t.shape[1]
    return pl.pallas_call(
        functools.partial(self_kernel, lanes, span_devs),
        out_shape=jax.ShapeDtypeStruct((lanes, HD + EXT + 8, rows), F32),
        in_specs=smem(1) + vmem(1 + 2 * span_devs),
        out_specs=pl.BlockSpec(memory_space=pltpu.VMEM),
        compiler_params=params(),
        cost_estimate=pl.CostEstimate(
            flops=3 * 10**9, bytes_accessed=5 * 10**6, transcendentals=4 * 10**6
        ),
        name="self_attention",
    )(me, q_t, *keys, *values)


def merge_kernel(lanes, cap, *refs):
    tokens, own = refs[:2]
    cached = refs[2 : 2 + lanes]
    w_o, gain, router, hits, slot_rows = refs[2 + lanes : 7 + lanes]
    state_ref, gates_ref = refs[7 + lanes : 9 + lanes]
    out_refs = refs[9 + lanes : 9 + 2 * lanes]
    attended, placing = refs[9 + 2 * lanes :]
    for s in range(lanes):
        part = cached[s][...].astype(F32)
        lse = part[HD : HD + 1] + part[HD + 1 : HD + 2] + part[HD + 2 : HD + 3]
        m = own[s, HD + EXT : HD + EXT + 1, :]
        total = own[s, HD : HD + 1, :]
        top = jnp.maximum(m, lse)
        w_cached, w_own = jnp.exp(lse - top), jnp.exp(m - top)
        norm = 1.0 / (w_cached + w_own * total)
        merged = part[0:HD] * (w_cached * norm) + own[s, 0:HD, :] * (w_own * norm)
        attended[s * HD : (s + 1) * HD, :] = merged.astype(BF16)
    state = tokens[...].astype(F32) + dot(attended[...].T, w_o[...])
    state_ref[...] = state
    mean_square = jnp.mean(state * state, axis=-1, keepdims=True)
    normed = (state * lax.rsqrt(mean_square + EPSILON) * gain[...]).astype(BF16)
    logits = dot(normed, router[...])
    squashed = jnp.where(hits[...] > 0, jax.nn.sigmoid(logits), 0.0)
    gates_ref[...] = squashed / jnp.sum(squashed, axis=1, keepdims=True)
    rows = tokens.shape[0]
    for s in range(lanes):
        at_slot = lax.broadcasted_iota(jnp.int32, (cap, rows), 0)
        placing[s * cap : (s + 1) * cap, :] = (at_slot == slot_rows[s : s + 1, :]).astype(F32).astype(BF16)
    for s in range(lanes):
        out_refs[s][...] = dot(placing[s * cap : (s + 1) * cap, :], normed).astype(BF16)


def merge_dispatch(tokens, own, cached, w_o, gain, router, hits, slot_rows, cap):
    lanes = len(cached)
    rows, width = tokens.shape
    return pl.pallas_call(
        functools.partial(merge_kernel, lanes, cap),
        out_shape=[
            jax.ShapeDtypeStruct((rows, width), F32),
            jax.ShapeDtypeStruct((rows, lanes), F32),
        ]
        + [jax.ShapeDtypeStruct((cap, width), BF16)] * lanes,
        in_specs=vmem(7 + lanes),
        out_specs=vmem(2 + lanes),
        scratch_shapes=[
            pltpu.VMEM((lanes * HD, rows), BF16),
            pltpu.VMEM((lanes * cap, rows), BF16),
        ],
        compiler_params=params(),
        cost_estimate=pl.CostEstimate(
            flops=4 * 10**9, bytes_accessed=10 * 10**6, transcendentals=10**5
        ),
        name="merge_and_dispatch",
    )(tokens, own, *cached, w_o, gain, router, hits, slot_rows)


def expert_kernel(count, *refs):
    x_refs = refs[:count]
    gate_ref, up_ref, down_ref = refs[count : count + 3]
    out_refs = refs[count + 3 : 2 * count + 3]
    x_all, total = refs[2 * count + 3 :]
    cap = x_refs[0].shape[0]
    step = pl.program_id(0)

    @pl.when(step == 0)
    def _():
        for n in range(count):
            x_all[n * cap : (n + 1) * cap, :] = x_refs[n][...]

    x = x_all[...]
    gate = dot(x, gate_ref[0])
    up = dot(x, up_ref[0])
    active = (jax.nn.gelu(gate, approximate=True) * up).astype(BF16)
    part = dot(active, down_ref[0])

    @pl.when(step == 0)
    def _():
        total[...] = part

    @pl.when(step > 0)
    def _():
        total[...] += part

    @pl.when(step == pl.num_programs(0) - 1)
    def _():
        for n in range(count):
            out_refs[n][...] = total[n * cap : (n + 1) * cap, :].astype(BF16)


def expert(chunks, w_in, w_out):
    count = len(chunks)
    cap, width = chunks[0].shape
    hidden = w_out.shape[1]
    tile = 256
    steps = hidden // tile
    whole = pl.BlockSpec((cap, width), lambda j: (0, 0))
    return pl.pallas_call(
        functools.partial(expert_kernel, count),
        grid=(steps,),
        out_shape=[jax.ShapeDtypeStruct((cap, width), BF16)] * count,
        in_specs=[whole] * count
        + [
            pl.BlockSpec((1, width, tile), lambda j: (0, 0, j)),
            pl.BlockSpec((1, width, tile), lambda j: (0, 0, j + steps)),
            pl.BlockSpec((1, tile, width), lambda j: (0, j, 0)),
        ],
        out_specs=[whole] * count,
        scratch_shapes=[
            pltpu.VMEM((count * cap, width), BF16),
            pltpu.VMEM((count * cap, width), F32),
        ],
        compiler_params=params(),
        cost_estimate=pl.CostEstimate(
            flops=6 * count * cap * width * hidden,
            bytes_accessed=6 * width * hidden,
            transcendentals=count * cap * hidden,
        ),
        name="expert",
    )(*chunks, w_in, w_in, w_out)


def combine_kernel(first, count, last, *refs):
    base, gates, slots = refs[:3]
    parts = refs[3 : 3 + count]
    out = refs[3 + count]
    rows = base.shape[0]
    cap = parts[0].shape[0]
    total = base[...]
    for n in range(count):
        s = first + n
        lane = lax.broadcasted_iota(jnp.int32, (rows, cap), 1)
        pick = (lane == slots[:, s : s + 1]).astype(F32).astype(BF16)
        total = total + gates[:, s : s + 1] * dot(pick, parts[n][...])
    out[...] = total.astype(out.dtype)


def combine(base, gates, slots, parts, first, last):
    count = len(parts)
    rows, width = base.shape
    return pl.pallas_call(
        functools.partial(combine_kernel, first, count, last),
        out_shape=jax.ShapeDtypeStruct((rows, width), BF16 if last else F32),
        in_specs=vmem(3 + count),
        out_specs=pl.BlockSpec(memory_space=pltpu.VMEM),
        compiler_params=params(),
        cost_estimate=pl.CostEstimate(
            flops=2 * count * rows * parts[0].shape[0] * width,
            bytes_accessed=6 * 10**6,
            transcendentals=0,
        ),
        name="combine",
    )(base, gates, slots, *parts)


def body(
    tokens,
    gain_attn,
    w_qkv,
    w_attn_out,
    kv_cache,
    page_table,
    cached_lengths,
    gain_moe,
    w_router,
    routes,
    w_in,
    w_out,
):
    lanes, groups = lax.axis_size("tensor"), lax.axis_size("batch")
    me, group = lax.axis_index("tensor"), lax.axis_index("batch")
    rows, width = tokens.shape
    requests = cached_lengths.shape[0]
    span_devs = lanes // requests
    share = width // groups
    here = me.astype(jnp.int32).reshape(1)

    w_t = w_qkv.T
    w_q = gather_xor(w_t[0:HD] * (1.0 / math.sqrt(HD)), lanes, groups)
    rest = jnp.concatenate([w_t[HD : 3 * HD], w_attn_out.T], axis=0)
    rest, w_q = lax.optimization_barrier((rest, w_q))
    w_rest = gather_xor(rest, lanes, groups)

    values = tokens.astype(F32)
    mean_square = jnp.mean(values * values, axis=-1, keepdims=True)
    normed = (values * lax.rsqrt(mean_square + EPSILON) * gain_attn).astype(BF16)
    normed = jnp.concatenate(
        [lax.dynamic_slice_in_dim(normed, (group ^ j) * share, share, 1) for j in range(groups)],
        axis=1,
    )

    def columns(pieces):
        return pieces.transpose(1, 2, 0, 3).reshape(lanes * HD, groups * share)

    q_t = dot(columns(w_q), normed, NT).astype(BF16)
    q_chunks = [q_t[s * HD : (s + 1) * HD] for s in range(lanes)]
    order = sorted(range(1, lanes), key=lambda s: -s)
    q_in = {0: q_chunks[0]}
    for s in order:
        q_in[s] = send(q_chunks[s], s, lanes, groups)

    keys = dot(normed, columns(w_rest[:, :, 0:HD]), NT).astype(BF16)
    vals = dot(columns(w_rest[:, :, HD : 2 * HD]), normed, NT).astype(BF16)
    near_keys, near_vals = [keys], [vals]
    for i in range(1, span_devs):
        pairs = [
            (b * lanes + t, b * lanes + (t ^ i))
            for b in range(groups)
            for t in range(lanes)
            if t % span_devs < (t ^ i) % span_devs
        ]
        near_keys.append(lax.ppermute(keys, AXES, pairs))
        near_vals.append(lax.ppermute(vals, AXES, pairs))
    o_pieces = w_rest[:, :, 2 * HD : 3 * HD].reshape(groups, lanes * HD, share)
    w_o = jnp.concatenate(
        [lax.dynamic_index_in_dim(o_pieces, group ^ n, 0, keepdims=False) for n in range(groups)],
        axis=1,
    )

    parts = cached_attention(
        here, cached_lengths, page_table, [q_in[s] for s in range(lanes)], kv_cache
    )
    back = {0: parts[0]}
    for s in order:
        back[s] = send(parts[s], s, lanes, groups)
    own = self_attention(here, q_t, near_keys, near_vals)

    names = me ^ jnp.arange(lanes, dtype=jnp.int32)
    hit_rows = (routes[:, 0][None, :] == names[:, None]) | (routes[:, 1][None, :] == names[:, None])
    earlier = jnp.triu(jnp.ones((rows, rows), BF16), 1)
    rank = dot(hit_rows.astype(BF16), earlier).astype(jnp.int32)
    slot_rows = jnp.where(hit_rows, rank, -1)
    slots = slot_rows.T
    hits = hit_rows.astype(jnp.int32).T
    capacity = max(2, (5 * rows * routes.shape[1] + 4 * lanes - 1) // (4 * lanes))
    cap = -(-capacity // 16) * 16
    router = jnp.take(w_router, names, axis=1)

    outcome = merge_dispatch(
        tokens,
        own,
        [back[s] for s in range(lanes)],
        w_o,
        gain_moe.reshape(1, width),
        router,
        hits,
        slot_rows,
        cap,
    )
    state, gates, buffers = outcome[0], outcome[1], outcome[2:]
    arrived = {0: buffers[0]}
    for s in order:
        arrived[s] = send(buffers[s], s, lanes, groups)
    half = lanes // 2
    mixed = state
    for first in (0, half):
        mine = range(first, first + half)
        results = expert([arrived[s] for s in mine], w_in, w_out)
        returned = [
            results[n] if s == 0 else send(results[n], s, lanes, groups)
            for n, s in enumerate(mine)
        ]
        mixed = combine(mixed, gates, slots, returned, first, first == half)
    return mixed


def solution(mesh):
    in_specs = (
        P(("batch", "tensor"), None),
        P(),
        P("batch", "tensor"),
        P("batch", "tensor"),
        P("batch", None, "tensor"),
        P("batch", None),
        P("batch"),
        P(),
        P(),
        P(("batch", "tensor"), None),
        P("tensor", None, None),
        P("tensor", None, None),
    )
    out_specs = P(("batch", "tensor"), None)
    return jax.shard_map(body, mesh=mesh, in_specs=in_specs, out_specs=out_specs, check_vma=False)
```

time: 768 us -> 261 us (0.34)
  waiting for transfers between devices: 441 us -> 116 us
  matrix products: 112 us -> 3.58 us
  blocking collectives: 75.7 us -> 0 us
  Pallas kernels: 0 us -> 69.7 us
  starting transfers between devices: 5.16 us -> 55 us
  local copies, waits for them, and re-layouts: 47.3 us -> 8.02 us
  other arithmetic: 41.1 us -> 4.66 us
  loops' own time: 26.6 us -> 0 us
  between operations: 13.6 us -> 0.5 us
    reduce_scatter x1 -> x0, waiting for transfers between devices: 274 us -> none  [body(): lax.psum_scatter(lax.dot_general(portion, out_columns, CONTRACT, preferre...]
    ppermute x0 -> x44, waiting for transfers between devices: none -> 116 us  [the longest x42 116 us: send(): return lax.ppermute(value, AXES, [(i, i ^ mask) for i in range(total)])]
    all_gather x1 -> x0, waiting for transfers between devices: 111 us -> none  [body(): lax.all_gather(normed, 'tensor', axis=0, tiled=True)]
    dot_general x24 -> x4, matrix products: 112 us -> 3.58 us  [dot(): return lax.dot_general(a, b, dims, preferred_element_type=F32)]
    pallas_call x0 -> x7, Pallas kernels: none -> 69.7 us  [the longest x2 36.7 us: expert(): pl.pallas_call(functools.partial(expert_kernel, count), grid=(steps,), ou...]
    all_to_all x1 -> x0, blocking collectives: 62.7 us -> none  [body(): lax.all_to_all(buffer, 'tensor', split_axis=0, concat_axis=0, tiled=True)]
    all_to_all x1 -> x0, waiting for transfers between devices: 56 us -> none  [body(): lax.all_to_all(results, 'tensor', split_axis=0, concat_axis=0, tiled=True)]
    ppermute x0 -> x44, starting transfers between devices: none -> 55 us  [the longest x42 51.1 us: send(): return lax.ppermute(value, AXES, [(i, i ^ mask) for i in range(total)])]
  transfers between devices with their start and end apart: 3 -> 44, of which waited for: 3 -> 23; matrix products, arithmetic and copies ran while one was open for 1% -> 5% of each run, Pallas kernels for 0% -> 23%
where the time goes in v1:
time: 261 us; the launch traced here: 257 us
  waiting for transfers between devices  116 us (44%)
  Pallas kernels  69.7 us (27%)
  starting transfers between devices  55 us (21%)
  local copies, waits for them, and re-layouts  8.02 us (3%)
  other arithmetic  4.66 us (2%)
  matrix products  3.58 us (1%)
    ppermute x42, waiting for transfers between devices, send(): return lax.ppermute(value, AXES, [(i, i ^ mask) for i in range(total)])  116 us
    ppermute x42, starting transfers between devices, send(): return lax.ppermute(value, AXES, [(i, i ^ mask) for i in range(total)])  51.1 us
    pallas_call x2, Pallas kernels, expert(): pl.pallas_call(functools.partial(expert_kernel, count), grid=(steps,), ou...  36.7 us
    pallas_call x1, Pallas kernels, cached_attention(): pl.pallas_call(functools.partial(cached_kernel, lanes, requests, span_dev...  12.6 us
    pallas_call x2, Pallas kernels, combine(): pl.pallas_call(functools.partial(combine_kernel, first, count, last), out...  8.44 us
    pallas_call x1, Pallas kernels, merge_dispatch(): pl.pallas_call(functools.partial(merge_kernel, lanes, cap), out_shape=[ja...  6.15 us
    pallas_call x1, Pallas kernels, self_attention(): pl.pallas_call(functools.partial(self_kernel, lanes, span_devs), out_shap...  5.87 us
  transfers between devices with their start and end apart: 44, of which 23 were waited for; matrix products, arithmetic and copies ran while one was open for 5% of the time, Pallas kernels for 23%

profile of v1, /device:TPU:9, one launch (start us, length us, event | category | flops | bytes accessed | tf_op | source)
XLA Modules:
  0.0 257.1 jit_solution(9220884191313236420)
XLA Ops:
  0.0 0.8 fusion.15
  0.8 2.5 collective-permute-start.1
  3.6 1.5 collective-permute-done.1
  5.0 1.6 collective-permute-done.2
  6.7 1.3 collective-permute-start.4
  8.0 1.2 collective-permute-start.5
  9.1 0.8 slice.62
  10.2 0.8 pad_maximum_fusion.12
  11.0 1.8 collective-permute-done.5
  12.8 1.8 collective-permute-done.3
  14.8 3.0 %collective-permute-start.6 = (bf16[2,8,64,256]{3,2,1,0:T(8,128)(2,1)S(1)}, bf16[2,8,64,256]{3,2,1,0:T(8,128)(2,1)S(1)}, u32[]{:S(2)}, u32[]{:S(2)}) collective-permute-start(bf16[2,8,64,256]{3,2,1,0:T(8,128)(2,1)S(1)} %pad_maximum_fusion.7), channel_id=1, source_target_pairs={{0,8},{1,9},{2,10},{3,11},{4,12},{5,13},{6,14},{7,15},{8,0},{9,1},... | collective-permute-start | bytes 1572872 | tf_op jit(solution)/shard_map/ppermute | solution.py:39
  17.8 1.4 fusion.8
  19.4 2.8 %collective-permute-start.7 = (bf16[192,256]{1,0:T(8,128)(2,1)S(1)}, bf16[192,256]{1,0:T(8,128)(2,1)S(1)}, u32[]{:S(2)}, u32[]{:S(2)}) collective-permute-start(bf16[192,256]{1,0:T(8,128)(2,1)S(1)} %pad_maximum_fusion.12), channel_id=1, source_target_pairs={{0,2},{1,3},{2,0},{3,1},{4,6},{5,7},{6,4},{7,5},{8,10},{9,11},{10,... | collective-permute-start | bytes 294920 | tf_op jit(solution)/shard_map/ppermute | solution.py:39
  22.2 1.3 collective-permute-start.9
  23.5 1.6 collective-permute-done.7
  25.1 1.6 collective-permute-done.8
  26.7 5.7 %collective-permute-done.9 = bf16[192,256]{1,0:T(8,128)(2,1)S(1)} collective-permute-done((bf16[192,256]{1,0:T(8,128)(2,1)S(1)}, bf16[192,256]{1,0:T(8,128)(2,1)S(1)}, u32[]{:S(2)}, u32[]{:S(2)}) %collective-permute-start.9) | collective-permute-done | bytes 98336 | tf_op jit(solution)/shard_map/ppermute | solution.py:39
  32.9 1.2 collective-permute-start.11
  34.1 1.1 collective-permute-start.12
  35.2 1.0 copy.45.refs_14_
  37.1 4.8 %collective-permute-done.10 = bf16[4,192,256]{2,1,0:T(8,128)(2,1)S(1)} collective-permute-done((bf16[4,192,256]{2,1,0:T(8,128)(2,1)S(1)}, bf16[4,192,256]{2,1,0:T(8,128)(2,1)S(1)}, u32[]{:S(2)}, u32[]{:S(2)}) %collective-permute-start.10) | collective-permute-done | bytes 393248 | tf_op jit(solution)/shard_map/ppermute | solution.py:39
  42.1 9.2 %collective-permute-done.12 = bf16[4,192,256]{2,1,0:T(8,128)(2,1)S(1)} collective-permute-done((bf16[4,192,256]{2,1,0:T(8,128)(2,1)S(1)}, bf16[4,192,256]{2,1,0:T(8,128)(2,1)S(1)}, u32[]{:S(2)}, u32[]{:S(2)}) %collective-permute-start.12) | collective-permute-done | bytes 393248 | tf_op jit(solution)/shard_map/ppermute | solution.py:39
  51.7 2.2 collective-permute-start.13
  54.8 0.8 copy.36
  55.9 0.7 convolution_convert_fusion.2.refs_1_
  57.3 2.1 collective-permute-start.18
  59.4 2.6 %collective-permute-start.20 = (bf16[64,512]{1,0:T(8,128)(2,1)S(1)}, bf16[64,512]{1,0:T(8,128)(2,1)S(1)}, u32[]{:S(2)}, u32[]{:S(2)}) collective-permute-start(bf16[64,512]{1,0:T(8,128)(2,1)S(1)} %get-tuple-element.74), channel_id=1, source_target_pairs={{0,5},{1,4},{2,7},{3,6},{4,1},{5,0},{6,3},{7,2},{8,13},{9,12},{10,... | collective-permute-start | bytes 196616 | tf_op jit(solution)/shard_map/ppermute | solution.py:39
  62.7 0.8 copy.48
  63.8 0.7 convolution_convert_fusion.refs_4_
  64.5 0.8 copy.47
  65.8 1.9 collective-permute-start.22
  68.5 2.5 collective-permute-start.15
  71.0 1.5 collective-permute-start.14
  72.6 12.6 %cached_attention.1 = (bf16[80,512]{1,0:T(8,128)(2,1)S(1)}, bf16[80,512]{1,0:T(8,128)(2,1)S(1)}, bf16[80,512]{1,0:T(8,128)(2,1)S(1)}, bf16[80,512]{1,0:T(8,128)(...) custom-call(s32[1]{0:T(128)} %bitcast.refs_0_, ...), custom_call_target="tpu_custom_call" | custom-call | flops 8000000000 | bytes 6000000 | tf_op jit(solution)/shard_map/cached_attention/pallas_call | solution.py:148
  85.3 1.9 collective-permute-start.24
  87.1 1.1 collective-permute-start.25
  88.3 1.1 pad_maximum_fusion.4.refs_10_
  89.4 5.9 %collective-permute-done.23.refs_3_ = bf16[80,512]{1,0:T(8,128)(2,1)S(1)} collective-permute-done((bf16[80,512]{1,0:T(8,128)(2,1)S(1)}, bf16[80,512]{1,0:T(8,128)(2,1)S(1)}, u32[]{:S(2)}, u32[]{:S(2)}) %collective-permute-start.23) | collective-permute-done | bytes 81952 | tf_op jit(solution)/shard_map/ppermute | solution.py:39
  95.3 2.2 collective-permute-start.26
  97.5 2.2 collective-permute-start.27
  99.7 0.9 collective-permute-start.28
  101.0 5.9 %self_attention.1.refs_1_ = f32[8,88,512]{2,1,0:T(8,128)} custom-call(s32[1]{0:T(128)} %bitcast.refs_0_, bf16[512,512]{1,0:T(8,128)(2,1)S(1)} %convolution_convert_fusion.2.refs_1_, bf16[512,512]{1,0:T(8,128)(2,1)S(1)} %convolution_convert_fusion.1.refs_2_, bf16[512,512]{1,0:T(8,128)(2,1)S(1)} %collective-permute-done.14.refs_3_, ...), custom_call_target="tpu_custom_call" | custom-call | flops 3000000000 | bytes 5000000 | tf_op jit(solution)/shard_map/self_attention/pallas_call | solution.py:221
  106.9 1.7 collective-permute-done.28.refs_8_
  108.6 4.6 %collective-permute-done.29.refs_9_ = bf16[80,512]{1,0:T(8,128)(2,1)S(1)} collective-permute-done((bf16[80,512]{1,0:T(8,128)(2,1)S(1)}, bf16[80,512]{1,0:T(8,128)(2,1)S(1)}, u32[]{:S(2)}, u32[]{:S(2)}) %collective-permute-start.29) | collective-permute-done | bytes 81952 | tf_op jit(solution)/shard_map/ppermute | solution.py:39
  113.2 6.2 %merge_and_dispatch.1 = (f32[512,1024]{1,0:T(8,128)}, f32[512,8]{1,0:T(8,128)S(1)}, bf16[160,1024]{1,0:T(8,128)(2,1)S(1)}, bf16[160,1024]{1,0:T(8,128)(2,1)}, bf...) custom-call(bf16[512,1024]{1,0:T(8,128)(2,1)} %refs_0_.1, ...), custom_call_target="tpu_custom_call" | custom-call | flops 4000000000 | bytes 10000000 | tf_op jit(solution)/shard_map/merge_and_dispatch/pallas_call | solution.py:269
  119.4 3.2 %collective-permute-start.31 = (bf16[160,1024]{1,0:T(8,128)(2,1)}, bf16[160,1024]{1,0:T(8,128)(2,1)S(1)}, u32[]{:S(2)}, u32[]{:S(2)}) collective-permute-start(bf16[160,1024]{1,0:T(8,128)(2,1)} %get-tuple-element.47), channel_id=1, source_target_pairs={{0,2},{1,3},{2,0},{3,1},{4,6},{5,7},{6,4},{7,5},{8,10},{9,11},{10,... | collective-permute-start | bytes 983048 | tf_op jit(solution)/shard_map/ppermute | solution.py:39
  122.6 1.2 collective-permute-start.36
  123.8 2.0 collective-permute-start.37
  126.5 2.8 %collective-permute-start.38 = (bf16[160,1024]{1,0:T(8,128)(2,1)}, bf16[160,1024]{1,0:T(8,128)(2,1)S(1)}, u32[]{:S(2)}, u32[]{:S(2)}) collective-permute-start(bf16[160,1024]{1,0:T(8,128)(2,1)} %get-tuple-element.55), channel_id=1, source_target_pairs={{0,6},{1,7},{2,4},{3,5},{4,2},{5,3},{6,0},{7,1},{8,14},{9,15},{10,... | collective-permute-start | bytes 983048 | tf_op jit(solution)/shard_map/ppermute | solution.py:39
  129.3 7.9 %collective-permute-done.31.refs_2_ = bf16[160,1024]{1,0:T(8,128)(2,1)S(1)} collective-permute-done((bf16[160,1024]{1,0:T(8,128)(2,1)}, bf16[160,1024]{1,0:T(8,128)(2,1)S(1)}, u32[]{:S(2)}, u32[]{:S(2)}) %collective-permute-start.31) | collective-permute-done | bytes 327712 | tf_op jit(solution)/shard_map/ppermute | solution.py:39
  137.2 8.4 %collective-permute-done.32.refs_3_ = bf16[160,1024]{1,0:T(8,128)(2,1)S(1)} collective-permute-done((bf16[160,1024]{1,0:T(8,128)(2,1)}, bf16[160,1024]{1,0:T(8,128)(2,1)S(1)}, u32[]{:S(2)}, u32[]{:S(2)}) %collective-permute-start.32) | collective-permute-done | bytes 327712 | tf_op jit(solution)/shard_map/ppermute | solution.py:39
  146.3 18.3 %expert.2 = (bf16[160,1024]{1,0:T(8,128)(2,1)S(1)}, bf16[160,1024]{1,0:T(8,128)(2,1)S(1)}, bf16[160,1024]{1,0:T(8,128)(2,1)S(1)}, bf16[160,1024]{1,0:T(8,128)(2,1)S(1)}) custom-call(bf16[160,1024]{1,0:T(8,128)(2,1)S(1)} %get-tuple-element.45.refs_0_, bf16[160,1024]{1,0:T(8,128)(2,1)S(1)} %collective-permute-done.30.refs_1_, bf16[160,1024]{1,0:T(8,128)(2,1)} %copy-done.13, ...), custom_call_target="tpu_custom_call" | custom-call | flops 11072962560 | bytes 17301504 | tf_op jit(solution)/shard_map/expert/pallas_call | solution.py:330
  164.8 3.3 %collective-permute-start.34 = (bf16[160,1024]{1,0:T(8,128)(2,1)S(1)}, bf16[160,1024]{1,0:T(8,128)(2,1)S(1)}, u32[]{:S(2)}, u32[]{:S(2)}) collective-permute-start(bf16[160,1024]{1,0:T(8,128)(2,1)S(1)} %get-tuple-element.51), channel_id=1, source_target_pairs={{0,2},{1,3},{2,0},{3,1},{4,6},{5,7},{6,4},{7,5},{8,10},{9,11},{10,... | collective-permute-start | bytes 983048 | tf_op jit(solution)/shard_map/ppermute | solution.py:39
  168.0 2.4 collective-permute-done.38.refs_2_
  170.4 8.1 %collective-permute-done.39.refs_3_ = bf16[160,1024]{1,0:T(8,128)(2,1)S(1)} collective-permute-done((bf16[160,1024]{1,0:T(8,128)(2,1)}, bf16[160,1024]{1,0:T(8,128)(2,1)S(1)}, u32[]{:S(2)}, u32[]{:S(2)}) %collective-permute-start.39) | collective-permute-done | bytes 327712 | tf_op jit(solution)/shard_map/ppermute | solution.py:39
  179.3 18.3 %expert.3 = (bf16[160,1024]{1,0:T(8,128)(2,1)S(1)}, bf16[160,1024]{1,0:T(8,128)(2,1)S(1)}, bf16[160,1024]{1,0:T(8,128)(2,1)S(1)}, bf16[160,1024]{1,0:T(8,128)(2,1)S(1)}) custom-call(bf16[160,1024]{1,0:T(8,128)(2,1)S(1)} %collective-permute-done.36.refs_0_, bf16[160,1024]{1,0:T(8,128)(2,1)S(1)} %collective-permute-done.37.refs_1_, ...), custom_call_target="tpu_custom_call" | custom-call | flops 11072962560 | bytes 17301504 | tf_op jit(solution)/shard_map/expert/pallas_call | solution.py:330
  197.7 2.5 collective-permute-start.41
  200.4 2.0 collective-permute-start.43
  202.6 4.4 %combine.2.refs_0_ = f32[512,1024]{1,0:T(8,128)} custom-call(f32[512,1024]{1,0:T(8,128)} %get-tuple-element.43.refs_0_, f32[512,8]{1,0:T(8,128)S(1)} %get-tuple-element.44.refs_1_, s32[512,8]{1,0:T(8,128)S(1)} %bitcast_select_fusion.refs_2_, bf16[160,1024]{1,0:T(8,128)(2,1)S(1)} %get-tuple-element.49.refs_3_, ...), custom_call_target="tpu_custom_call" | custom-call | flops 671088640 | bytes 6000000 | tf_op jit(solution)/shard_map/combine/pallas_call | solution.py:373
  207.0 25.0 %collective-permute-done.40.refs_3_ = bf16[160,1024]{1,0:T(8,128)(2,1)S(1)} collective-permute-done((bf16[160,1024]{1,0:T(8,128)(2,1)S(1)}, bf16[160,1024]{1,0:T(8,128)(2,1)S(1)}, u32[]{:S(2)}, u32[]{:S(2)}) %collective-permute-start.40) | collective-permute-done | bytes 327712 | tf_op jit(solution)/shard_map/ppermute | solution.py:39
  232.0 7.0 %collective-permute-done.41.refs_4_ = bf16[160,1024]{1,0:T(8,128)(2,1)S(1)} collective-permute-done((bf16[160,1024]{1,0:T(8,128)(2,1)S(1)}, bf16[160,1024]{1,0:T(8,128)(2,1)S(1)}, u32[]{:S(2)}, u32[]{:S(2)}) %collective-permute-start.41) | collective-permute-done | bytes 327712 | tf_op jit(solution)/shard_map/ppermute | solution.py:39
  239.1 7.0 %collective-permute-done.42.refs_5_ = bf16[160,1024]{1,0:T(8,128)(2,1)S(1)} collective-permute-done((bf16[160,1024]{1,0:T(8,128)(2,1)S(1)}, bf16[160,1024]{1,0:T(8,128)(2,1)S(1)}, u32[]{:S(2)}, u32[]{:S(2)}) %collective-permute-start.42) | collective-permute-done | bytes 327712 | tf_op jit(solution)/shard_map/ppermute | solution.py:39
  246.1 7.0 %collective-permute-done.43.refs_6_ = bf16[160,1024]{1,0:T(8,128)(2,1)S(1)} collective-permute-done((bf16[160,1024]{1,0:T(8,128)(2,1)S(1)}, bf16[160,1024]{1,0:T(8,128)(2,1)S(1)}, u32[]{:S(2)}, u32[]{:S(2)}) %collective-permute-start.43) | collective-permute-done | bytes 327712 | tf_op jit(solution)/shard_map/ppermute | solution.py:39
  253.1 4.0 %combine.3 = bf16[512,1024]{1,0:T(8,128)(2,1)} custom-call(f32[512,1024]{1,0:T(8,128)} %combine.2.refs_0_, f32[512,8]{1,0:T(8,128)S(1)} %get-tuple-element.44.refs_1_, s32[512,8]{1,0:T(8,128)S(1)} %bitcast_select_fusion.refs_2_, bf16[160,1024]{1,0:T(8,128)(2,1)S(1)} %collective-permute-done.40.refs_3_, ...), custom_call_target="tpu_custom_call" | custom-call | flops 671088640 | bytes 6000000 | tf_op jit(solution)/shard_map/combine/pallas_call | solution.py:373
  (106 shorter events, 9.9 us)
Async XLA Ops:
  0.0 36.3 %copy-start = (bf16[1024,8]{0,1:T(8,128)(2,1)S(1)}, bf16[1024,8]{0,1:T(8,128)(2,1)}, u32[]{:S(2)}) copy-start(bf16[1024,8]{0,1:T(8,128)(2,1)} %param.20) | copy-start | bytes 49156
  0.0 17.8 %copy-start.8 = (s32[512,2]{0,1:T(2,128)S(1)}, s32[512,2]{0,1:T(2,128)}, u32[]{:S(2)}) copy-start(s32[512,2]{0,1:T(2,128)} %param.21) | copy-start | bytes 12292
  0.8 2.8 %collective-permute-start = (bf16[64,256]{1,0:T(8,128)(2,1)S(1)}, bf16[64,256]{1,0:T(8,128)(2,1)S(1)}, u32[]{:S(2)}, u32[]{:S(2)}) collective-permute-start(bf16[64,256]{1,0:T(8,128)(2,1)S(1)} %get-tuple-element.85), channel_id=1, source_target_pairs={{0,2},{1,3},{2,0},{3,1},{4,6},{5,7},{6,4},{7,5},{8,10},{9,11},{10,... | collective-permute-start | bytes 98312 | tf_op jit(solution)/shard_map/ppermute | solution.py:39
  0.8 4.2 %collective-permute-start.1 = (bf16[64,256]{1,0:T(8,128)(2,1)S(1)}, bf16[64,256]{1,0:T(8,128)(2,1)S(1)}, u32[]{:S(2)}, u32[]{:S(2)}) collective-permute-start(bf16[64,256]{1,0:T(8,128)(2,1)S(1)} %get-tuple-element.85), channel_id=1, source_target_pairs={{0,4},{1,5},{2,6},{3,7},{4,0},{5,1},{6,2},{7,3},{8,12},{9,13},{10,... | collective-permute-start | bytes 98312 | tf_op jit(solution)/shard_map/ppermute | solution.py:39
  3.3 3.4 %collective-permute-start.2 = (bf16[64,256]{1,0:T(8,128)(2,1)S(1)}, bf16[64,256]{1,0:T(8,128)(2,1)S(1)}, u32[]{:S(2)}, u32[]{:S(2)}) collective-permute-start(bf16[64,256]{1,0:T(8,128)(2,1)S(1)} %get-tuple-element.85), channel_id=1, source_target_pairs={{0,6},{1,7},{2,4},{3,5},{4,2},{5,3},{6,0},{7,1},{8,14},{9,15},{10,... | collective-permute-start | bytes 98312 | tf_op jit(solution)/shard_map/ppermute | solution.py:39
  6.7 4.3 %collective-permute-start.4 = (bf16[4,64,256]{2,1,0:T(8,128)(2,1)S(1)}, bf16[4,64,256]{2,1,0:T(8,128)(2,1)S(1)}, u32[]{:S(2)}, u32[]{:S(2)}) collective-permute-start(bf16[4,64,256]{2,1,0:T(8,128)(2,1)S(1)} %get-tuple-element.83), channel_id=1, source_target_pairs={{0,16},{1,17},{2,18},{3,19},{4,20},{5,21},{6,22},{7,23},{8,24},{9,... | collective-permute-start | bytes 393224 | tf_op jit(solution)/shard_map/ppermute | solution.py:39
  8.0 4.8 %collective-permute-start.5 = (bf16[4,64,256]{2,1,0:T(8,128)(2,1)S(1)}, bf16[4,64,256]{2,1,0:T(8,128)(2,1)S(1)}, u32[]{:S(2)}, u32[]{:S(2)}) collective-permute-start(bf16[4,64,256]{2,1,0:T(8,128)(2,1)S(1)} %get-tuple-element.83), channel_id=1, source_target_pairs={{0,17},{1,16},{2,19},{3,18},{4,21},{5,20},{6,23},{7,22},{8,25},{9,... | collective-permute-start | bytes 393224 | tf_op jit(solution)/shard_map/ppermute | solution.py:39
  10.0 4.7 %collective-permute-start.3 = (bf16[4,64,256]{2,1,0:T(8,128)(2,1)S(1)}, bf16[4,64,256]{2,1,0:T(8,128)(2,1)S(1)}, u32[]{:S(2)}, u32[]{:S(2)}) collective-permute-start(bf16[4,64,256]{2,1,0:T(8,128)(2,1)S(1)} %get-tuple-element.83), channel_id=1, source_target_pairs={{0,1},{1,0},{2,3},{3,2},{4,5},{5,4},{6,7},{7,6},{8,9},{9,8},{10,11... | collective-permute-start | bytes 393224 | tf_op jit(solution)/shard_map/ppermute | solution.py:39
  14.8 4.6 %collective-permute-start.6 = (bf16[2,8,64,256]{3,2,1,0:T(8,128)(2,1)S(1)}, bf16[2,8,64,256]{3,2,1,0:T(8,128)(2,1)S(1)}, u32[]{:S(2)}, u32[]{:S(2)}) collective-permute-start(bf16[2,8,64,256]{3,2,1,0:T(8,128)(2,1)S(1)} %pad_maximum_fusion.7), channel_id=1, source_target_pairs={{0,8},{1,9},{2,10},{3,11},{4,12},{5,13},{6,14},{7,15},{8,0},{9,1},... | collective-permute-start | bytes 1572872 | tf_op jit(solution)/shard_map/ppermute | solution.py:39
  19.4 5.7 %collective-permute-start.7 = (bf16[192,256]{1,0:T(8,128)(2,1)S(1)}, bf16[192,256]{1,0:T(8,128)(2,1)S(1)}, u32[]{:S(2)}, u32[]{:S(2)}) collective-permute-start(bf16[192,256]{1,0:T(8,128)(2,1)S(1)} %pad_maximum_fusion.12), channel_id=1, source_target_pairs={{0,2},{1,3},{2,0},{3,1},{4,6},{5,7},{6,4},{7,5},{8,10},{9,11},{10,... | collective-permute-start | bytes 294920 | tf_op jit(solution)/shard_map/ppermute | solution.py:39
  22.2 4.5 %collective-permute-start.8 = (bf16[192,256]{1,0:T(8,128)(2,1)S(1)}, bf16[192,256]{1,0:T(8,128)(2,1)S(1)}, u32[]{:S(2)}, u32[]{:S(2)}) collective-permute-start(bf16[192,256]{1,0:T(8,128)(2,1)S(1)} %pad_maximum_fusion.12), channel_id=1, source_target_pairs={{0,4},{1,5},{2,6},{3,7},{4,0},{5,1},{6,2},{7,3},{8,12},{9,13},{10,... | collective-permute-start | bytes 294920 | tf_op jit(solution)/shard_map/ppermute | solution.py:39
  22.2 10.2 %collective-permute-start.9 = (bf16[192,256]{1,0:T(8,128)(2,1)S(1)}, bf16[192,256]{1,0:T(8,128)(2,1)S(1)}, u32[]{:S(2)}, u32[]{:S(2)}) collective-permute-start(bf16[192,256]{1,0:T(8,128)(2,1)S(1)} %pad_maximum_fusion.12), channel_id=1, source_target_pairs={{0,6},{1,7},{2,4},{3,5},{4,2},{5,3},{6,0},{7,1},{8,14},{9,15},{10,... | collective-permute-start | bytes 294920 | tf_op jit(solution)/shard_map/ppermute | solution.py:39
  32.5 9.5 %collective-permute-start.10 = (bf16[4,192,256]{2,1,0:T(8,128)(2,1)S(1)}, bf16[4,192,256]{2,1,0:T(8,128)(2,1)S(1)}, u32[]{:S(2)}, u32[]{:S(2)}) collective-permute-start(bf16[4,192,256]{2,1,0:T(8,128)(2,1)S(1)} %get-tuple-element.81), channel_id=1, source_target_pairs={{0,1},{1,0},{2,3},{3,2},{4,5},{5,4},{6,7},{7,6},{8,9},{9,8},{10,11... | collective-permute-start | bytes 1179656 | tf_op jit(solution)/shard_map/ppermute | solution.py:39
  32.9 9.2 %collective-permute-start.11 = (bf16[4,192,256]{2,1,0:T(8,128)(2,1)S(1)}, bf16[4,192,256]{2,1,0:T(8,128)(2,1)S(1)}, u32[]{:S(2)}, u32[]{:S(2)}) collective-permute-start(bf16[4,192,256]{2,1,0:T(8,128)(2,1)S(1)} %get-tuple-element.81), channel_id=1, source_target_pairs={{0,16},{1,17},{2,18},{3,19},{4,20},{5,21},{6,22},{7,23},{8,24},{9,... | collective-permute-start | bytes 1179656 | tf_op jit(solution)/shard_map/ppermute | solution.py:39
  34.1 17.3 %collective-permute-start.12 = (bf16[4,192,256]{2,1,0:T(8,128)(2,1)S(1)}, bf16[4,192,256]{2,1,0:T(8,128)(2,1)S(1)}, u32[]{:S(2)}, u32[]{:S(2)}) collective-permute-start(bf16[4,192,256]{2,1,0:T(8,128)(2,1)S(1)} %get-tuple-element.81), channel_id=1, source_target_pairs={{0,17},{1,16},{2,19},{3,18},{4,21},{5,20},{6,23},{7,22},{8,25},{9,... | collective-permute-start | bytes 1179656 | tf_op jit(solution)/shard_map/ppermute | solution.py:39
  51.4 2.4 copy-start.5
  51.5 2.6 %copy-start.7 = (f32[1024]{0:T(1024)S(1)}, f32[1024]{0:T(1024)}, u32[]{:S(2)}) copy-start(f32[1024]{0:T(1024)} %param.13) | copy-start | bytes 12292
  51.7 7.7 %collective-permute-start.13 = (bf16[2,8,192,256]{3,2,1,0:T(8,128)(2,1)S(1)}, bf16[2,8,192,256]{3,2,1,0:T(8,128)(2,1)S(1)}, u32[]{:S(2)}, u32[]{:S(2)}) collective-permute-start(bf16[2,8,192,256]{3,2,1,0:T(8,128)(2,1)S(1)} %pad_maximum_fusion.1), channel_id=1, source_target_pairs={{0,8},{1,9},{2,10},{3,11},{4,12},{5,13},{6,14},{7,15},{8,0},{9,1},... | collective-permute-start | bytes 4718600 | tf_op jit(solution)/shard_map/ppermute | solution.py:39
  56.7 8.9 %collective-permute-start.16 = (bf16[64,512]{1,0:T(8,128)(2,1)S(1)}, bf16[64,512]{1,0:T(8,128)(2,1)S(1)}, u32[]{:S(2)}, u32[]{:S(2)}) collective-permute-start(bf16[64,512]{1,0:T(8,128)(2,1)S(1)} %get-tuple-element.78), channel_id=1, source_target_pairs={{0,1},{1,0},{2,3},{3,2},{4,5},{5,4},{6,7},{7,6},{8,9},{9,8},{10,11... | collective-permute-start | bytes 196616 | tf_op jit(solution)/shard_map/ppermute | solution.py:39
  57.3 8.6 %collective-permute-start.17 = (bf16[64,512]{1,0:T(8,128)(2,1)S(1)}, bf16[64,512]{1,0:T(8,128)(2,1)S(1)}, u32[]{:S(2)}, u32[]{:S(2)}) collective-permute-start(bf16[64,512]{1,0:T(8,128)(2,1)S(1)} %get-tuple-element.77), channel_id=1, source_target_pairs={{0,2},{1,3},{2,0},{3,1},{4,6},{5,7},{6,4},{7,5},{8,10},{9,11},{10,... | collective-permute-start | bytes 196616 | tf_op jit(solution)/shard_map/ppermute | solution.py:39
  57.3 11.3 %collective-permute-start.18 = (bf16[64,512]{1,0:T(8,128)(2,1)S(1)}, bf16[64,512]{1,0:T(8,128)(2,1)S(1)}, u32[]{:S(2)}, u32[]{:S(2)}) collective-permute-start(bf16[64,512]{1,0:T(8,128)(2,1)S(1)} %get-tuple-element.76), channel_id=1, source_target_pairs={{0,3},{1,2},{2,1},{3,0},{4,7},{5,6},{6,5},{7,4},{8,11},{9,10},{10,... | collective-permute-start | bytes 196616 | tf_op jit(solution)/shard_map/ppermute | solution.py:39
  59.4 11.6 %collective-permute-start.19 = (bf16[64,512]{1,0:T(8,128)(2,1)S(1)}, bf16[64,512]{1,0:T(8,128)(2,1)S(1)}, u32[]{:S(2)}, u32[]{:S(2)}) collective-permute-start(bf16[64,512]{1,0:T(8,128)(2,1)S(1)} %get-tuple-element.75), channel_id=1, source_target_pairs={{0,4},{1,5},{2,6},{3,7},{4,0},{5,1},{6,2},{7,3},{8,12},{9,13},{10,... | collective-permute-start | bytes 196616 | tf_op jit(solution)/shard_map/ppermute | solution.py:39
  59.4 13.1 %collective-permute-start.20 = (bf16[64,512]{1,0:T(8,128)(2,1)S(1)}, bf16[64,512]{1,0:T(8,128)(2,1)S(1)}, u32[]{:S(2)}, u32[]{:S(2)}) collective-permute-start(bf16[64,512]{1,0:T(8,128)(2,1)S(1)} %get-tuple-element.74), channel_id=1, source_target_pairs={{0,5},{1,4},{2,7},{3,6},{4,1},{5,0},{6,3},{7,2},{8,13},{9,12},{10,... | collective-permute-start | bytes 196616 | tf_op jit(solution)/shard_map/ppermute | solution.py:39
  64.5 4.0 %copy-start.9 = (bf16[512,512]{1,0:T(8,128)(2,1)}, bf16[512,512]{1,0:T(8,128)(2,1)S(1)}, u32[]{:S(2)}) copy-start(bf16[512,512]{1,0:T(8,128)(2,1)S(1)} %convolution_convert_fusion.refs_4_) | copy-start | bytes 1572868
  65.6 7.0 %collective-permute-start.21 = (bf16[64,512]{1,0:T(8,128)(2,1)S(1)}, bf16[64,512]{1,0:T(8,128)(2,1)S(1)}, u32[]{:S(2)}, u32[]{:S(2)}) collective-permute-start(bf16[64,512]{1,0:T(8,128)(2,1)S(1)} %get-tuple-element.73), channel_id=1, source_target_pairs={{0,6},{1,7},{2,4},{3,5},{4,2},{5,3},{6,0},{7,1},{8,14},{9,15},{10,... | collective-permute-start | bytes 196616 | tf_op jit(solution)/shard_map/ppermute | solution.py:39
  65.8 6.7 %collective-permute-start.22 = (bf16[64,512]{1,0:T(8,128)(2,1)S(1)}, bf16[64,512]{1,0:T(8,128)(2,1)S(1)}, u32[]{:S(2)}, u32[]{:S(2)}) collective-permute-start(bf16[64,512]{1,0:T(8,128)(2,1)S(1)} %get-tuple-element.72), channel_id=1, source_target_pairs={{0,7},{1,6},{2,5},{3,4},{4,3},{5,2},{6,1},{7,0},{8,15},{9,14},{10,... | collective-permute-start | bytes 196616 | tf_op jit(solution)/shard_map/ppermute | solution.py:39
  67.8 4.8 %copy-start.3 = (s32[4]{0:T(128)S(1)}, s32[4]{0:T(128)}, u32[]{:S(2)}) copy-start(s32[4]{0:T(128)} %refs_1_.1) | copy-start | bytes 52
  67.8 4.8 %copy-start.4 = (s32[1,128]{1,0:T(1,128)S(1)}, s32[1,128]{1,0:T(1,128)}, u32[]{:S(2)}) copy-start(s32[1,128]{1,0:T(1,128)} %refs_2_.1) | copy-start | bytes 1540
  68.5 31.2 %collective-permute-start.15 = (bf16[512,512]{1,0:T(8,128)(2,1)S(1)}, bf16[512,512]{1,0:T(8,128)(2,1)S(1)}, u32[]{:S(2)}, u32[]{:S(2)}) collective-permute-start(bf16[512,512]{1,0:T(8,128)(2,1)S(1)} %convolution_convert_fusion.refs_4_), channel_id=1, source_target_pairs={{0,1},{2,3},{4,5},{6,7},{8,9},{10,11},{12,13},{14,15},{16,17},{18,... | collective-permute-start | bytes 1572872 | tf_op jit(solution)/shard_map/ppermute | solution.py:445
  71.0 29.6 %collective-permute-start.14 = (bf16[512,512]{1,0:T(8,128)(2,1)S(1)}, bf16[512,512]{1,0:T(8,128)(2,1)S(1)}, u32[]{:S(2)}, u32[]{:S(2)}) collective-permute-start(bf16[512,512]{1,0:T(8,128)(2,1)S(1)} %convolution_convert_fusion.1.refs_2_), channel_id=1, source_target_pairs={{0,1},{2,3},{4,5},{6,7},{8,9},{10,11},{12,13},{14,15},{16,17},{18,... | collective-permute-start | bytes 1572872 | tf_op jit(solution)/shard_map/ppermute | solution.py:444
  85.2 10.1 %collective-permute-start.23 = (bf16[80,512]{1,0:T(8,128)(2,1)S(1)}, bf16[80,512]{1,0:T(8,128)(2,1)S(1)}, u32[]{:S(2)}, u32[]{:S(2)}) collective-permute-start(bf16[80,512]{1,0:T(8,128)(2,1)S(1)} %get-tuple-element.36), channel_id=1, source_target_pairs={{0,1},{1,0},{2,3},{3,2},{4,5},{5,4},{6,7},{7,6},{8,9},{9,8},{10,11... | collective-permute-start | bytes 245768 | tf_op jit(solution)/shard_map/ppermute | solution.py:39
  85.3 12.3 %collective-permute-start.24 = (bf16[80,512]{1,0:T(8,128)(2,1)S(1)}, bf16[80,512]{1,0:T(8,128)(2,1)S(1)}, u32[]{:S(2)}, u32[]{:S(2)}) collective-permute-start(bf16[80,512]{1,0:T(8,128)(2,1)S(1)} %get-tuple-element.37), channel_id=1, source_target_pairs={{0,2},{1,3},{2,0},{3,1},{4,6},{5,7},{6,4},{7,5},{8,10},{9,11},{10,... | collective-permute-start | bytes 245768 | tf_op jit(solution)/shard_map/ppermute | solution.py:39
  87.1 19.8 %collective-permute-start.25 = (bf16[80,512]{1,0:T(8,128)(2,1)S(1)}, bf16[80,512]{1,0:T(8,128)(2,1)S(1)}, u32[]{:S(2)}, u32[]{:S(2)}) collective-permute-start(bf16[80,512]{1,0:T(8,128)(2,1)S(1)} %get-tuple-element.38), channel_id=1, source_target_pairs={{0,3},{1,2},{2,1},{3,0},{4,7},{5,6},{6,5},{7,4},{8,11},{9,10},{10,... | collective-permute-start | bytes 245768 | tf_op jit(solution)/shard_map/ppermute | solution.py:39
  95.3 11.6 %collective-permute-start.26 = (bf16[80,512]{1,0:T(8,128)(2,1)S(1)}, bf16[80,512]{1,0:T(8,128)(2,1)S(1)}, u32[]{:S(2)}, u32[]{:S(2)}) collective-permute-start(bf16[80,512]{1,0:T(8,128)(2,1)S(1)} %get-tuple-element.39), channel_id=1, source_target_pairs={{0,4},{1,5},{2,6},{3,7},{4,0},{5,1},{6,2},{7,3},{8,12},{9,13},{10,... | collective-permute-start | bytes 245768 | tf_op jit(solution)/shard_map/ppermute | solution.py:39
  97.5 9.4 %collective-permute-start.27 = (bf16[80,512]{1,0:T(8,128)(2,1)S(1)}, bf16[80,512]{1,0:T(8,128)(2,1)S(1)}, u32[]{:S(2)}, u32[]{:S(2)}) collective-permute-start(bf16[80,512]{1,0:T(8,128)(2,1)S(1)} %get-tuple-element.40), channel_id=1, source_target_pairs={{0,5},{1,4},{2,7},{3,6},{4,1},{5,0},{6,3},{7,2},{8,13},{9,12},{10,... | collective-permute-start | bytes 245768 | tf_op jit(solution)/shard_map/ppermute | solution.py:39
  99.7 1.3 copy-start.10
  99.7 8.9 %collective-permute-start.28 = (bf16[80,512]{1,0:T(8,128)(2,1)S(1)}, bf16[80,512]{1,0:T(8,128)(2,1)S(1)}, u32[]{:S(2)}, u32[]{:S(2)}) collective-permute-start(bf16[80,512]{1,0:T(8,128)(2,1)S(1)} %get-tuple-element.41), channel_id=1, source_target_pairs={{0,6},{1,7},{2,4},{3,5},{4,2},{5,3},{6,0},{7,1},{8,14},{9,15},{10,... | collective-permute-start | bytes 245768 | tf_op jit(solution)/shard_map/ppermute | solution.py:39
  100.6 12.6 %copy-start.2 = (f32[1024]{0:T(1024)S(1)}, f32[1024]{0:T(1024)}, u32[]{:S(2)}) copy-start(f32[1024]{0:T(1024)} %param.19) | copy-start | bytes 12292
  100.6 12.5 %collective-permute-start.29 = (bf16[80,512]{1,0:T(8,128)(2,1)S(1)}, bf16[80,512]{1,0:T(8,128)(2,1)S(1)}, u32[]{:S(2)}, u32[]{:S(2)}) collective-permute-start(bf16[80,512]{1,0:T(8,128)(2,1)S(1)} %get-tuple-element.42), channel_id=1, source_target_pairs={{0,7},{1,6},{2,5},{3,4},{4,3},{5,2},{6,1},{7,0},{8,15},{9,14},{10,... | collective-permute-start | bytes 245768 | tf_op jit(solution)/shard_map/ppermute | solution.py:39
  119.3 7.2 %collective-permute-start.30 = (bf16[160,1024]{1,0:T(8,128)(2,1)}, bf16[160,1024]{1,0:T(8,128)(2,1)S(1)}, u32[]{:S(2)}, u32[]{:S(2)}) collective-permute-start(bf16[160,1024]{1,0:T(8,128)(2,1)} %get-tuple-element.46), channel_id=1, source_target_pairs={{0,1},{1,0},{2,3},{3,2},{4,5},{5,4},{6,7},{7,6},{8,9},{9,8},{10,11... | collective-permute-start | bytes 983048 | tf_op jit(solution)/shard_map/ppermute | solution.py:39
  119.4 17.8 %collective-permute-start.31 = (bf16[160,1024]{1,0:T(8,128)(2,1)}, bf16[160,1024]{1,0:T(8,128)(2,1)S(1)}, u32[]{:S(2)}, u32[]{:S(2)}) collective-permute-start(bf16[160,1024]{1,0:T(8,128)(2,1)} %get-tuple-element.47), channel_id=1, source_target_pairs={{0,2},{1,3},{2,0},{3,1},{4,6},{5,7},{6,4},{7,5},{8,10},{9,11},{10,... | collective-permute-start | bytes 983048 | tf_op jit(solution)/shard_map/ppermute | solution.py:39
  122.6 23.0 %collective-permute-start.32 = (bf16[160,1024]{1,0:T(8,128)(2,1)}, bf16[160,1024]{1,0:T(8,128)(2,1)S(1)}, u32[]{:S(2)}, u32[]{:S(2)}) collective-permute-start(bf16[160,1024]{1,0:T(8,128)(2,1)} %get-tuple-element.48), channel_id=1, source_target_pairs={{0,3},{1,2},{2,1},{3,0},{4,7},{5,6},{6,5},{7,4},{8,11},{9,10},{10,... | collective-permute-start | bytes 983048 | tf_op jit(solution)/shard_map/ppermute | solution.py:39
  122.6 42.1 %collective-permute-start.36 = (bf16[160,1024]{1,0:T(8,128)(2,1)}, bf16[160,1024]{1,0:T(8,128)(2,1)S(1)}, u32[]{:S(2)}, u32[]{:S(2)}) collective-permute-start(bf16[160,1024]{1,0:T(8,128)(2,1)} %get-tuple-element.53), channel_id=1, source_target_pairs={{0,4},{1,5},{2,6},{3,7},{4,0},{5,1},{6,2},{7,3},{8,12},{9,13},{10,... | collective-permute-start | bytes 983048 | tf_op jit(solution)/shard_map/ppermute | solution.py:39
  123.8 44.2 %collective-permute-start.37 = (bf16[160,1024]{1,0:T(8,128)(2,1)}, bf16[160,1024]{1,0:T(8,128)(2,1)S(1)}, u32[]{:S(2)}, u32[]{:S(2)}) collective-permute-start(bf16[160,1024]{1,0:T(8,128)(2,1)} %get-tuple-element.54), channel_id=1, source_target_pairs={{0,5},{1,4},{2,7},{3,6},{4,1},{5,0},{6,3},{7,2},{8,13},{9,12},{10,... | collective-permute-start | bytes 983048 | tf_op jit(solution)/shard_map/ppermute | solution.py:39
  126.5 43.9 %collective-permute-start.38 = (bf16[160,1024]{1,0:T(8,128)(2,1)}, bf16[160,1024]{1,0:T(8,128)(2,1)S(1)}, u32[]{:S(2)}, u32[]{:S(2)}) collective-permute-start(bf16[160,1024]{1,0:T(8,128)(2,1)} %get-tuple-element.55), channel_id=1, source_target_pairs={{0,6},{1,7},{2,4},{3,5},{4,2},{5,3},{6,0},{7,1},{8,14},{9,15},{10,... | collective-permute-start | bytes 983048 | tf_op jit(solution)/shard_map/ppermute | solution.py:39
  137.2 8.4 %copy-start.13 = (bf16[160,1024]{1,0:T(8,128)(2,1)}, bf16[160,1024]{1,0:T(8,128)(2,1)S(1)}, u32[]{:S(2)}) copy-start(bf16[160,1024]{1,0:T(8,128)(2,1)S(1)} %collective-permute-done.31.refs_2_) | copy-start | bytes 983044
  137.2 41.3 %collective-permute-start.39 = (bf16[160,1024]{1,0:T(8,128)(2,1)}, bf16[160,1024]{1,0:T(8,128)(2,1)S(1)}, u32[]{:S(2)}, u32[]{:S(2)}) collective-permute-start(bf16[160,1024]{1,0:T(8,128)(2,1)} %get-tuple-element.56), channel_id=1, source_target_pairs={{0,7},{1,6},{2,5},{3,4},{4,3},{5,2},{6,1},{7,0},{8,15},{9,14},{10,... | collective-permute-start | bytes 983048 | tf_op jit(solution)/shard_map/ppermute | solution.py:39
  145.6 0.7 copy-start.14
  164.7 35.5 %collective-permute-start.33 = (bf16[160,1024]{1,0:T(8,128)(2,1)S(1)}, bf16[160,1024]{1,0:T(8,128)(2,1)S(1)}, u32[]{:S(2)}, u32[]{:S(2)}) collective-permute-start(bf16[160,1024]{1,0:T(8,128)(2,1)S(1)} %get-tuple-element.50), channel_id=1, source_target_pairs={{0,1},{1,0},{2,3},{3,2},{4,5},{5,4},{6,7},{7,6},{8,9},{9,8},{10,11... | collective-permute-start | bytes 983048 | tf_op jit(solution)/shard_map/ppermute | solution.py:39
  164.8 35.6 %collective-permute-start.34 = (bf16[160,1024]{1,0:T(8,128)(2,1)S(1)}, bf16[160,1024]{1,0:T(8,128)(2,1)S(1)}, u32[]{:S(2)}, u32[]{:S(2)}) collective-permute-start(bf16[160,1024]{1,0:T(8,128)(2,1)S(1)} %get-tuple-element.51), channel_id=1, source_target_pairs={{0,2},{1,3},{2,0},{3,1},{4,6},{5,7},{6,4},{7,5},{8,10},{9,11},{10,... | collective-permute-start | bytes 983048 | tf_op jit(solution)/shard_map/ppermute | solution.py:39
  168.0 34.4 %copy-start.6 = (s32[8,512]{0,1:T(8,128)S(1)}, s32[8,512]{0,1:T(8,128)}, u32[]{:S(2)}) copy-start(s32[8,512]{0,1:T(8,128)} %get-tuple-element.89) | copy-start | bytes 49156
  168.0 34.6 %collective-permute-start.35 = (bf16[160,1024]{1,0:T(8,128)(2,1)S(1)}, bf16[160,1024]{1,0:T(8,128)(2,1)S(1)}, u32[]{:S(2)}, u32[]{:S(2)}) collective-permute-start(bf16[160,1024]{1,0:T(8,128)(2,1)S(1)} %get-tuple-element.52), channel_id=1, source_target_pairs={{0,3},{1,2},{2,1},{3,0},{4,7},{5,6},{6,5},{7,4},{8,11},{9,10},{10,... | collective-permute-start | bytes 983048 | tf_op jit(solution)/shard_map/ppermute | solution.py:39
  170.4 8.1 %copy-start.11 = (bf16[160,1024]{1,0:T(8,128)(2,1)}, bf16[160,1024]{1,0:T(8,128)(2,1)S(1)}, u32[]{:S(2)}) copy-start(bf16[160,1024]{1,0:T(8,128)(2,1)S(1)} %collective-permute-done.38.refs_2_) | copy-start | bytes 983044
  178.5 0.7 copy-start.12
  197.6 34.4 %collective-permute-start.40 = (bf16[160,1024]{1,0:T(8,128)(2,1)S(1)}, bf16[160,1024]{1,0:T(8,128)(2,1)S(1)}, u32[]{:S(2)}, u32[]{:S(2)}) collective-permute-start(bf16[160,1024]{1,0:T(8,128)(2,1)S(1)} %get-tuple-element.57), channel_id=1, source_target_pairs={{0,4},{1,5},{2,6},{3,7},{4,0},{5,1},{6,2},{7,3},{8,12},{9,13},{10,... | collective-permute-start | bytes 983048 | tf_op jit(solution)/shard_map/ppermute | solution.py:39
  197.7 41.4 %collective-permute-start.41 = (bf16[160,1024]{1,0:T(8,128)(2,1)S(1)}, bf16[160,1024]{1,0:T(8,128)(2,1)S(1)}, u32[]{:S(2)}, u32[]{:S(2)}) collective-permute-start(bf16[160,1024]{1,0:T(8,128)(2,1)S(1)} %get-tuple-element.58), channel_id=1, source_target_pairs={{0,5},{1,4},{2,7},{3,6},{4,1},{5,0},{6,3},{7,2},{8,13},{9,12},{10,... | collective-permute-start | bytes 983048 | tf_op jit(solution)/shard_map/ppermute | solution.py:39
  200.2 45.8 %collective-permute-start.42 = (bf16[160,1024]{1,0:T(8,128)(2,1)S(1)}, bf16[160,1024]{1,0:T(8,128)(2,1)S(1)}, u32[]{:S(2)}, u32[]{:S(2)}) collective-permute-start(bf16[160,1024]{1,0:T(8,128)(2,1)S(1)} %get-tuple-element.59), channel_id=1, source_target_pairs={{0,6},{1,7},{2,4},{3,5},{4,2},{5,3},{6,0},{7,1},{8,14},{9,15},{10,... | collective-permute-start | bytes 983048 | tf_op jit(solution)/shard_map/ppermute | solution.py:39
  200.4 52.7 %collective-permute-start.43 = (bf16[160,1024]{1,0:T(8,128)(2,1)S(1)}, bf16[160,1024]{1,0:T(8,128)(2,1)S(1)}, u32[]{:S(2)}, u32[]{:S(2)}) collective-permute-start(bf16[160,1024]{1,0:T(8,128)(2,1)S(1)} %get-tuple-element.60), channel_id=1, source_target_pairs={{0,7},{1,6},{2,5},{3,4},{4,3},{5,2},{6,1},{7,0},{8,15},{9,14},{10,... | collective-permute-start | bytes 983048 | tf_op jit(solution)/shard_map/ppermute | solution.py:39
  202.6 54.5 %copy-start.1 = (bf16[1024,8]{0,1:T(8,128)(2,1)S(1)}, bf16[1024,8]{0,1:T(8,128)(2,1)}, u32[]{:S(2)}) copy-start(bf16[1024,8]{0,1:T(8,128)(2,1)} %param.20) | copy-start | bytes 49156

commit v2 on v1

v2 whole, which is shorter than its diff:
```python
import functools
import math

import jax
import jax.numpy as jnp
from jax import lax
from jax.experimental import pallas as pl
from jax.experimental.pallas import tpu as pltpu
from jax.sharding import PartitionSpec as P

HD = 64
EXT = 16
EPSILON = 1e-06
NEGATIVE = -1e30
F32, BF16 = jnp.float32, jnp.bfloat16
NT = (((1,), (1,)), ((), ()))
VMEM_LIMIT = 52 * 1024 * 1024
AXES = ("batch", "tensor")


def dot(a, b, dims=(((1,), (0,)), ((), ()))):
    return lax.dot_general(a, b, dims, preferred_element_type=F32)


def vmem(count):
    return [pl.BlockSpec(memory_space=pltpu.VMEM)] * count


def smem(count):
    return [pl.BlockSpec(memory_space=pltpu.SMEM)] * count


def params():
    return pltpu.CompilerParams(vmem_limit_bytes=VMEM_LIMIT)


def send(value, mask, lanes, groups):
    total = lanes * groups
    return lax.ppermute(value, AXES, [(i, i ^ mask) for i in range(total)])


def gather_high(piece, lanes, groups):
    low = max(1, lanes // 4)
    return jnp.stack([piece] + [send(piece, s, lanes, groups) for s in range(low, lanes, low)])


def gather_plane(block, lanes, groups):
    low = max(1, lanes // 4)
    rows = []
    for j in range(0, groups, 2):
        masks = [j * lanes + s for s in range(low)]
        rows.append(
            jnp.stack([send(block, m, lanes, groups) if m else block for m in masks], axis=1)
        )
    return jnp.stack(rows).reshape((groups // 2, lanes) + block.shape[1:])


def after(value, *others):
    return lax.optimization_barrier((value,) + others)[0]


def ones_rows(keys):
    return jnp.ones((EXT, keys), BF16)


def softmax_steps(scores, values, old):
    tops = [jnp.maximum(m, jnp.max(s, axis=0, keepdims=True)) for s, (m, acc) in zip(scores, old)]
    return [
        (top, acc * jnp.exp2(m - top) + dot(v, jnp.exp2(s - top).astype(BF16)))
        for s, v, top, (m, acc) in zip(scores, values, tops, old)
    ]


def cached_kernel(requests, span_devs, block_pages, lengths, table, q_ref, kv_ref, out_ref, q_all, m_ref, acc_ref):
    page = kv_ref.shape[1]
    pages = table.shape[1] // requests
    rows = q_ref.shape[2]
    queries = rows * span_devs
    keys = block_pages * page
    tile = min(256, queries)
    tiles = [slice(t, t + tile) for t in range(0, queries, tile)]
    q_all[HD : 2 * HD, :] = jnp.zeros((HD, queries), BF16)

    def one_request(request, carry):
        length = lengths[request]
        for i in range(span_devs):
            q_all[0:HD, i * rows : (i + 1) * rows] = q_ref[request * span_devs + i]
        m_ref[...] = jnp.full((1, queries), NEGATIVE, F32)
        acc_ref[...] = jnp.zeros((HD + EXT, queries), F32)

        def block(j, masked):
            parts = [
                kv_ref[
                    table[0, request * pages + jnp.minimum(j * block_pages + n, pages - 1)]
                ]
                for n in range(block_pages)
            ]
            both = jnp.concatenate(parts, axis=0)
            values = jnp.concatenate([both.T[HD : 2 * HD], ones_rows(keys)], axis=0)
            scores = [dot(both, q_all[:, at]) for at in tiles]
            if masked:
                position = j * keys + lax.broadcasted_iota(jnp.int32, scores[0].shape, 0)
                scores = [jnp.where(position < length, s, NEGATIVE) for s in scores]
            old = [(m_ref[:, at], acc_ref[:, at]) for at in tiles]
            new = softmax_steps(scores, [values] * len(tiles), old)
            for at, (top, acc) in zip(tiles, new):
                m_ref[:, at] = top
                acc_ref[:, at] = acc

        whole = length // keys

        def step(j, c):
            block(j, False)
            return c

        lax.fori_loop(0, whole, step, 0)

        @pl.when(whole * keys < length)
        def _():
            block(whole, True)

        total = acc_ref[HD : HD + 1, :]
        lse = m_ref[...] + jnp.log2(total)
        hi = lse.astype(BF16).astype(F32)
        mid = (lse - hi).astype(BF16).astype(F32)
        lo = lse - hi - mid
        at_row = lax.broadcasted_iota(jnp.int32, (EXT, queries), 0)
        stats = jnp.where(
            at_row == 0, hi, jnp.where(at_row == 1, mid, jnp.where(at_row == 2, lo, 0.0))
        ).astype(BF16)
        values = (acc_ref[0:HD, :] * (1.0 / total)).astype(BF16)
        for i in range(span_devs):
            at = slice(i * rows, (i + 1) * rows)
            out_ref[request * span_devs + i, 0:HD, :] = values[:, at]
            out_ref[request * span_devs + i, HD : HD + EXT, :] = stats[:, at]
        return carry

    lax.fori_loop(0, requests, one_request, 0)


def cached_attention(lengths, table, q, kv_cache):
    lanes, _, rows = q.shape
    requests = lengths.shape[0]
    span_devs = lanes // requests
    queries = rows * span_devs
    return pl.pallas_call(
        functools.partial(cached_kernel, requests, span_devs, 4),
        out_shape=jax.ShapeDtypeStruct((lanes, HD + EXT, rows), BF16),
        in_specs=smem(2) + vmem(2),
        out_specs=pl.BlockSpec(memory_space=pltpu.VMEM),
        scratch_shapes=[
            pltpu.VMEM((2 * HD, queries), BF16),
            pltpu.VMEM((1, queries), F32),
            pltpu.VMEM((HD + EXT, queries), F32),
        ],
        compiler_params=params(),
        cost_estimate=pl.CostEstimate(
            flops=8 * 10**9, bytes_accessed=6 * 10**6, transcendentals=8 * 10**6
        ),
        name="cached_attention",
    )(lengths, table, q, kv_cache)


def query_kernel(scale, info, normed, even, odd, out_ref):
    lanes, _, rows = out_ref.shape
    halves, _, _, share = even.shape
    total = jnp.zeros((lanes * HD, rows), F32)
    for n in range(halves):
        for low, ref in enumerate((even, odd)):
            at = jnp.bitwise_xor(info[1], 2 * n + low) * share
            columns = normed[:, pl.ds(pl.multiple_of(at, share), share)]
            total = total + dot(ref[n].reshape(lanes * HD, share), columns, NT)
    q = (total * scale).astype(BF16)
    for s in range(lanes):
        out_ref[jnp.bitwise_xor(info[0], s)] = q[s * HD : (s + 1) * HD]


def project_queries(info, normed, even, odd):
    lanes = even.shape[1]
    rows = normed.shape[0]
    scale = math.log2(math.e) / math.sqrt(HD)
    return pl.pallas_call(
        functools.partial(query_kernel, scale),
        out_shape=jax.ShapeDtypeStruct((lanes, HD, rows), BF16),
        in_specs=smem(1) + vmem(3),
        out_specs=pl.BlockSpec(memory_space=pltpu.VMEM),
        compiler_params=params(),
        cost_estimate=pl.CostEstimate(flops=10**9, bytes_accessed=2 * 10**6, transcendentals=0),
        name="project_queries",
    )(info, normed, even, odd)


def self_kernel(span_devs, *refs):
    info, q_ref = refs[:2]
    normed_refs = refs[2 : 2 + span_devs]
    even, odd = refs[2 + span_devs : 4 + span_devs]
    out_ref, w_o_ref, w_k, w_v, keys_ref, values_ref = refs[5 + span_devs :]
    lanes, _, rows = q_ref.shape
    halves, _, _, share = even.shape
    groups = 2 * halves
    me, group = info[0], info[1]
    at = me % span_devs

    for n in range(halves):
        for low, ref in enumerate((even, odd)):
            column = pl.ds(
                pl.multiple_of(jnp.bitwise_xor(group, 2 * n + low) * share, share), share
            )
            for h in range(lanes):
                piece = ref[n, jnp.bitwise_xor(me, h)]
                head = slice(h * HD, (h + 1) * HD)
                w_k[head, column] = piece[0:HD]
                w_v[head, column] = piece[HD : 2 * HD]
                w_o_ref[head, column] = piece[2 * HD : 3 * HD]

    def project(normed):
        keys_ref[...] = dot(normed[...], w_k[...], NT).astype(BF16)
        values_ref[...] = dot(w_v[...], normed[...], NT).astype(BF16)

    together = 4
    tile = min(256, rows)

    def run(causal):
        def step(g, carry):
            scores, values, old, places = [], [], [], []
            nothing = jnp.zeros((HD, tile), BF16)
            for p in range(together // 2):
                block = pl.multiple_of((g * together + 2 * p) * HD, 2 * HD)
                keys = keys_ref[:, pl.ds(block, 2 * HD)]
                both_v = values_ref[pl.ds(block, 2 * HD), :]
                for h in range(2):
                    s = g * together + 2 * p + h
                    q = q_ref[s]
                    value = jnp.concatenate([both_v[h * HD : (h + 1) * HD], ones_rows(rows)], axis=0)
                    for t in range(0, rows, tile):
                        here = slice(t, t + tile)
                        seen = t + tile if causal else rows
                        part = [nothing, q[:, here]] if h else [q[:, here], nothing]
                        score = dot(keys[0:seen], jnp.concatenate(part, axis=0))
                        if causal:
                            position = lax.broadcasted_iota(jnp.int32, score.shape, 0)
                            line = t + lax.broadcasted_iota(jnp.int32, score.shape, 1)
                            score = jnp.where(position <= line, score, NEGATIVE)
                            m = jnp.full((1, tile), NEGATIVE, F32)
                            acc = jnp.zeros((HD + EXT, tile), F32)
                        else:
                            m = out_ref[s, HD + EXT : HD + EXT + 1, here]
                            acc = out_ref[s, 0 : HD + EXT, here]
                        scores.append(score)
                        values.append(value[:, 0:seen])
                        old.append((m, acc))
                        places.append((s, here))
            for (s, here), (top, acc) in zip(places, softmax_steps(scores, values, old)):
                out_ref[s, 0 : HD + EXT, here] = acc
                out_ref[s, HD + EXT : HD + EXT + 8, here] = jnp.broadcast_to(top, (8, tile))
            return carry

        lax.fori_loop(0, lanes // together, step, 0)

    project(normed_refs[0])
    run(True)
    for other in range(1, span_devs):

        @pl.when(jnp.bitwise_xor(at, other) < at)
        def _(other=other):
            project(normed_refs[other])
            run(False)


def self_attention(info, q, normed, even, odd, earlier):
    span_devs = len(normed)
    lanes, _, rows = q.shape
    width = normed[0].shape[1]
    anywhere = [pl.BlockSpec(memory_space=pl.ANY)]
    return pl.pallas_call(
        functools.partial(self_kernel, span_devs),
        out_shape=[
            jax.ShapeDtypeStruct((lanes, HD + EXT + 8, rows), F32),
            jax.ShapeDtypeStruct((lanes * HD, width), BF16),
        ],
        in_specs=smem(1) + vmem(3 + span_devs) + anywhere,
        out_specs=vmem(2),
        scratch_shapes=[
            pltpu.VMEM((lanes * HD, width), BF16),
            pltpu.VMEM((lanes * HD, width), BF16),
            pltpu.VMEM((rows, lanes * HD), BF16),
            pltpu.VMEM((lanes * HD, rows), BF16),
        ],
        compiler_params=params(),
        cost_estimate=pl.CostEstimate(
            flops=4 * 10**9, bytes_accessed=5 * 10**6, transcendentals=4 * 10**6
        ),
        name="self_attention",
    )(info, q, *normed, even, odd, earlier)


def fill(out_refs, which, normed, slot_rows, placing):
    cap = out_refs[0].shape[0]
    rows = normed.shape[0]
    for n, s in enumerate(which):
        at_slot = lax.broadcasted_iota(jnp.int32, (cap, rows), 0)
        placing[n * cap : (n + 1) * cap, :] = (
            (at_slot == slot_rows[s : s + 1, :]).astype(F32).astype(BF16)
        )
    for n in range(len(which)):
        out_refs[n][...] = dot(placing[n * cap : (n + 1) * cap, :], normed).astype(BF16)


def dispatch_kernel(which, *refs):
    normed, slot_rows = refs[:2]
    out_refs = refs[3 : 3 + len(which)]
    fill(out_refs, which, normed[...], slot_rows, refs[3 + len(which)])


def dispatch(normed, slot_rows, which, cap, earlier):
    rows, width = normed.shape
    return pl.pallas_call(
        functools.partial(dispatch_kernel, tuple(which)),
        out_shape=[jax.ShapeDtypeStruct((cap, width), BF16)] * len(which),
        in_specs=vmem(2) + [pl.BlockSpec(memory_space=pl.ANY)],
        out_specs=vmem(len(which)),
        scratch_shapes=[pltpu.VMEM((len(which) * cap, rows), BF16)],
        compiler_params=params(),
        cost_estimate=pl.CostEstimate(
            flops=2 * len(which) * cap * rows * width, bytes_accessed=10**6, transcendentals=0
        ),
        name="dispatch",
    )(normed, slot_rows, earlier)


def merge_kernel(which, tokens, own, cached, w_o, gain, router, hits, slot_rows, *refs):
    state_ref, gates_ref, normed_ref = refs[:3]
    out_refs = refs[3 : 3 + len(which)]
    attended, placing = refs[3 + len(which) :]
    for s in range(own.shape[0]):
        part = cached[s].astype(F32)
        lse = part[HD : HD + 1] + part[HD + 1 : HD + 2] + part[HD + 2 : HD + 3]
        m = own[s, HD + EXT : HD + EXT + 1, :]
        total = own[s, HD : HD + 1, :]
        top = jnp.maximum(m, lse)
        w_cached, w_own = jnp.exp2(lse - top), jnp.exp2(m - top)
        norm = 1.0 / (w_cached + w_own * total)
        merged = part[0:HD] * (w_cached * norm) + own[s, 0:HD, :] * (w_own * norm)
        attended[s * HD : (s + 1) * HD, :] = merged.astype(BF16)
    state = tokens[...].astype(F32) + dot(attended[...].T, w_o[...])
    state_ref[...] = state
    mean_square = jnp.mean(state * state, axis=-1, keepdims=True)
    normed = (state * lax.rsqrt(mean_square + EPSILON) * gain[...]).astype(BF16)
    logits = dot(normed, router[...])
    squashed = jnp.where(hits[...] > 0, jax.nn.sigmoid(logits), 0.0)
    gates_ref[...] = squashed / jnp.sum(squashed, axis=1, keepdims=True)
    normed_ref[...] = normed
    fill(out_refs, which, normed, slot_rows, placing)


def merge_dispatch(tokens, own, cached, w_o, gain, router, hits, slot_rows, which, cap):
    lanes = own.shape[0]
    rows, width = tokens.shape
    return pl.pallas_call(
        functools.partial(merge_kernel, tuple(which)),
        out_shape=[
            jax.ShapeDtypeStruct((rows, width), F32),
            jax.ShapeDtypeStruct((rows, lanes), F32),
            jax.ShapeDtypeStruct((rows, width), BF16),
        ]
        + [jax.ShapeDtypeStruct((cap, width), BF16)] * len(which),
        in_specs=vmem(8),
        out_specs=vmem(3 + len(which)),
        scratch_shapes=[
            pltpu.VMEM((lanes * HD, rows), BF16),
            pltpu.VMEM((len(which) * cap, rows), BF16),
        ],
        compiler_params=params(),
        cost_estimate=pl.CostEstimate(
            flops=4 * 10**9, bytes_accessed=10 * 10**6, transcendentals=10**5
        ),
        name="merge_and_dispatch",
    )(tokens, own, cached, w_o, gain, router, hits, slot_rows)


def expert_kernel(count, *refs):
    x_refs = refs[:count]
    gate_ref, up_ref, down_ref = refs[count : count + 3]
    out_refs = refs[count + 4 : 2 * count + 4]
    x_all, total = refs[2 * count + 4 :]
    cap = x_refs[0].shape[0]
    step = pl.program_id(0)

    @pl.when(step == 0)
    def _():
        for n in range(count):
            x_all[n * cap : (n + 1) * cap, :] = x_refs[n][...]

    x = x_all[...]
    gate = dot(x, gate_ref[0])
    up = dot(x, up_ref[0])
    active = (jax.nn.gelu(gate, approximate=True) * up).astype(BF16)
    part = dot(active, down_ref[0])

    @pl.when(step == 0)
    def _():
        total[...] = part

    @pl.when(step > 0)
    def _():
        total[...] += part

    @pl.when(step == pl.num_programs(0) - 1)
    def _():
        for n in range(count):
            out_refs[n][...] = total[n * cap : (n + 1) * cap, :].astype(BF16)


def expert(chunks, w_in, w_out, earlier):
    count = len(chunks)
    cap, width = chunks[0].shape
    hidden = w_out.shape[1]
    tile = 256
    steps = hidden // tile
    whole = pl.BlockSpec((cap, width), lambda j: (0, 0))
    return pl.pallas_call(
        functools.partial(expert_kernel, count),
        grid=(steps,),
        out_shape=[jax.ShapeDtypeStruct((cap, width), BF16)] * count,
        in_specs=[whole] * count
        + [
            pl.BlockSpec((1, width, tile), lambda j: (0, 0, j)),
            pl.BlockSpec((1, width, tile), lambda j: (0, 0, j + steps)),
            pl.BlockSpec((1, tile, width), lambda j: (0, j, 0)),
            pl.BlockSpec(memory_space=pl.ANY),
        ],
        out_specs=[whole] * count,
        scratch_shapes=[
            pltpu.VMEM((count * cap, width), BF16),
            pltpu.VMEM((count * cap, width), F32),
        ],
        compiler_params=params(),
        cost_estimate=pl.CostEstimate(
            flops=6 * count * cap * width * hidden,
            bytes_accessed=6 * width * hidden,
            transcendentals=count * cap * hidden,
        ),
        name="expert",
    )(*chunks, w_in, w_in, w_out, earlier)


def combine_kernel(first, count, last, *refs):
    base, gates, slots = refs[:3]
    parts = refs[3 : 3 + count]
    out = refs[3 + count]
    rows = base.shape[0]
    cap = parts[0].shape[0]
    total = base[...]
    for n in range(count):
        s = first + n
        lane = lax.broadcasted_iota(jnp.int32, (rows, cap), 1)
        pick = (lane == slots[:, s : s + 1]).astype(F32).astype(BF16)
        total = total + gates[:, s : s + 1] * dot(pick, parts[n][...])
    out[...] = total.astype(out.dtype)


def combine(base, gates, slots, parts, first, last):
    count = len(parts)
    rows, width = base.shape
    return pl.pallas_call(
        functools.partial(combine_kernel, first, count, last),
        out_shape=jax.ShapeDtypeStruct((rows, width), BF16 if last else F32),
        in_specs=vmem(3 + count),
        out_specs=pl.BlockSpec(memory_space=pltpu.VMEM),
        compiler_params=params(),
        cost_estimate=pl.CostEstimate(
            flops=2 * count * rows * parts[0].shape[0] * width,
            bytes_accessed=6 * 10**6,
            transcendentals=0,
        ),
        name="combine",
    )(base, gates, slots, *parts)


def body(
    tokens,
    gain_attn,
    w_qkv,
    w_attn_out,
    kv_cache,
    page_table,
    cached_lengths,
    gain_moe,
    w_router,
    routes,
    w_in,
    w_out,
):
    lanes, groups = lax.axis_size("tensor"), lax.axis_size("batch")
    me, group = lax.axis_index("tensor"), lax.axis_index("batch")
    rows, width = tokens.shape
    requests = cached_lengths.shape[0]
    span_devs = lanes // requests
    share = width // groups
    info = jnp.stack([me, group]).astype(jnp.int32)

    w_t = w_qkv.T
    q_plane = gather_plane(gather_high(w_t[0:HD], lanes, groups), lanes, groups)
    q_other = send(q_plane, lanes, lanes, groups)
    values = tokens.astype(F32)
    mean_square = jnp.mean(values * values, axis=-1, keepdims=True)
    normed = (values * lax.rsqrt(mean_square + EPSILON) * gain_attn).astype(BF16)
    q = project_queries(info, normed, q_plane, q_other)
    q_here = lax.all_to_all(q, "tensor", split_axis=0, concat_axis=0, tiled=True)

    near = [normed]
    ready = after(normed, q_plane)
    for i in range(1, span_devs):
        pairs = [
            (b * lanes + t, b * lanes + (t ^ i))
            for b in range(groups)
            for t in range(lanes)
            if t % span_devs < (t ^ i) % span_devs
        ]
        near.append(lax.ppermute(ready, AXES, pairs))
    rest = jnp.concatenate([w_t[HD : 3 * HD], w_attn_out.T], axis=0)
    rest = gather_high(after(rest, q_other), lanes, groups)
    rest = gather_plane(rest, lanes, groups)
    rest_other = send(rest, lanes, lanes, groups)

    parts = cached_attention(cached_lengths, page_table, q_here, kv_cache)
    cached = lax.all_to_all(parts, "tensor", split_axis=0, concat_axis=0, tiled=True)
    own, w_o = self_attention(info, q, near, rest, rest_other, parts)

    names = me ^ jnp.arange(lanes, dtype=jnp.int32)
    hit_rows = (routes[:, 0][None, :] == names[:, None]) | (routes[:, 1][None, :] == names[:, None])
    earlier = jnp.triu(jnp.ones((rows, rows), BF16), 1)
    rank = dot(hit_rows.astype(BF16), earlier).astype(jnp.int32)
    slot_rows = jnp.where(hit_rows, rank, -1)
    slots = slot_rows.T
    hits = hit_rows.astype(jnp.int32).T
    capacity = max(2, (5 * rows * routes.shape[1] + 4 * lanes - 1) // (4 * lanes))
    cap = -(-capacity // 16) * 16
    router = jnp.take(w_router, names, axis=1)

    half, quarter = lanes // 2, lanes // 4
    near = list(range(half))
    far = [list(range(half, half + quarter)), list(range(half + quarter, lanes))]
    outcome = merge_dispatch(
        tokens,
        own,
        cached,
        w_o,
        gain_moe.reshape(1, width),
        router,
        hits,
        slot_rows,
        far[0] + near,
        cap,
    )
    state, gates, normed_moe = outcome[:3]
    buffers = dict(zip(far[0] + near, outcome[3:]))
    arrived = {s: send(buffers[s], s, lanes, groups) if s else buffers[s] for s in buffers}
    buffers.update(zip(far[1], dispatch(normed_moe, slot_rows, far[1], cap, arrived[near[-1]])))
    arrived.update({s: send(buffers[s], s, lanes, groups) for s in far[1]})
    mixed = state
    results = [gates]
    for part in (near, far[0], far[1]):
        results = expert([arrived[s] for s in part], w_in, w_out, results[0])
        returned = [
            results[n] if s == 0 else send(results[n], s, lanes, groups)
            for n, s in enumerate(part)
        ]
        mixed = combine(mixed, gates, slots, returned, part[0], part is far[1])
    return mixed


def solution(mesh):
    in_specs = (
        P(("batch", "tensor"), None),
        P(),
        P("batch", "tensor"),
        P("batch", "tensor"),
        P("batch", None, "tensor"),
        P("batch", None),
        P("batch"),
        P(),
        P(),
        P(("batch", "tensor"), None),
        P("tensor", None, None),
        P("tensor", None, None),
    )
    out_specs = P(("batch", "tensor"), None)
    return jax.shard_map(body, mesh=mesh, in_specs=in_specs, out_specs=out_specs, check_vma=False)
```

time: 261 us -> 236 us (0.904)
  waiting for transfers between devices: 116 us -> 83.9 us
  Pallas kernels: 69.7 us -> 89.6 us
  starting transfers between devices: 55 us -> 49.8 us
  local copies, waits for them, and re-layouts: 8.02 us -> 4.35 us
    ppermute x42 -> x28, waiting for transfers between devices: 116 us -> 76.2 us  [send(): return lax.ppermute(value, AXES, [(i, i ^ mask) for i in range(total)])]
    ppermute x42 -> x28, starting transfers between devices: 51.1 us -> 38.4 us  [send(): return lax.ppermute(value, AXES, [(i, i ^ mask) for i in range(total)])]
    pallas_call x2 -> x3, Pallas kernels: 36.7 us -> 46.6 us  [expert(): pl.pallas_call(functools.partial(expert_kernel, count), grid=(steps,), ou...]
    all_to_all x0 -> x2, starting transfers between devices: none -> 7.98 us  [the longest x1 4.54 us: body(): lax.all_to_all(parts, 'tensor', split_axis=0, concat_axis=0, tiled=True)]
    ppermute x2 -> x1, waiting for transfers between devices: 0.01 us -> 7.67 us  [body(): near.append(lax.ppermute(ready, AXES, pairs))]
    pallas_call x3 -> x5, Pallas kernels: 24.6 us -> 31.5 us  [the longest x1 13.5 us: cached_attention(): pl.pallas_call(functools.partial(cached_kernel, requests, span_devs, 4),...]
    pallas_call x2 -> x3, Pallas kernels: 8.44 us -> 11.5 us  [combine(): pl.pallas_call(functools.partial(combine_kernel, first, count, last), out...]
    unnamed x35 -> x28, local copies, waits for them, and re-layouts: 3.79 us -> 0.8 us
  transfers between devices with their start and end apart: 44 -> 31, of which waited for: 23 -> 20; matrix products, arithmetic and copies ran while one was open for 5% -> 3% of each run, Pallas kernels for 23% -> 35%
where the time goes in v2:
time: 236 us; the launch traced here: 233 us
  Pallas kernels  89.6 us (38%)
  waiting for transfers between devices  83.9 us (36%)
  starting transfers between devices  49.8 us (21%)
  local copies, waits for them, and re-layouts  4.35 us (2%)
  other arithmetic  3.87 us (2%)
    ppermute x28, waiting for transfers between devices, send(): return lax.ppermute(value, AXES, [(i, i ^ mask) for i in range(total)])  76.2 us
    pallas_call x3, Pallas kernels, expert(): pl.pallas_call(functools.partial(expert_kernel, count), grid=(steps,), ou...  46.6 us
    ppermute x28, starting transfers between devices, send(): return lax.ppermute(value, AXES, [(i, i ^ mask) for i in range(total)])  38.4 us
    pallas_call x1, Pallas kernels, cached_attention(): pl.pallas_call(functools.partial(cached_kernel, requests, span_devs, 4),...  13.5 us
    pallas_call x3, Pallas kernels, combine(): pl.pallas_call(functools.partial(combine_kernel, first, count, last), out...  11.5 us
    pallas_call x1, Pallas kernels, self_attention(): pl.pallas_call(functools.partial(self_kernel, span_devs), out_shape=[jax....  7.79 us
    ppermute x1, waiting for transfers between devices, body(): near.append(lax.ppermute(ready, AXES, pairs))  7.67 us
    pallas_call x1, Pallas kernels, merge_dispatch(): pl.pallas_call(functools.partial(merge_kernel, tuple(which)), out_shape=[...  5.49 us
  transfers between devices with their start and end apart: 31, of which 20 were waited for; matrix products, arithmetic and copies ran while one was open for 3% of the time, Pallas kernels for 35%

profile of v2, /device:TPU:9, one launch (start us, length us, event | category | flops | bytes accessed | tf_op | source)
XLA Modules:
  0.0 233.2 jit_solution(11904776391438894022)
XLA Ops:
  0.0 0.8 slice_bitcast_fusion
  0.8 2.5 %collective-permute-start.1 = (bf16[64,256]{1,0:T(8,128)(2,1)S(1)}, bf16[64,256]{1,0:T(8,128)(2,1)S(1)}, u32[]{:S(2)}, u32[]{:S(2)}) collective-permute-start(bf16[64,256]{1,0:T(8,128)(2,1)S(1)} %get-tuple-element.56), channel_id=1, source_target_pairs={{0,4},{1,5},{2,6},{3,7},{4,0},{5,1},{6,2},{7,3},{8,12},{9,13},{10,... | collective-permute-start | bytes 98312 | tf_op jit(solution)/shard_map/ppermute | solution.py:39
  3.5 1.5 collective-permute-done.1
  5.0 1.6 collective-permute-done.2
  6.7 1.3 collective-permute-start.4
  8.0 1.2 collective-permute-start.5
  9.1 0.3 collective-permute-start.3
  9.4 1.5 fusion
  10.9 0.8 slice.19
  11.7 1.1 collective-permute-done.5
  12.9 0.6 collective-permute-done.3
  13.6 3.4 %collective-permute-start.6 = (bf16[2,8,64,256]{3,2,1,0:T(8,128)(2,1)S(1)}, bf16[2,8,64,256]{3,2,1,0:T(8,128)(2,1)S(1)}, u32[]{:S(2)}, u32[]{:S(2)}) collective-permute-start(bf16[2,8,64,256]{3,2,1,0:T(8,128)(2,1)S(1)} %pad_maximum_fusion.3.even), channel_id=1, source_target_pairs={{0,8},{1,9},{2,10},{3,11},{4,12},{5,13},{6,14},{7,15},{8,0},{9,1},... | collective-permute-start | bytes 1572872 | tf_op jit(solution)/shard_map/ppermute | solution.py:39
  17.0 1.3 fusion.2.normed.refs_2_
  18.3 0.2 collective-permute-done.6.odd
  18.5 2.7 %collective-permute-start.8 = (bf16[192,256]{1,0:T(8,128)(2,1)S(1)}, bf16[192,256]{1,0:T(8,128)(2,1)S(1)}, u32[]{:S(2)}, u32[]{:S(2)}) collective-permute-start(bf16[192,256]{1,0:T(8,128)(2,1)S(1)} %pad_maximum_fusion.8), channel_id=1, source_target_pairs={{0,2},{1,3},{2,0},{3,1},{4,6},{5,7},{6,4},{7,5},{8,10},{9,11},{10,... | collective-permute-start | bytes 294920 | tf_op jit(solution)/shard_map/ppermute | solution.py:39
  21.3 1.2 collective-permute-start.10
  22.5 1.6 collective-permute-done.8
  24.1 1.6 collective-permute-done.9
  25.7 5.6 %collective-permute-done.10 = bf16[192,256]{1,0:T(8,128)(2,1)S(1)} collective-permute-done((bf16[192,256]{1,0:T(8,128)(2,1)S(1)}, bf16[192,256]{1,0:T(8,128)(2,1)S(1)}, u32[]{:S(2)}, u32[]{:S(2)}) %collective-permute-start.10) | collective-permute-done | bytes 98336 | tf_op jit(solution)/shard_map/ppermute | solution.py:39
  31.5 1.2 collective-permute-start.11
  32.7 2.9 %project_queries.1.refs_1_ = bf16[8,64,512]{2,1,0:T(8,128)(2,1)} custom-call(s32[2]{0:T(128)S(1)} %pad_add_fusion.info.refs_0_, bf16[512,1024]{1,0:T(8,128)(2,1)} %fusion.2.normed.refs_2_, bf16[2,8,64,256]{3,2,1,0:T(8,128)(2,1)S(1)} %pad_maximum_fusion.3.even, bf16[2,8,64,256]{3,2,1,0:T(8,128)(2,1)S(1)} %collective-permute-done.6.odd), custom_call_target="tpu_custom_call" | custom-call | flops 1000000000 | bytes 2000000 | tf_op jit(solution)/shard_map/project_queries/pallas_call | solution.py:182
  35.5 3.4 %all-to-all-start = ((bf16[8,64,512]{2,1,0:T(8,128)(2,1)}), bf16[8,64,512]{2,1,0:T(8,128)(2,1)S(1)}, u32[]{:S(2)}, u32[]{:S(2)}) async-start(bf16[8,64,512]{2,1,0:T(8,128)(2,1)} %project_queries.1.refs_1_), calls=%async_computation | async-start | bytes 1048576 | tf_op jit(solution)/shard_map/all_to_all | solution.py:509
  39.0 1.3 collective-permute-start.12
  40.3 0.4 collective-permute-start.13
  40.7 0.3 collective-permute-done.11
  41.1 10.2 %collective-permute-done.12 = bf16[4,192,256]{2,1,0:T(8,128)(2,1)S(1)} collective-permute-done((bf16[4,192,256]{2,1,0:T(8,128)(2,1)S(1)}, bf16[4,192,256]{2,1,0:T(8,128)(2,1)S(1)}, u32[]{:S(2)}, u32[]{:S(2)}) %collective-permute-start.12) | collective-permute-done | bytes 393248 | tf_op jit(solution)/shard_map/ppermute | solution.py:39
  51.2 5.4 %collective-permute-done.13 = bf16[4,192,256]{2,1,0:T(8,128)(2,1)S(1)} collective-permute-done((bf16[4,192,256]{2,1,0:T(8,128)(2,1)S(1)}, bf16[4,192,256]{2,1,0:T(8,128)(2,1)S(1)}, u32[]{:S(2)}, u32[]{:S(2)}) %collective-permute-start.13) | collective-permute-done | bytes 393248 | tf_op jit(solution)/shard_map/ppermute | solution.py:39
  56.9 2.5 %collective-permute-start.14 = (bf16[2,8,192,256]{3,2,1,0:T(8,128)(2,1)S(1)}, bf16[2,8,192,256]{3,2,1,0:T(8,128)(2,1)}, u32[]{:S(2)}, u32[]{:S(2)}) collective-permute-start(bf16[2,8,192,256]{3,2,1,0:T(8,128)(2,1)S(1)} %pad_maximum_fusion.refs_4_), channel_id=1, source_target_pairs={{0,8},{1,9},{2,10},{3,11},{4,12},{5,13},{6,14},{7,15},{8,0},{9,1},... | collective-permute-start | bytes 4718600 | tf_op jit(solution)/shard_map/ppermute | solution.py:39
  59.4 1.4 fusion.8
  60.8 1.0 copy.29.slot_rows.refs_1_
  61.8 3.4 %collective-permute-start.7 = (bf16[512,1024]{1,0:T(8,128)(2,1)S(1)}, bf16[512,1024]{1,0:T(8,128)(2,1)}, u32[]{:S(2)}, u32[]{:S(2)}) collective-permute-start(bf16[512,1024]{1,0:T(8,128)(2,1)S(1)} %copy-done.7), channel_id=1, source_target_pairs={{0,1},{2,3},{4,5},{6,7},{8,9},{10,11},{12,13},{14,15},{16,17},{18,... | collective-permute-start | bytes 3145736 | tf_op jit(solution)/shard_map/ppermute | solution.py:520
  65.2 13.5 %cached_attention.1.refs_6_ = bf16[8,80,512]{2,1,0:T(8,128)(2,1)} custom-call(s32[4]{0:T(128)S(1)} %copy-done.3, s32[1,128]{1,0:T(1,128)S(1)} %copy-done.4, bf16[8,64,512]{2,1,0:T(8,128)(2,1)S(1)} %all-to-all-done.q_ref, bf16[128,128,128]{2,1,0:T(8,128)(2,1)} %kv_ref.1), custom_call_target="tpu_custom_call" | custom-call | flops 8000000000 | bytes 6000000 | tf_op jit(solution)/shard_map/cached_attention/pallas_call | solution.py:146
  78.7 4.5 %all-to-all-start.1 = ((bf16[8,80,512]{2,1,0:T(8,128)(2,1)}), bf16[8,80,512]{2,1,0:T(8,128)(2,1)}, u32[]{:S(2)}, u32[]{:S(2)}) async-start(bf16[8,80,512]{2,1,0:T(8,128)(2,1)} %cached_attention.1.refs_6_), calls=%async_computation.1 | async-start | bytes 1310720 | tf_op jit(solution)/shard_map/all_to_all | solution.py:527
  83.2 0.6 gather_fusion
  84.1 0.2 fusion.7.hits
  84.3 7.7 %collective-permute-done.7.refs_3_ = bf16[512,1024]{1,0:T(8,128)(2,1)} collective-permute-done((bf16[512,1024]{1,0:T(8,128)(2,1)S(1)}, bf16[512,1024]{1,0:T(8,128)(2,1)}, u32[]{:S(2)}, u32[]{:S(2)}) %collective-permute-start.7) | collective-permute-done | bytes 1048608 | tf_op jit(solution)/shard_map/ppermute | solution.py:520
  92.0 7.8 %self_attention.1 = (f32[8,88,512]{2,1,0:T(8,128)}, bf16[512,1024]{1,0:T(8,128)(2,1)}) custom-call(s32[2]{0:T(128)S(1)} %pad_add_fusion.info.refs_0_, bf16[8,64,512]{2,1,0:T(8,128)(2,1)} %project_queries.1.refs_1_, bf16[512,1024]{1,0:T(8,128)(2,1)} %fusion.2.normed.refs_2_, bf16[512,1024]{1,0:T(8,128)(2,1)} %collective-permute-done.7.refs_3_, ...), custom_call_target="tpu_custom_call" | custom-call | flops 4000000000 | bytes 5000000 | tf_op jit(solution)/shard_map/self_attention/pallas_call | solution.py:275
  99.8 5.5 %merge_and_dispatch.1 = (f32[512,1024]{1,0:T(8,128)}, f32[512,8]{1,0:T(8,128)S(1)}, bf16[512,1024]{1,0:T(8,128)(2,1)}, bf16[160,1024]{1,0:T(8,128)(2,1)S(1)}, bf...) custom-call(bf16[512,1024]{1,0:T(8,128)(2,1)} %tokens.1, ...), custom_call_target="tpu_custom_call" | custom-call | flops 4000000000 | bytes 10000000 | tf_op jit(solution)/shard_map/merge_and_dispatch/pallas_call | solution.py:359
  105.3 5.5 %collective-permute-start.17 = (bf16[160,1024]{1,0:T(8,128)(2,1)}, bf16[160,1024]{1,0:T(8,128)(2,1)S(1)}, u32[]{:S(2)}, u32[]{:S(2)}) collective-permute-start(bf16[160,1024]{1,0:T(8,128)(2,1)} %get-tuple-element.37), channel_id=1, source_target_pairs={{0,3},{1,2},{2,1},{3,0},{4,7},{5,6},{6,5},{7,4},{8,11},{9,10},{10,... | collective-permute-start | bytes 983048 | tf_op jit(solution)/shard_map/ppermute | solution.py:39
  110.7 0.9 collective-permute-start.15
  111.6 1.2 collective-permute-start.16
  112.8 2.1 collective-permute-start.21
  114.9 1.5 collective-permute-start.22
  116.3 14.2 %collective-permute-done.17.refs_3_.refs_2_ = bf16[160,1024]{1,0:T(8,128)(2,1)S(1)} collective-permute-done((bf16[160,1024]{1,0:T(8,128)(2,1)}, bf16[160,1024]{1,0:T(8,128)(2,1)S(1)}, u32[]{:S(2)}, u32[]{:S(2)}) %collective-permute-start.17) | collective-permute-done | bytes 327712 | tf_op jit(solution)/shard_map/ppermute | solution.py:39
  130.5 1.9 dispatch.1
  132.4 1.4 collective-permute-start.25
  133.8 3.9 %collective-permute-done.16.refs_2_ = bf16[160,1024]{1,0:T(8,128)(2,1)S(1)} collective-permute-done((bf16[160,1024]{1,0:T(8,128)(2,1)}, bf16[160,1024]{1,0:T(8,128)(2,1)S(1)}, u32[]{:S(2)}, u32[]{:S(2)}) %collective-permute-start.16) | collective-permute-done | bytes 327712 | tf_op jit(solution)/shard_map/ppermute | solution.py:39
  137.7 0.7 copy-done.13
  138.4 18.5 %expert.3 = (bf16[160,1024]{1,0:T(8,128)(2,1)S(1)}, bf16[160,1024]{1,0:T(8,128)(2,1)S(1)}, bf16[160,1024]{1,0:T(8,128)(2,1)S(1)}, bf16[160,1024]{1,0:T(8,128)(2,1)S(1)}) custom-call(bf16[160,1024]{1,0:T(8,128)(2,1)S(1)} %get-tuple-element.34.refs_0_, bf16[160,1024]{1,0:T(8,128)(2,1)} %copy-done.12, bf16[160,1024]{1,0:T(8,128)(2,1)} %copy-done.13, ...), custom_call_target="tpu_custom_call" | custom-call | flops 11072962560 | bytes 17301504 | tf_op jit(solution)/shard_map/expert/pallas_call | solution.py:421
  156.9 14.0 %expert.4 = (bf16[160,1024]{1,0:T(8,128)(2,1)S(1)}, bf16[160,1024]{1,0:T(8,128)(2,1)S(1)}) custom-call(bf16[160,1024]{1,0:T(8,128)(2,1)S(1)} %collective-permute-done.21.refs_0_, bf16[160,1024]{1,0:T(8,128)(2,1)S(1)} %collective-permute-done.22.refs_1_, bf16[1,1024,5632]{2,1,0:T(8,128)(2,1)} %refs_3_.3, bf16[1,1024,5632]{2,1,0:T(8,128)(2,1)} %refs_3_.3, ...), custom_call_target="tpu_custom_call" | custom-call | flops 5536481280 | bytes 17301504 | tf_op jit(solution)/shard_map/expert/pallas_call | solution.py:421
  171.0 3.1 %collective-permute-start.23 = (bf16[160,1024]{1,0:T(8,128)(2,1)S(1)}, bf16[160,1024]{1,0:T(8,128)(2,1)S(1)}, u32[]{:S(2)}, u32[]{:S(2)}) collective-permute-start(bf16[160,1024]{1,0:T(8,128)(2,1)S(1)} %get-tuple-element.44.refs_5_), channel_id=1, source_target_pairs={{0,4},{1,5},{2,6},{3,7},{4,0},{5,1},{6,2},{7,3},{8,12},{9,13},{10,... | collective-permute-start | bytes 983048 | tf_op jit(solution)/shard_map/ppermute | solution.py:39
  174.1 1.3 collective-permute-start.18
  175.3 1.4 collective-permute-start.19
  176.7 14.0 %expert.5 = (bf16[160,1024]{1,0:T(8,128)(2,1)S(1)}, bf16[160,1024]{1,0:T(8,128)(2,1)S(1)}) custom-call(bf16[160,1024]{1,0:T(8,128)(2,1)S(1)} %collective-permute-done.25.refs_0_, bf16[160,1024]{1,0:T(8,128)(2,1)S(1)} %collective-permute-done.26.refs_1_, bf16[1,1024,5632]{2,1,0:T(8,128)(2,1)} %refs_3_.3, bf16[1,1024,5632]{2,1,0:T(8,128)(2,1)} %refs_3_.3, ...), custom_call_target="tpu_custom_call" | custom-call | flops 5536481280 | bytes 17301504 | tf_op jit(solution)/shard_map/expert/pallas_call | solution.py:421
  190.8 1.3 collective-permute-start.27
  192.1 0.3 collective-permute-done.19.refs_5_
  192.4 0.9 collective-permute-start.28
  193.5 5.6 %collective-permute-done.20.refs_6_ = bf16[160,1024]{1,0:T(8,128)(2,1)S(1)} collective-permute-done((bf16[160,1024]{1,0:T(8,128)(2,1)S(1)}, bf16[160,1024]{1,0:T(8,128)(2,1)S(1)}, u32[]{:S(2)}, u32[]{:S(2)}) %collective-permute-start.20) | collective-permute-done | bytes 327712 | tf_op jit(solution)/shard_map/ppermute | solution.py:39
  199.1 4.4 %combine.3.refs_0_ = f32[512,1024]{1,0:T(8,128)} custom-call(f32[512,1024]{1,0:T(8,128)} %get-tuple-element.32.refs_0_, f32[512,8]{1,0:T(8,128)S(1)} %get-tuple-element.33.refs_7_.refs_1_, s32[512,8]{1,0:T(8,128)S(1)} %bitcast_select_fusion.refs_2_, bf16[160,1024]{1,0:T(8,128)(2,1)S(1)} %get-tuple-element.38.refs_3_.refs_5_, ...), custom_call_target="tpu_custom_call" | custom-call | flops 671088640 | bytes 6000000 | tf_op jit(solution)/shard_map/combine/pallas_call | solution.py:465
  203.5 1.0 collective-permute-done.24.refs_4_
  204.5 3.7 %combine.4.refs_0_ = f32[512,1024]{1,0:T(8,128)} custom-call(f32[512,1024]{1,0:T(8,128)} %combine.3.refs_0_, f32[512,8]{1,0:T(8,128)S(1)} %get-tuple-element.33.refs_7_.refs_1_, s32[512,8]{1,0:T(8,128)S(1)} %bitcast_select_fusion.refs_2_, bf16[160,1024]{1,0:T(8,128)(2,1)S(1)} %collective-permute-done.23.refs_3_, ...), custom_call_target="tpu_custom_call" | custom-call | flops 335544320 | bytes 6000000 | tf_op jit(solution)/shard_map/combine/pallas_call | solution.py:465
  208.2 16.2 %collective-permute-done.27.refs_3_ = bf16[160,1024]{1,0:T(8,128)(2,1)S(1)} collective-permute-done((bf16[160,1024]{1,0:T(8,128)(2,1)S(1)}, bf16[160,1024]{1,0:T(8,128)(2,1)S(1)}, u32[]{:S(2)}, u32[]{:S(2)}) %collective-permute-start.27) | collective-permute-done | bytes 327712 | tf_op jit(solution)/shard_map/ppermute | solution.py:39
  224.4 5.4 %collective-permute-done.28.refs_4_ = bf16[160,1024]{1,0:T(8,128)(2,1)S(1)} collective-permute-done((bf16[160,1024]{1,0:T(8,128)(2,1)S(1)}, bf16[160,1024]{1,0:T(8,128)(2,1)S(1)}, u32[]{:S(2)}, u32[]{:S(2)}) %collective-permute-start.28) | collective-permute-done | bytes 327712 | tf_op jit(solution)/shard_map/ppermute | solution.py:39
  229.8 3.4 %combine.5 = bf16[512,1024]{1,0:T(8,128)(2,1)} custom-call(f32[512,1024]{1,0:T(8,128)} %combine.4.refs_0_, f32[512,8]{1,0:T(8,128)S(1)} %get-tuple-element.33.refs_7_.refs_1_, s32[512,8]{1,0:T(8,128)S(1)} %bitcast_select_fusion.refs_2_, bf16[160,1024]{1,0:T(8,128)(2,1)S(1)} %collective-permute-done.27.refs_3_, ...), custom_call_target="tpu_custom_call" | custom-call | flops 335544320 | bytes 6000000 | tf_op jit(solution)/shard_map/combine/pallas_call | solution.py:465
  (68 shorter events, 1.6 us)
Async XLA Ops:
  0.0 83.2 %copy-start = (bf16[1024,8]{0,1:T(8,128)(2,1)S(1)}, bf16[1024,8]{0,1:T(8,128)(2,1)}, u32[]{:S(2)}) copy-start(bf16[1024,8]{0,1:T(8,128)(2,1)} %param.20) | copy-start | bytes 49156
  0.8 2.8 %collective-permute-start = (bf16[64,256]{1,0:T(8,128)(2,1)S(1)}, bf16[64,256]{1,0:T(8,128)(2,1)S(1)}, u32[]{:S(2)}, u32[]{:S(2)}) collective-permute-start(bf16[64,256]{1,0:T(8,128)(2,1)S(1)} %get-tuple-element.56), channel_id=1, source_target_pairs={{0,2},{1,3},{2,0},{3,1},{4,6},{5,7},{6,4},{7,5},{8,10},{9,11},{10,... | collective-permute-start | bytes 98312 | tf_op jit(solution)/shard_map/ppermute | solution.py:39
  0.8 4.2 %collective-permute-start.1 = (bf16[64,256]{1,0:T(8,128)(2,1)S(1)}, bf16[64,256]{1,0:T(8,128)(2,1)S(1)}, u32[]{:S(2)}, u32[]{:S(2)}) collective-permute-start(bf16[64,256]{1,0:T(8,128)(2,1)S(1)} %get-tuple-element.56), channel_id=1, source_target_pairs={{0,4},{1,5},{2,6},{3,7},{4,0},{5,1},{6,2},{7,3},{8,12},{9,13},{10,... | collective-permute-start | bytes 98312 | tf_op jit(solution)/shard_map/ppermute | solution.py:39
  3.3 3.4 %collective-permute-start.2 = (bf16[64,256]{1,0:T(8,128)(2,1)S(1)}, bf16[64,256]{1,0:T(8,128)(2,1)S(1)}, u32[]{:S(2)}, u32[]{:S(2)}) collective-permute-start(bf16[64,256]{1,0:T(8,128)(2,1)S(1)} %get-tuple-element.56), channel_id=1, source_target_pairs={{0,6},{1,7},{2,4},{3,5},{4,2},{5,3},{6,0},{7,1},{8,14},{9,15},{10,... | collective-permute-start | bytes 98312 | tf_op jit(solution)/shard_map/ppermute | solution.py:39
  6.6 10.4 %copy-start.9 = (bf16[256,64]{0,1:T(8,128)(2,1)S(1)}, bf16[256,64]{0,1:T(8,128)(2,1)}, u32[]{:S(2)}) copy-start(bf16[256,64]{0,1:T(8,128)(2,1)} %param.15) | copy-start | bytes 98308
  6.7 10.4 %copy-start.5 = (bf16[512,1024]{1,0:T(8,128)(2,1)S(1)}, bf16[512,1024]{1,0:T(8,128)(2,1)}, u32[]{:S(2)}) copy-start(bf16[512,1024]{1,0:T(8,128)(2,1)} %tokens.1) | copy-start | bytes 3145732
  6.7 10.4 %copy-start.10 = (f32[1024]{0:T(1024)S(1)}, f32[1024]{0:T(1024)}, u32[]{:S(2)}) copy-start(f32[1024]{0:T(1024)} %param.13) | copy-start | bytes 12292
  6.7 5.1 %collective-permute-start.4 = (bf16[4,64,256]{2,1,0:T(8,128)(2,1)S(1)}, bf16[4,64,256]{2,1,0:T(8,128)(2,1)S(1)}, u32[]{:S(2)}, u32[]{:S(2)}) collective-permute-start(bf16[4,64,256]{2,1,0:T(8,128)(2,1)S(1)} %get-tuple-element.54), channel_id=1, source_target_pairs={{0,16},{1,17},{2,18},{3,19},{4,20},{5,21},{6,22},{7,23},{8,24},{9,... | collective-permute-start | bytes 393224 | tf_op jit(solution)/shard_map/ppermute | solution.py:39
  8.0 4.8 %collective-permute-start.5 = (bf16[4,64,256]{2,1,0:T(8,128)(2,1)S(1)}, bf16[4,64,256]{2,1,0:T(8,128)(2,1)S(1)}, u32[]{:S(2)}, u32[]{:S(2)}) collective-permute-start(bf16[4,64,256]{2,1,0:T(8,128)(2,1)S(1)} %get-tuple-element.54), channel_id=1, source_target_pairs={{0,17},{1,16},{2,19},{3,18},{4,21},{5,20},{6,23},{7,22},{8,25},{9,... | collective-permute-start | bytes 393224 | tf_op jit(solution)/shard_map/ppermute | solution.py:39
  9.1 4.4 %collective-permute-start.3 = (bf16[4,64,256]{2,1,0:T(8,128)(2,1)S(1)}, bf16[4,64,256]{2,1,0:T(8,128)(2,1)S(1)}, u32[]{:S(2)}, u32[]{:S(2)}) collective-permute-start(bf16[4,64,256]{2,1,0:T(8,128)(2,1)S(1)} %get-tuple-element.54), channel_id=1, source_target_pairs={{0,1},{1,0},{2,3},{3,2},{4,5},{5,4},{6,7},{7,6},{8,9},{9,8},{10,11... | collective-permute-start | bytes 393224 | tf_op jit(solution)/shard_map/ppermute | solution.py:39
  13.6 4.9 %collective-permute-start.6 = (bf16[2,8,64,256]{3,2,1,0:T(8,128)(2,1)S(1)}, bf16[2,8,64,256]{3,2,1,0:T(8,128)(2,1)S(1)}, u32[]{:S(2)}, u32[]{:S(2)}) collective-permute-start(bf16[2,8,64,256]{3,2,1,0:T(8,128)(2,1)S(1)} %pad_maximum_fusion.3.even), channel_id=1, source_target_pairs={{0,8},{1,9},{2,10},{3,11},{4,12},{5,13},{6,14},{7,15},{8,0},{9,1},... | collective-permute-start | bytes 1572872 | tf_op jit(solution)/shard_map/ppermute | solution.py:39
  18.5 5.6 %collective-permute-start.8 = (bf16[192,256]{1,0:T(8,128)(2,1)S(1)}, bf16[192,256]{1,0:T(8,128)(2,1)S(1)}, u32[]{:S(2)}, u32[]{:S(2)}) collective-permute-start(bf16[192,256]{1,0:T(8,128)(2,1)S(1)} %pad_maximum_fusion.8), channel_id=1, source_target_pairs={{0,2},{1,3},{2,0},{3,1},{4,6},{5,7},{6,4},{7,5},{8,10},{9,11},{10,... | collective-permute-start | bytes 294920 | tf_op jit(solution)/shard_map/ppermute | solution.py:39
  21.3 4.5 %collective-permute-start.9 = (bf16[192,256]{1,0:T(8,128)(2,1)S(1)}, bf16[192,256]{1,0:T(8,128)(2,1)S(1)}, u32[]{:S(2)}, u32[]{:S(2)}) collective-permute-start(bf16[192,256]{1,0:T(8,128)(2,1)S(1)} %pad_maximum_fusion.8), channel_id=1, source_target_pairs={{0,4},{1,5},{2,6},{3,7},{4,0},{5,1},{6,2},{7,3},{8,12},{9,13},{10,... | collective-permute-start | bytes 294920 | tf_op jit(solution)/shard_map/ppermute | solution.py:39
  21.3 10.1 %collective-permute-start.10 = (bf16[192,256]{1,0:T(8,128)(2,1)S(1)}, bf16[192,256]{1,0:T(8,128)(2,1)S(1)}, u32[]{:S(2)}, u32[]{:S(2)}) collective-permute-start(bf16[192,256]{1,0:T(8,128)(2,1)S(1)} %pad_maximum_fusion.8), channel_id=1, source_target_pairs={{0,6},{1,7},{2,4},{3,5},{4,2},{5,3},{6,0},{7,1},{8,14},{9,15},{10,... | collective-permute-start | bytes 294920 | tf_op jit(solution)/shard_map/ppermute | solution.py:39
  31.4 9.2 %copy-start.11 = (s32[512,2]{0,1:T(2,128)S(1)}, s32[512,2]{0,1:T(2,128)}, u32[]{:S(2)}) copy-start(s32[512,2]{0,1:T(2,128)} %param.21) | copy-start | bytes 12292
  31.5 9.5 %collective-permute-start.11 = (bf16[4,192,256]{2,1,0:T(8,128)(2,1)S(1)}, bf16[4,192,256]{2,1,0:T(8,128)(2,1)S(1)}, u32[]{:S(2)}, u32[]{:S(2)}) collective-permute-start(bf16[4,192,256]{2,1,0:T(8,128)(2,1)S(1)} %get-tuple-element.52), channel_id=1, source_target_pairs={{0,1},{1,0},{2,3},{3,2},{4,5},{5,4},{6,7},{7,6},{8,9},{9,8},{10,11... | collective-permute-start | bytes 1179656 | tf_op jit(solution)/shard_map/ppermute | solution.py:39
  35.5 29.6 %all-to-all-start = ((bf16[8,64,512]{2,1,0:T(8,128)(2,1)}), bf16[8,64,512]{2,1,0:T(8,128)(2,1)S(1)}, u32[]{:S(2)}, u32[]{:S(2)}) async-start(bf16[8,64,512]{2,1,0:T(8,128)(2,1)} %project_queries.1.refs_1_), calls=%async_computation | async-start | bytes 1048576 | tf_op jit(solution)/shard_map/all_to_all | solution.py:509
  39.0 12.3 %collective-permute-start.12 = (bf16[4,192,256]{2,1,0:T(8,128)(2,1)S(1)}, bf16[4,192,256]{2,1,0:T(8,128)(2,1)S(1)}, u32[]{:S(2)}, u32[]{:S(2)}) collective-permute-start(bf16[4,192,256]{2,1,0:T(8,128)(2,1)S(1)} %get-tuple-element.52), channel_id=1, source_target_pairs={{0,16},{1,17},{2,18},{3,19},{4,20},{5,21},{6,22},{7,23},{8,24},{9,... | collective-permute-start | bytes 1179656 | tf_op jit(solution)/shard_map/ppermute | solution.py:39
  40.3 16.3 %collective-permute-start.13 = (bf16[4,192,256]{2,1,0:T(8,128)(2,1)S(1)}, bf16[4,192,256]{2,1,0:T(8,128)(2,1)S(1)}, u32[]{:S(2)}, u32[]{:S(2)}) collective-permute-start(bf16[4,192,256]{2,1,0:T(8,128)(2,1)S(1)} %get-tuple-element.52), channel_id=1, source_target_pairs={{0,17},{1,16},{2,19},{3,18},{4,21},{5,20},{6,23},{7,22},{8,25},{9,... | collective-permute-start | bytes 1179656 | tf_op jit(solution)/shard_map/ppermute | solution.py:39
  56.7 5.1 %copy-start.7 = (bf16[512,1024]{1,0:T(8,128)(2,1)S(1)}, bf16[512,1024]{1,0:T(8,128)(2,1)}, u32[]{:S(2)}) copy-start(bf16[512,1024]{1,0:T(8,128)(2,1)} %fusion.2.normed.refs_2_) | copy-start | bytes 3145732
  56.7 8.4 %copy-start.3 = (s32[4]{0:T(128)S(1)}, s32[4]{0:T(128)}, u32[]{:S(2)}) copy-start(s32[4]{0:T(128)} %lengths.1) | copy-start | bytes 52
  56.8 8.4 %copy-start.4 = (s32[1,128]{1,0:T(1,128)S(1)}, s32[1,128]{1,0:T(1,128)}, u32[]{:S(2)}) copy-start(s32[1,128]{1,0:T(1,128)} %table.1) | copy-start | bytes 1540
  56.9 21.8 %copy-start.6 = (bf16[2,8,192,256]{3,2,1,0:T(8,128)(2,1)}, bf16[2,8,192,256]{3,2,1,0:T(8,128)(2,1)S(1)}, u32[]{:S(2)}) copy-start(bf16[2,8,192,256]{3,2,1,0:T(8,128)(2,1)S(1)} %pad_maximum_fusion.refs_4_) | copy-start | bytes 4718596
  56.9 35.0 %collective-permute-start.14 = (bf16[2,8,192,256]{3,2,1,0:T(8,128)(2,1)S(1)}, bf16[2,8,192,256]{3,2,1,0:T(8,128)(2,1)}, u32[]{:S(2)}, u32[]{:S(2)}) collective-permute-start(bf16[2,8,192,256]{3,2,1,0:T(8,128)(2,1)S(1)} %pad_maximum_fusion.refs_4_), channel_id=1, source_target_pairs={{0,8},{1,9},{2,10},{3,11},{4,12},{5,13},{6,14},{7,15},{8,0},{9,1},... | collective-permute-start | bytes 4718600 | tf_op jit(solution)/shard_map/ppermute | solution.py:39
  61.8 30.2 %collective-permute-start.7 = (bf16[512,1024]{1,0:T(8,128)(2,1)S(1)}, bf16[512,1024]{1,0:T(8,128)(2,1)}, u32[]{:S(2)}, u32[]{:S(2)}) collective-permute-start(bf16[512,1024]{1,0:T(8,128)(2,1)S(1)} %copy-done.7), channel_id=1, source_target_pairs={{0,1},{2,3},{4,5},{6,7},{8,9},{10,11},{12,13},{14,15},{16,17},{18,... | collective-permute-start | bytes 3145736 | tf_op jit(solution)/shard_map/ppermute | solution.py:520
  78.7 21.1 %all-to-all-start.1 = ((bf16[8,80,512]{2,1,0:T(8,128)(2,1)}), bf16[8,80,512]{2,1,0:T(8,128)(2,1)}, u32[]{:S(2)}, u32[]{:S(2)}) async-start(bf16[8,80,512]{2,1,0:T(8,128)(2,1)} %cached_attention.1.refs_6_), calls=%async_computation.1 | async-start | bytes 1310720 | tf_op jit(solution)/shard_map/all_to_all | solution.py:527
  84.3 15.5 %copy-start.2 = (f32[1024]{0:T(1024)S(1)}, f32[1024]{0:T(1024)}, u32[]{:S(2)}) copy-start(f32[1024]{0:T(1024)} %param.19) | copy-start | bytes 12292
  105.3 25.3 %collective-permute-start.17 = (bf16[160,1024]{1,0:T(8,128)(2,1)}, bf16[160,1024]{1,0:T(8,128)(2,1)S(1)}, u32[]{:S(2)}, u32[]{:S(2)}) collective-permute-start(bf16[160,1024]{1,0:T(8,128)(2,1)} %get-tuple-element.37), channel_id=1, source_target_pairs={{0,3},{1,2},{2,1},{3,0},{4,7},{5,6},{6,5},{7,4},{8,11},{9,10},{10,... | collective-permute-start | bytes 983048 | tf_op jit(solution)/shard_map/ppermute | solution.py:39
  110.7 23.1 %collective-permute-start.15 = (bf16[160,1024]{1,0:T(8,128)(2,1)}, bf16[160,1024]{1,0:T(8,128)(2,1)S(1)}, u32[]{:S(2)}, u32[]{:S(2)}) collective-permute-start(bf16[160,1024]{1,0:T(8,128)(2,1)} %get-tuple-element.35), channel_id=1, source_target_pairs={{0,1},{1,0},{2,3},{3,2},{4,5},{5,4},{6,7},{7,6},{8,9},{9,8},{10,11... | collective-permute-start | bytes 983048 | tf_op jit(solution)/shard_map/ppermute | solution.py:39
  111.6 26.1 %collective-permute-start.16 = (bf16[160,1024]{1,0:T(8,128)(2,1)}, bf16[160,1024]{1,0:T(8,128)(2,1)S(1)}, u32[]{:S(2)}, u32[]{:S(2)}) collective-permute-start(bf16[160,1024]{1,0:T(8,128)(2,1)} %get-tuple-element.36), channel_id=1, source_target_pairs={{0,2},{1,3},{2,0},{3,1},{4,6},{5,7},{6,4},{7,5},{8,10},{9,11},{10,... | collective-permute-start | bytes 983048 | tf_op jit(solution)/shard_map/ppermute | solution.py:39
  112.8 44.1 %collective-permute-start.21 = (bf16[160,1024]{1,0:T(8,128)(2,1)S(1)}, bf16[160,1024]{1,0:T(8,128)(2,1)S(1)}, u32[]{:S(2)}, u32[]{:S(2)}) collective-permute-start(bf16[160,1024]{1,0:T(8,128)(2,1)S(1)} %get-tuple-element.42), channel_id=1, source_target_pairs={{0,4},{1,5},{2,6},{3,7},{4,0},{5,1},{6,2},{7,3},{8,12},{9,13},{10,... | collective-permute-start | bytes 983048 | tf_op jit(solution)/shard_map/ppermute | solution.py:39
  114.9 42.1 %collective-permute-start.22 = (bf16[160,1024]{1,0:T(8,128)(2,1)S(1)}, bf16[160,1024]{1,0:T(8,128)(2,1)S(1)}, u32[]{:S(2)}, u32[]{:S(2)}) collective-permute-start(bf16[160,1024]{1,0:T(8,128)(2,1)S(1)} %get-tuple-element.43), channel_id=1, source_target_pairs={{0,5},{1,4},{2,7},{3,6},{4,1},{5,0},{6,3},{7,2},{8,13},{9,12},{10,... | collective-permute-start | bytes 983048 | tf_op jit(solution)/shard_map/ppermute | solution.py:39
  130.5 7.2 %copy-start.1 = (bf16[160,1024]{1,0:T(8,128)(2,1)}, bf16[160,1024]{1,0:T(8,128)(2,1)S(1)}, u32[]{:S(2)}) copy-start(bf16[160,1024]{1,0:T(8,128)(2,1)S(1)} %collective-permute-done.17.refs_3_.refs_2_) | copy-start | bytes 983044
  132.4 42.9 %collective-permute-start.25 = (bf16[160,1024]{1,0:T(8,128)(2,1)S(1)}, bf16[160,1024]{1,0:T(8,128)(2,1)S(1)}, u32[]{:S(2)}, u32[]{:S(2)}) collective-permute-start(bf16[160,1024]{1,0:T(8,128)(2,1)S(1)} %get-tuple-element.47), channel_id=1, source_target_pairs={{0,6},{1,7},{2,4},{3,5},{4,2},{5,3},{6,0},{7,1},{8,14},{9,15},{10,... | collective-permute-start | bytes 983048 | tf_op jit(solution)/shard_map/ppermute | solution.py:39
  133.8 3.9 %copy-start.12 = (bf16[160,1024]{1,0:T(8,128)(2,1)}, bf16[160,1024]{1,0:T(8,128)(2,1)S(1)}, u32[]{:S(2)}) copy-start(bf16[160,1024]{1,0:T(8,128)(2,1)S(1)} %collective-permute-done.15.refs_1_) | copy-start | bytes 983044
  133.8 42.9 %collective-permute-start.26 = (bf16[160,1024]{1,0:T(8,128)(2,1)S(1)}, bf16[160,1024]{1,0:T(8,128)(2,1)S(1)}, u32[]{:S(2)}, u32[]{:S(2)}) collective-permute-start(bf16[160,1024]{1,0:T(8,128)(2,1)S(1)} %get-tuple-element.48), channel_id=1, source_target_pairs={{0,7},{1,6},{2,5},{3,4},{4,3},{5,2},{6,1},{7,0},{8,15},{9,14},{10,... | collective-permute-start | bytes 983048 | tf_op jit(solution)/shard_map/ppermute | solution.py:39
  137.7 0.7 copy-start.13
  171.0 32.6 %collective-permute-start.23 = (bf16[160,1024]{1,0:T(8,128)(2,1)S(1)}, bf16[160,1024]{1,0:T(8,128)(2,1)S(1)}, u32[]{:S(2)}, u32[]{:S(2)}) collective-permute-start(bf16[160,1024]{1,0:T(8,128)(2,1)S(1)} %get-tuple-element.44.refs_5_), channel_id=1, source_target_pairs={{0,4},{1,5},{2,6},{3,7},{4,0},{5,1},{6,2},{7,3},{8,12},{9,13},{10,... | collective-permute-start | bytes 983048 | tf_op jit(solution)/shard_map/ppermute | solution.py:39
  174.1 30.4 %collective-permute-start.24 = (bf16[160,1024]{1,0:T(8,128)(2,1)S(1)}, bf16[160,1024]{1,0:T(8,128)(2,1)S(1)}, u32[]{:S(2)}, u32[]{:S(2)}) collective-permute-start(bf16[160,1024]{1,0:T(8,128)(2,1)S(1)} %get-tuple-element.45), channel_id=1, source_target_pairs={{0,5},{1,4},{2,7},{3,6},{4,1},{5,0},{6,3},{7,2},{8,13},{9,12},{10,... | collective-permute-start | bytes 983048 | tf_op jit(solution)/shard_map/ppermute | solution.py:39
  174.1 16.7 %collective-permute-start.18 = (bf16[160,1024]{1,0:T(8,128)(2,1)S(1)}, bf16[160,1024]{1,0:T(8,128)(2,1)S(1)}, u32[]{:S(2)}, u32[]{:S(2)}) collective-permute-start(bf16[160,1024]{1,0:T(8,128)(2,1)S(1)} %get-tuple-element.39), channel_id=1, source_target_pairs={{0,1},{1,0},{2,3},{3,2},{4,5},{5,4},{6,7},{7,6},{8,9},{9,8},{10,11... | collective-permute-start | bytes 983048 | tf_op jit(solution)/shard_map/ppermute | solution.py:39
  175.3 17.0 %collective-permute-start.19 = (bf16[160,1024]{1,0:T(8,128)(2,1)S(1)}, bf16[160,1024]{1,0:T(8,128)(2,1)S(1)}, u32[]{:S(2)}, u32[]{:S(2)}) collective-permute-start(bf16[160,1024]{1,0:T(8,128)(2,1)S(1)} %get-tuple-element.40), channel_id=1, source_target_pairs={{0,2},{1,3},{2,0},{3,1},{4,6},{5,7},{6,4},{7,5},{8,10},{9,11},{10,... | collective-permute-start | bytes 983048 | tf_op jit(solution)/shard_map/ppermute | solution.py:39
  176.7 16.6 %copy-start.8 = (s32[8,512]{0,1:T(8,128)S(1)}, s32[8,512]{0,1:T(8,128)}, u32[]{:S(2)}) copy-start(s32[8,512]{0,1:T(8,128)} %get-tuple-element.60) | copy-start | bytes 49156
  176.7 22.4 %collective-permute-start.20 = (bf16[160,1024]{1,0:T(8,128)(2,1)S(1)}, bf16[160,1024]{1,0:T(8,128)(2,1)S(1)}, u32[]{:S(2)}, u32[]{:S(2)}) collective-permute-start(bf16[160,1024]{1,0:T(8,128)(2,1)S(1)} %get-tuple-element.41), channel_id=1, source_target_pairs={{0,3},{1,2},{2,1},{3,0},{4,7},{5,6},{6,5},{7,4},{8,11},{9,10},{10,... | collective-permute-start | bytes 983048 | tf_op jit(solution)/shard_map/ppermute | solution.py:39
  190.8 33.6 %collective-permute-start.27 = (bf16[160,1024]{1,0:T(8,128)(2,1)S(1)}, bf16[160,1024]{1,0:T(8,128)(2,1)S(1)}, u32[]{:S(2)}, u32[]{:S(2)}) collective-permute-start(bf16[160,1024]{1,0:T(8,128)(2,1)S(1)} %get-tuple-element.49), channel_id=1, source_target_pairs={{0,6},{1,7},{2,4},{3,5},{4,2},{5,3},{6,0},{7,1},{8,14},{9,15},{10,... | collective-permute-start | bytes 983048 | tf_op jit(solution)/shard_map/ppermute | solution.py:39
  192.4 37.4 %collective-permute-start.28 = (bf16[160,1024]{1,0:T(8,128)(2,1)S(1)}, bf16[160,1024]{1,0:T(8,128)(2,1)S(1)}, u32[]{:S(2)}, u32[]{:S(2)}) collective-permute-start(bf16[160,1024]{1,0:T(8,128)(2,1)S(1)} %get-tuple-element.50), channel_id=1, source_target_pairs={{0,7},{1,6},{2,5},{3,4},{4,3},{5,2},{6,1},{7,0},{8,15},{9,14},{10,... | collective-permute-start | bytes 983048 | tf_op jit(solution)/shard_map/ppermute | solution.py:39

commit v3 on v2

--- a/solution.py
+++ b/solution.py
@@ -500,7 +500,8 @@
     info = jnp.stack([me, group]).astype(jnp.int32)
 
     w_t = w_qkv.T
-    q_plane = gather_plane(gather_high(w_t[0:HD], lanes, groups), lanes, groups)
+    q_high = gather_high(w_t[0:HD], lanes, groups)
+    q_plane = gather_plane(q_high, lanes, groups)
     q_other = send(q_plane, lanes, lanes, groups)
     values = tokens.astype(F32)
     mean_square = jnp.mean(values * values, axis=-1, keepdims=True)
@@ -509,7 +510,8 @@
     q_here = lax.all_to_all(q, "tensor", split_axis=0, concat_axis=0, tiled=True)
 
     near = [normed]
-    ready = after(normed, q_plane)
+    rest = jnp.concatenate([w_t[HD : 3 * HD], w_attn_out.T], axis=0)
+    ready, rest = lax.optimization_barrier((normed, rest, q))[:2]
     for i in range(1, span_devs):
         pairs = [
             (b * lanes + t, b * lanes + (t ^ i))
@@ -518,12 +520,11 @@
             if t % span_devs < (t ^ i) % span_devs
         ]
         near.append(lax.ppermute(ready, AXES, pairs))
-    rest = jnp.concatenate([w_t[HD : 3 * HD], w_attn_out.T], axis=0)
-    rest = gather_high(after(rest, q_other), lanes, groups)
-    rest = gather_plane(rest, lanes, groups)
-    rest_other = send(rest, lanes, lanes, groups)
+    rest = gather_high(rest, lanes, groups)
+    rest = gather_plane(after(rest, *near[1:]), lanes, groups)
 
     parts = cached_attention(cached_lengths, page_table, q_here, kv_cache)
+    rest_other = send(after(rest, parts), lanes, lanes, groups)
     cached = lax.all_to_all(parts, "tensor", split_axis=0, concat_axis=0, tiled=True)
     own, w_o = self_attention(info, q, near, rest, rest_other, parts)
 

time: 236 us -> 229 us (0.970)
  Pallas kernels: 89.6 us -> 84.6 us
    ppermute x1, waiting for transfers between devices: 7.67 us -> 0.01 us  [body(): near.append(lax.ppermute(ready, AXES, pairs))]
    all_to_all x1, waiting for transfers between devices: 0.01 us -> 6.13 us  [body(): lax.all_to_all(parts, 'tensor', split_axis=0, concat_axis=0, tiled=True)]
    ppermute x28, starting transfers between devices: 38.4 us -> 33.3 us  [send(): return lax.ppermute(value, AXES, [(i, i ^ mask) for i in range(total)])]
    pallas_call x1, Pallas kernels: 13.5 us -> 8.5 us  [cached_attention(): pl.pallas_call(functools.partial(cached_kernel, requests, span_devs, 4),...]
    ppermute x28, waiting for transfers between devices: 76.2 us -> 79.7 us  [send(): return lax.ppermute(value, AXES, [(i, i ^ mask) for i in range(total)])]
    all_to_all x1, starting transfers between devices: 3.44 us -> 6.14 us  [body(): lax.all_to_all(q, 'tensor', split_axis=0, concat_axis=0, tiled=True)]
  transfers between devices with their start and end apart: 31 -> 31, of which waited for: 20 -> 17; matrix products, arithmetic and copies ran while one was open for 3% -> 3% of each run, Pallas kernels for 35% -> 32%
where the time goes in v3:
time: 229 us; the launch traced here: 228 us
  waiting for transfers between devices  85.9 us (38%)
  Pallas kernels  84.6 us (37%)
  starting transfers between devices  47.7 us (21%)
  other arithmetic  4.61 us (2%)
  local copies, waits for them, and re-layouts  4.21 us (2%)
    ppermute x28, waiting for transfers between devices, send(): return lax.ppermute(value, AXES, [(i, i ^ mask) for i in range(total)])  79.7 us
    pallas_call x3, Pallas kernels, expert(): pl.pallas_call(functools.partial(expert_kernel, count), grid=(steps,), ou...  46.5 us
    ppermute x28, starting transfers between devices, send(): return lax.ppermute(value, AXES, [(i, i ^ mask) for i in range(total)])  33.3 us
    pallas_call x3, Pallas kernels, combine(): pl.pallas_call(functools.partial(combine_kernel, first, count, last), out...  11.5 us
    pallas_call x1, Pallas kernels, cached_attention(): pl.pallas_call(functools.partial(cached_kernel, requests, span_devs, 4),...  8.5 us
    pallas_call x1, Pallas kernels, self_attention(): pl.pallas_call(functools.partial(self_kernel, span_devs), out_shape=[jax....  7.79 us
    all_to_all x1, starting transfers between devices, body(): lax.all_to_all(q, 'tensor', split_axis=0, concat_axis=0, tiled=True)  6.14 us
    all_to_all x1, waiting for transfers between devices, body(): lax.all_to_all(parts, 'tensor', split_axis=0, concat_axis=0, tiled=True)  6.13 us
  transfers between devices with their start and end apart: 31, of which 17 were waited for; matrix products, arithmetic and copies ran while one was open for 3% of the time, Pallas kernels for 32%

profile of v3, /device:TPU:9, one launch (start us, length us, event | category | flops | bytes accessed | tf_op | source)
XLA Modules:
  0.0 227.9 jit_solution(17389333241692005845)
XLA Ops:
  0.0 0.8 slice_bitcast_fusion
  0.8 2.5 %collective-permute-start.1 = (bf16[64,256]{1,0:T(8,128)(2,1)S(1)}, bf16[64,256]{1,0:T(8,128)(2,1)S(1)}, u32[]{:S(2)}, u32[]{:S(2)}) collective-permute-start(bf16[64,256]{1,0:T(8,128)(2,1)S(1)} %get-tuple-element.58), channel_id=1, source_target_pairs={{0,4},{1,5},{2,6},{3,7},{4,0},{5,1},{6,2},{7,3},{8,12},{9,13},{10,... | collective-permute-start | bytes 98312 | tf_op jit(solution)/shard_map/ppermute | solution.py:39
  3.3 0.2 collective-permute-start.2
  3.5 1.5 collective-permute-done.1
  5.0 1.6 collective-permute-done.2
  6.7 1.3 collective-permute-start.4
  8.0 1.2 collective-permute-start.5
  9.1 1.5 fusion
  10.6 0.8 slice.19
  11.5 0.3 collective-permute-start.3
  11.7 0.8 pad_maximum_fusion.8
  12.5 0.3 collective-permute-done.5
  12.8 3.5 %collective-permute-done.3 = bf16[4,64,256]{2,1,0:T(8,128)(2,1)S(1)} collective-permute-done((bf16[4,64,256]{2,1,0:T(8,128)(2,1)S(1)}, bf16[4,64,256]{2,1,0:T(8,128)(2,1)S(1)}, u32[]{:S(2)}, u32[]{:S(2)}) %collective-permute-start.3) | collective-permute-done | bytes 131104 | tf_op jit(solution)/shard_map/ppermute | solution.py:39
  16.4 2.9 %collective-permute-start.6 = (bf16[2,8,64,256]{3,2,1,0:T(8,128)(2,1)S(1)}, bf16[2,8,64,256]{3,2,1,0:T(8,128)(2,1)S(1)}, u32[]{:S(2)}, u32[]{:S(2)}) collective-permute-start(bf16[2,8,64,256]{3,2,1,0:T(8,128)(2,1)S(1)} %pad_maximum_fusion.3.even), channel_id=1, source_target_pairs={{0,8},{1,9},{2,10},{3,11},{4,12},{5,13},{6,14},{7,15},{8,0},{9,1},... | collective-permute-start | bytes 1572872 | tf_op jit(solution)/shard_map/ppermute | solution.py:39
  19.4 1.3 fusion.2.normed.refs_2_
  20.9 2.9 %project_queries.1.refs_1_ = bf16[8,64,512]{2,1,0:T(8,128)(2,1)} custom-call(s32[2]{0:T(128)S(1)} %pad_add_fusion.info.refs_0_, bf16[512,1024]{1,0:T(8,128)(2,1)} %fusion.2.normed.refs_2_, bf16[2,8,64,256]{3,2,1,0:T(8,128)(2,1)S(1)} %pad_maximum_fusion.3.even, bf16[2,8,64,256]{3,2,1,0:T(8,128)(2,1)S(1)} %collective-permute-done.6.odd), custom_call_target="tpu_custom_call" | custom-call | flops 1000000000 | bytes 2000000 | tf_op jit(solution)/shard_map/project_queries/pallas_call | solution.py:182
  23.8 3.2 %collective-permute-start.7 = (bf16[512,1024]{1,0:T(8,128)(2,1)S(1)}, bf16[512,1024]{1,0:T(8,128)(2,1)}, u32[]{:S(2)}, u32[]{:S(2)}) collective-permute-start(bf16[512,1024]{1,0:T(8,128)(2,1)S(1)} %copy-done.7), channel_id=1, source_target_pairs={{0,1},{2,3},{4,5},{6,7},{8,9},{10,11},{12,13},{14,15},{16,17},{18,... | collective-permute-start | bytes 3145736 | tf_op jit(solution)/shard_map/ppermute | solution.py:522
  26.9 6.1 %all-to-all-start = ((bf16[8,64,512]{2,1,0:T(8,128)(2,1)}), bf16[8,64,512]{2,1,0:T(8,128)(2,1)S(1)}, u32[]{:S(2)}, u32[]{:S(2)}) async-start(bf16[8,64,512]{2,1,0:T(8,128)(2,1)} %project_queries.1.refs_1_), calls=%async_computation | async-start | bytes 1048576 | tf_op jit(solution)/shard_map/all_to_all | solution.py:510
  33.1 0.2 collective-permute-start.8
  33.2 2.2 collective-permute-start.9
  35.5 0.3 collective-permute-start.10
  35.7 8.7 %collective-permute-done.8 = bf16[192,256]{1,0:T(8,128)(2,1)S(1)} collective-permute-done((bf16[192,256]{1,0:T(8,128)(2,1)S(1)}, bf16[192,256]{1,0:T(8,128)(2,1)S(1)}, u32[]{:S(2)}, u32[]{:S(2)}) %collective-permute-start.8) | collective-permute-done | bytes 98336 | tf_op jit(solution)/shard_map/ppermute | solution.py:39
  44.4 6.4 %collective-permute-done.9 = bf16[192,256]{1,0:T(8,128)(2,1)S(1)} collective-permute-done((bf16[192,256]{1,0:T(8,128)(2,1)S(1)}, bf16[192,256]{1,0:T(8,128)(2,1)S(1)}, u32[]{:S(2)}, u32[]{:S(2)}) %collective-permute-start.9) | collective-permute-done | bytes 98336 | tf_op jit(solution)/shard_map/ppermute | solution.py:39
  50.8 3.5 %collective-permute-done.10 = bf16[192,256]{1,0:T(8,128)(2,1)S(1)} collective-permute-done((bf16[192,256]{1,0:T(8,128)(2,1)S(1)}, bf16[192,256]{1,0:T(8,128)(2,1)S(1)}, u32[]{:S(2)}, u32[]{:S(2)}) %collective-permute-start.10) | collective-permute-done | bytes 98336 | tf_op jit(solution)/shard_map/ppermute | solution.py:39
  54.4 1.4 collective-permute-start.11
  55.8 1.2 collective-permute-start.12
  57.1 8.5 %cached_attention.1.refs_6_ = bf16[8,80,512]{2,1,0:T(8,128)(2,1)} custom-call(s32[4]{0:T(128)S(1)} %copy-done.3, s32[1,128]{1,0:T(1,128)S(1)} %copy-done.4, bf16[8,64,512]{2,1,0:T(8,128)(2,1)S(1)} %all-to-all-done.q_ref, bf16[128,128,128]{2,1,0:T(8,128)(2,1)} %kv_ref.1), custom_call_target="tpu_custom_call" | custom-call | flops 8000000000 | bytes 6000000 | tf_op jit(solution)/shard_map/cached_attention/pallas_call | solution.py:146
  65.8 7.3 %collective-permute-done.13 = bf16[4,192,256]{2,1,0:T(8,128)(2,1)S(1)} collective-permute-done((bf16[4,192,256]{2,1,0:T(8,128)(2,1)S(1)}, bf16[4,192,256]{2,1,0:T(8,128)(2,1)S(1)}, u32[]{:S(2)}, u32[]{:S(2)}) %collective-permute-start.13) | collective-permute-done | bytes 393248 | tf_op jit(solution)/shard_map/ppermute | solution.py:39
  73.4 2.7 %collective-permute-start.14 = (bf16[2,8,192,256]{3,2,1,0:T(8,128)(2,1)S(1)}, bf16[2,8,192,256]{3,2,1,0:T(8,128)(2,1)}, u32[]{:S(2)}, u32[]{:S(2)}) collective-permute-start(bf16[2,8,192,256]{3,2,1,0:T(8,128)(2,1)S(1)} %pad_maximum_fusion.refs_4_), channel_id=1, source_target_pairs={{0,8},{1,9},{2,10},{3,11},{4,12},{5,13},{6,14},{7,15},{8,0},{9,1},... | collective-permute-start | bytes 4718600 | tf_op jit(solution)/shard_map/ppermute | solution.py:39
  76.2 0.6 fusion.8
  76.8 5.1 %all-to-all-start.1 = ((bf16[8,80,512]{2,1,0:T(8,128)(2,1)}), bf16[8,80,512]{2,1,0:T(8,128)(2,1)S(1)}, u32[]{:S(2)}, u32[]{:S(2)}) async-start(bf16[8,80,512]{2,1,0:T(8,128)(2,1)} %cached_attention.1.refs_6_), calls=%async_computation.1 | async-start | bytes 1310720 | tf_op jit(solution)/shard_map/all_to_all | solution.py:528
  81.9 0.6 gather_fusion
  82.6 0.2 copy.27
  82.8 0.2 fusion.7.hits
  83.0 7.8 %self_attention.1 = (f32[8,88,512]{2,1,0:T(8,128)}, bf16[512,1024]{1,0:T(8,128)(2,1)}) custom-call(s32[2]{0:T(128)S(1)} %pad_add_fusion.info.refs_0_, bf16[8,64,512]{2,1,0:T(8,128)(2,1)} %project_queries.1.refs_1_, bf16[512,1024]{1,0:T(8,128)(2,1)} %fusion.2.normed.refs_2_, bf16[512,1024]{1,0:T(8,128)(2,1)} %collective-permute-done.7.refs_3_, ...), custom_call_target="tpu_custom_call" | custom-call | flops 4000000000 | bytes 5000000 | tf_op jit(solution)/shard_map/self_attention/pallas_call | solution.py:275
  90.8 6.1 %all-to-all-done.1.cached = bf16[8,80,512]{2,1,0:T(8,128)(2,1)S(1)} async-done(((bf16[8,80,512]{2,1,0:T(8,128)(2,1)}), bf16[8,80,512]{2,1,0:T(8,128)(2,1)S(1)}, u32[]{:S(2)}, u32[]{:S(2)}) %all-to-all-start.1) | async-done | bytes 655392 | tf_op jit(solution)/shard_map/all_to_all | solution.py:528
  97.0 0.8 copy-done.8
  97.8 5.5 %merge_and_dispatch.1 = (f32[512,1024]{1,0:T(8,128)}, f32[512,8]{1,0:T(8,128)S(1)}, bf16[512,1024]{1,0:T(8,128)(2,1)}, bf16[160,1024]{1,0:T(8,128)(2,1)S(1)}, bf...) custom-call(bf16[512,1024]{1,0:T(8,128)(2,1)} %tokens.1, ...), custom_call_target="tpu_custom_call" | custom-call | flops 4000000000 | bytes 10000000 | tf_op jit(solution)/shard_map/merge_and_dispatch/pallas_call | solution.py:359
  103.3 2.9 %collective-permute-start.17 = (bf16[160,1024]{1,0:T(8,128)(2,1)}, bf16[160,1024]{1,0:T(8,128)(2,1)S(1)}, u32[]{:S(2)}, u32[]{:S(2)}) collective-permute-start(bf16[160,1024]{1,0:T(8,128)(2,1)} %get-tuple-element.41), channel_id=1, source_target_pairs={{0,3},{1,2},{2,1},{3,0},{4,7},{5,6},{6,5},{7,4},{8,11},{9,10},{10,... | collective-permute-start | bytes 983048 | tf_op jit(solution)/shard_map/ppermute | solution.py:39
  106.2 0.3 collective-permute-start.15
  106.5 2.2 collective-permute-start.21
  108.7 1.1 collective-permute-start.22
  109.8 13.9 %collective-permute-done.17.refs_3_.refs_2_ = bf16[160,1024]{1,0:T(8,128)(2,1)S(1)} collective-permute-done((bf16[160,1024]{1,0:T(8,128)(2,1)}, bf16[160,1024]{1,0:T(8,128)(2,1)S(1)}, u32[]{:S(2)}, u32[]{:S(2)}) %collective-permute-start.17) | collective-permute-done | bytes 327712 | tf_op jit(solution)/shard_map/ppermute | solution.py:39
  123.7 1.9 dispatch.1
  125.5 1.5 collective-permute-start.25
  127.1 3.6 %collective-permute-done.16.refs_2_ = bf16[160,1024]{1,0:T(8,128)(2,1)S(1)} collective-permute-done((bf16[160,1024]{1,0:T(8,128)(2,1)}, bf16[160,1024]{1,0:T(8,128)(2,1)S(1)}, u32[]{:S(2)}, u32[]{:S(2)}) %collective-permute-start.16) | collective-permute-done | bytes 327712 | tf_op jit(solution)/shard_map/ppermute | solution.py:39
  130.7 0.7 copy-done.12
  131.4 18.5 %expert.3 = (bf16[160,1024]{1,0:T(8,128)(2,1)S(1)}, bf16[160,1024]{1,0:T(8,128)(2,1)S(1)}, bf16[160,1024]{1,0:T(8,128)(2,1)S(1)}, bf16[160,1024]{1,0:T(8,128)(2,1)S(1)}) custom-call(bf16[160,1024]{1,0:T(8,128)(2,1)S(1)} %get-tuple-element.38.refs_0_, bf16[160,1024]{1,0:T(8,128)(2,1)} %copy-done.11, bf16[160,1024]{1,0:T(8,128)(2,1)} %copy-done.12, ...), custom_call_target="tpu_custom_call" | custom-call | flops 11072962560 | bytes 17301504 | tf_op jit(solution)/shard_map/expert/pallas_call | solution.py:421
  149.9 14.0 %expert.4 = (bf16[160,1024]{1,0:T(8,128)(2,1)S(1)}, bf16[160,1024]{1,0:T(8,128)(2,1)S(1)}) custom-call(bf16[160,1024]{1,0:T(8,128)(2,1)S(1)} %collective-permute-done.21.refs_0_, bf16[160,1024]{1,0:T(8,128)(2,1)S(1)} %collective-permute-done.22.refs_1_, bf16[1,1024,5632]{2,1,0:T(8,128)(2,1)} %refs_3_.3, bf16[1,1024,5632]{2,1,0:T(8,128)(2,1)} %refs_3_.3, ...), custom_call_target="tpu_custom_call" | custom-call | flops 5536481280 | bytes 17301504 | tf_op jit(solution)/shard_map/expert/pallas_call | solution.py:421
  163.9 3.8 %collective-permute-start.23 = (bf16[160,1024]{1,0:T(8,128)(2,1)S(1)}, bf16[160,1024]{1,0:T(8,128)(2,1)S(1)}, u32[]{:S(2)}, u32[]{:S(2)}) collective-permute-start(bf16[160,1024]{1,0:T(8,128)(2,1)S(1)} %get-tuple-element.48.refs_5_), channel_id=1, source_target_pairs={{0,4},{1,5},{2,6},{3,7},{4,0},{5,1},{6,2},{7,3},{8,12},{9,13},{10,... | collective-permute-start | bytes 983048 | tf_op jit(solution)/shard_map/ppermute | solution.py:39
  167.7 1.2 collective-permute-start.18
  169.0 0.8 collective-permute-start.19
  169.8 0.6 collective-permute-start.20
  170.4 14.0 %expert.5 = (bf16[160,1024]{1,0:T(8,128)(2,1)S(1)}, bf16[160,1024]{1,0:T(8,128)(2,1)S(1)}) custom-call(bf16[160,1024]{1,0:T(8,128)(2,1)S(1)} %collective-permute-done.25.refs_0_, bf16[160,1024]{1,0:T(8,128)(2,1)S(1)} %collective-permute-done.26.refs_1_, bf16[1,1024,5632]{2,1,0:T(8,128)(2,1)} %refs_3_.3, bf16[1,1024,5632]{2,1,0:T(8,128)(2,1)} %refs_3_.3, ...), custom_call_target="tpu_custom_call" | custom-call | flops 5536481280 | bytes 17301504 | tf_op jit(solution)/shard_map/expert/pallas_call | solution.py:421
  184.4 1.2 collective-permute-start.27
  185.7 1.2 collective-permute-start.28
  186.9 0.2 bitcast_select_fusion.refs_2_
  187.1 2.9 %collective-permute-done.20.refs_6_ = bf16[160,1024]{1,0:T(8,128)(2,1)S(1)} collective-permute-done((bf16[160,1024]{1,0:T(8,128)(2,1)S(1)}, bf16[160,1024]{1,0:T(8,128)(2,1)S(1)}, u32[]{:S(2)}, u32[]{:S(2)}) %collective-permute-start.20) | collective-permute-done | bytes 327712 | tf_op jit(solution)/shard_map/ppermute | solution.py:39
  190.0 4.4 %combine.3.refs_0_ = f32[512,1024]{1,0:T(8,128)} custom-call(f32[512,1024]{1,0:T(8,128)} %get-tuple-element.36.refs_0_, f32[512,8]{1,0:T(8,128)S(1)} %get-tuple-element.37.refs_7_.refs_1_, s32[512,8]{1,0:T(8,128)S(1)} %bitcast_select_fusion.refs_2_, bf16[160,1024]{1,0:T(8,128)(2,1)S(1)} %get-tuple-element.42.refs_3_.refs_5_, ...), custom_call_target="tpu_custom_call" | custom-call | flops 671088640 | bytes 6000000 | tf_op jit(solution)/shard_map/combine/pallas_call | solution.py:465
  194.4 5.0 %collective-permute-done.24.refs_4_ = bf16[160,1024]{1,0:T(8,128)(2,1)S(1)} collective-permute-done((bf16[160,1024]{1,0:T(8,128)(2,1)S(1)}, bf16[160,1024]{1,0:T(8,128)(2,1)S(1)}, u32[]{:S(2)}, u32[]{:S(2)}) %collective-permute-start.24) | collective-permute-done | bytes 327712 | tf_op jit(solution)/shard_map/ppermute | solution.py:39
  199.4 3.7 %combine.4.refs_0_ = f32[512,1024]{1,0:T(8,128)} custom-call(f32[512,1024]{1,0:T(8,128)} %combine.3.refs_0_, f32[512,8]{1,0:T(8,128)S(1)} %get-tuple-element.37.refs_7_.refs_1_, s32[512,8]{1,0:T(8,128)S(1)} %bitcast_select_fusion.refs_2_, bf16[160,1024]{1,0:T(8,128)(2,1)S(1)} %collective-permute-done.23.refs_3_, ...), custom_call_target="tpu_custom_call" | custom-call | flops 335544320 | bytes 6000000 | tf_op jit(solution)/shard_map/combine/pallas_call | solution.py:465
  203.1 14.2 %collective-permute-done.27.refs_3_ = bf16[160,1024]{1,0:T(8,128)(2,1)S(1)} collective-permute-done((bf16[160,1024]{1,0:T(8,128)(2,1)S(1)}, bf16[160,1024]{1,0:T(8,128)(2,1)S(1)}, u32[]{:S(2)}, u32[]{:S(2)}) %collective-permute-start.27) | collective-permute-done | bytes 327712 | tf_op jit(solution)/shard_map/ppermute | solution.py:39
  217.4 7.1 %collective-permute-done.28.refs_4_ = bf16[160,1024]{1,0:T(8,128)(2,1)S(1)} collective-permute-done((bf16[160,1024]{1,0:T(8,128)(2,1)S(1)}, bf16[160,1024]{1,0:T(8,128)(2,1)S(1)}, u32[]{:S(2)}, u32[]{:S(2)}) %collective-permute-start.28) | collective-permute-done | bytes 327712 | tf_op jit(solution)/shard_map/ppermute | solution.py:39
  224.5 3.4 %combine.5 = bf16[512,1024]{1,0:T(8,128)(2,1)} custom-call(f32[512,1024]{1,0:T(8,128)} %combine.4.refs_0_, f32[512,8]{1,0:T(8,128)S(1)} %get-tuple-element.37.refs_7_.refs_1_, s32[512,8]{1,0:T(8,128)S(1)} %bitcast_select_fusion.refs_2_, bf16[160,1024]{1,0:T(8,128)(2,1)S(1)} %collective-permute-done.27.refs_3_, ...), custom_call_target="tpu_custom_call" | custom-call | flops 335544320 | bytes 6000000 | tf_op jit(solution)/shard_map/combine/pallas_call | solution.py:465
  (66 shorter events, 1.5 us)
Async XLA Ops:
  0.0 81.9 %copy-start = (bf16[1024,8]{0,1:T(8,128)(2,1)S(1)}, bf16[1024,8]{0,1:T(8,128)(2,1)}, u32[]{:S(2)}) copy-start(bf16[1024,8]{0,1:T(8,128)(2,1)} %param.20) | copy-start | bytes 49156
  0.8 2.8 %collective-permute-start = (bf16[64,256]{1,0:T(8,128)(2,1)S(1)}, bf16[64,256]{1,0:T(8,128)(2,1)S(1)}, u32[]{:S(2)}, u32[]{:S(2)}) collective-permute-start(bf16[64,256]{1,0:T(8,128)(2,1)S(1)} %get-tuple-element.58), channel_id=1, source_target_pairs={{0,2},{1,3},{2,0},{3,1},{4,6},{5,7},{6,4},{7,5},{8,10},{9,11},{10,... | collective-permute-start | bytes 98312 | tf_op jit(solution)/shard_map/ppermute | solution.py:39
  0.8 4.2 %collective-permute-start.1 = (bf16[64,256]{1,0:T(8,128)(2,1)S(1)}, bf16[64,256]{1,0:T(8,128)(2,1)S(1)}, u32[]{:S(2)}, u32[]{:S(2)}) collective-permute-start(bf16[64,256]{1,0:T(8,128)(2,1)S(1)} %get-tuple-element.58), channel_id=1, source_target_pairs={{0,4},{1,5},{2,6},{3,7},{4,0},{5,1},{6,2},{7,3},{8,12},{9,13},{10,... | collective-permute-start | bytes 98312 | tf_op jit(solution)/shard_map/ppermute | solution.py:39
  3.3 3.4 %collective-permute-start.2 = (bf16[64,256]{1,0:T(8,128)(2,1)S(1)}, bf16[64,256]{1,0:T(8,128)(2,1)S(1)}, u32[]{:S(2)}, u32[]{:S(2)}) collective-permute-start(bf16[64,256]{1,0:T(8,128)(2,1)S(1)} %get-tuple-element.58), channel_id=1, source_target_pairs={{0,6},{1,7},{2,4},{3,5},{4,2},{5,3},{6,0},{7,1},{8,14},{9,15},{10,... | collective-permute-start | bytes 98312 | tf_op jit(solution)/shard_map/ppermute | solution.py:39
  6.6 12.8 %copy-start.5 = (bf16[512,1024]{1,0:T(8,128)(2,1)S(1)}, bf16[512,1024]{1,0:T(8,128)(2,1)}, u32[]{:S(2)}) copy-start(bf16[512,1024]{1,0:T(8,128)(2,1)} %tokens.1) | copy-start | bytes 3145732
  6.7 12.8 %copy-start.9 = (f32[1024]{0:T(1024)S(1)}, f32[1024]{0:T(1024)}, u32[]{:S(2)}) copy-start(f32[1024]{0:T(1024)} %param.13) | copy-start | bytes 12292
  6.7 5.8 %collective-permute-start.4 = (bf16[4,64,256]{2,1,0:T(8,128)(2,1)S(1)}, bf16[4,64,256]{2,1,0:T(8,128)(2,1)S(1)}, u32[]{:S(2)}, u32[]{:S(2)}) collective-permute-start(bf16[4,64,256]{2,1,0:T(8,128)(2,1)S(1)} %get-tuple-element.56), channel_id=1, source_target_pairs={{0,16},{1,17},{2,18},{3,19},{4,20},{5,21},{6,22},{7,23},{8,24},{9,... | collective-permute-start | bytes 393224 | tf_op jit(solution)/shard_map/ppermute | solution.py:39
  8.0 4.8 %collective-permute-start.5 = (bf16[4,64,256]{2,1,0:T(8,128)(2,1)S(1)}, bf16[4,64,256]{2,1,0:T(8,128)(2,1)S(1)}, u32[]{:S(2)}, u32[]{:S(2)}) collective-permute-start(bf16[4,64,256]{2,1,0:T(8,128)(2,1)S(1)} %get-tuple-element.56), channel_id=1, source_target_pairs={{0,17},{1,16},{2,19},{3,18},{4,21},{5,20},{6,23},{7,22},{8,25},{9,... | collective-permute-start | bytes 393224 | tf_op jit(solution)/shard_map/ppermute | solution.py:39
  11.5 4.8 %collective-permute-start.3 = (bf16[4,64,256]{2,1,0:T(8,128)(2,1)S(1)}, bf16[4,64,256]{2,1,0:T(8,128)(2,1)S(1)}, u32[]{:S(2)}, u32[]{:S(2)}) collective-permute-start(bf16[4,64,256]{2,1,0:T(8,128)(2,1)S(1)} %get-tuple-element.56), channel_id=1, source_target_pairs={{0,1},{1,0},{2,3},{3,2},{4,5},{5,4},{6,7},{7,6},{8,9},{9,8},{10,11... | collective-permute-start | bytes 393224 | tf_op jit(solution)/shard_map/ppermute | solution.py:39
  16.4 4.4 %collective-permute-start.6 = (bf16[2,8,64,256]{3,2,1,0:T(8,128)(2,1)S(1)}, bf16[2,8,64,256]{3,2,1,0:T(8,128)(2,1)S(1)}, u32[]{:S(2)}, u32[]{:S(2)}) collective-permute-start(bf16[2,8,64,256]{3,2,1,0:T(8,128)(2,1)S(1)} %pad_maximum_fusion.3.even), channel_id=1, source_target_pairs={{0,8},{1,9},{2,10},{3,11},{4,12},{5,13},{6,14},{7,15},{8,0},{9,1},... | collective-permute-start | bytes 1572872 | tf_op jit(solution)/shard_map/ppermute | solution.py:39
  20.7 3.1 %copy-start.7 = (bf16[512,1024]{1,0:T(8,128)(2,1)S(1)}, bf16[512,1024]{1,0:T(8,128)(2,1)}, u32[]{:S(2)}) copy-start(bf16[512,1024]{1,0:T(8,128)(2,1)} %fusion.2.normed.refs_2_) | copy-start | bytes 3145732
  20.7 36.4 %copy-start.3 = (s32[4]{0:T(128)S(1)}, s32[4]{0:T(128)}, u32[]{:S(2)}) copy-start(s32[4]{0:T(128)} %lengths.1) | copy-start | bytes 52
  20.7 36.4 %copy-start.4 = (s32[1,128]{1,0:T(1,128)S(1)}, s32[1,128]{1,0:T(1,128)}, u32[]{:S(2)}) copy-start(s32[1,128]{1,0:T(1,128)} %table.1) | copy-start | bytes 1540
  23.8 30.6 %collective-permute-start.7 = (bf16[512,1024]{1,0:T(8,128)(2,1)S(1)}, bf16[512,1024]{1,0:T(8,128)(2,1)}, u32[]{:S(2)}, u32[]{:S(2)}) collective-permute-start(bf16[512,1024]{1,0:T(8,128)(2,1)S(1)} %copy-done.7), channel_id=1, source_target_pairs={{0,1},{2,3},{4,5},{6,7},{8,9},{10,11},{12,13},{14,15},{16,17},{18,... | collective-permute-start | bytes 3145736 | tf_op jit(solution)/shard_map/ppermute | solution.py:522
  26.9 30.2 %all-to-all-start = ((bf16[8,64,512]{2,1,0:T(8,128)(2,1)}), bf16[8,64,512]{2,1,0:T(8,128)(2,1)S(1)}, u32[]{:S(2)}, u32[]{:S(2)}) async-start(bf16[8,64,512]{2,1,0:T(8,128)(2,1)} %project_queries.1.refs_1_), calls=%async_computation | async-start | bytes 1048576 | tf_op jit(solution)/shard_map/all_to_all | solution.py:510
  33.1 11.3 %collective-permute-start.8 = (bf16[192,256]{1,0:T(8,128)(2,1)S(1)}, bf16[192,256]{1,0:T(8,128)(2,1)S(1)}, u32[]{:S(2)}, u32[]{:S(2)}) collective-permute-start(bf16[192,256]{1,0:T(8,128)(2,1)S(1)} %pad_maximum_fusion.8), channel_id=1, source_target_pairs={{0,2},{1,3},{2,0},{3,1},{4,6},{5,7},{6,4},{7,5},{8,10},{9,11},{10,... | collective-permute-start | bytes 294920 | tf_op jit(solution)/shard_map/ppermute | solution.py:39
  33.2 17.6 %collective-permute-start.9 = (bf16[192,256]{1,0:T(8,128)(2,1)S(1)}, bf16[192,256]{1,0:T(8,128)(2,1)S(1)}, u32[]{:S(2)}, u32[]{:S(2)}) collective-permute-start(bf16[192,256]{1,0:T(8,128)(2,1)S(1)} %pad_maximum_fusion.8), channel_id=1, source_target_pairs={{0,4},{1,5},{2,6},{3,7},{4,0},{5,1},{6,2},{7,3},{8,12},{9,13},{10,... | collective-permute-start | bytes 294920 | tf_op jit(solution)/shard_map/ppermute | solution.py:39
  35.5 18.9 %collective-permute-start.10 = (bf16[192,256]{1,0:T(8,128)(2,1)S(1)}, bf16[192,256]{1,0:T(8,128)(2,1)S(1)}, u32[]{:S(2)}, u32[]{:S(2)}) collective-permute-start(bf16[192,256]{1,0:T(8,128)(2,1)S(1)} %pad_maximum_fusion.8), channel_id=1, source_target_pairs={{0,6},{1,7},{2,4},{3,5},{4,2},{5,3},{6,0},{7,1},{8,14},{9,15},{10,... | collective-permute-start | bytes 294920 | tf_op jit(solution)/shard_map/ppermute | solution.py:39
  54.4 11.2 %collective-permute-start.11 = (bf16[4,192,256]{2,1,0:T(8,128)(2,1)S(1)}, bf16[4,192,256]{2,1,0:T(8,128)(2,1)S(1)}, u32[]{:S(2)}, u32[]{:S(2)}) collective-permute-start(bf16[4,192,256]{2,1,0:T(8,128)(2,1)S(1)} %pad_maximum_fusion.4), channel_id=1, source_target_pairs={{0,1},{1,0},{2,3},{3,2},{4,5},{5,4},{6,7},{7,6},{8,9},{9,8},{10,11... | collective-permute-start | bytes 1179656 | tf_op jit(solution)/shard_map/ppermute | solution.py:39
  55.8 10.0 %collective-permute-start.12 = (bf16[4,192,256]{2,1,0:T(8,128)(2,1)S(1)}, bf16[4,192,256]{2,1,0:T(8,128)(2,1)S(1)}, u32[]{:S(2)}, u32[]{:S(2)}) collective-permute-start(bf16[4,192,256]{2,1,0:T(8,128)(2,1)S(1)} %pad_maximum_fusion.4), channel_id=1, source_target_pairs={{0,16},{1,17},{2,18},{3,19},{4,20},{5,21},{6,22},{7,23},{8,24},{9,... | collective-permute-start | bytes 1179656 | tf_op jit(solution)/shard_map/ppermute | solution.py:39
  57.0 16.1 %collective-permute-start.13 = (bf16[4,192,256]{2,1,0:T(8,128)(2,1)S(1)}, bf16[4,192,256]{2,1,0:T(8,128)(2,1)S(1)}, u32[]{:S(2)}, u32[]{:S(2)}) collective-permute-start(bf16[4,192,256]{2,1,0:T(8,128)(2,1)S(1)} %pad_maximum_fusion.4), channel_id=1, source_target_pairs={{0,17},{1,16},{2,19},{3,18},{4,21},{5,20},{6,23},{7,22},{8,25},{9,... | collective-permute-start | bytes 1179656 | tf_op jit(solution)/shard_map/ppermute | solution.py:39
  73.2 3.0 %copy-start.10 = (s32[512,2]{0,1:T(2,128)S(1)}, s32[512,2]{0,1:T(2,128)}, u32[]{:S(2)}) copy-start(s32[512,2]{0,1:T(2,128)} %param.21) | copy-start | bytes 12292
  73.4 9.1 %copy-start.6 = (bf16[2,8,192,256]{3,2,1,0:T(8,128)(2,1)}, bf16[2,8,192,256]{3,2,1,0:T(8,128)(2,1)S(1)}, u32[]{:S(2)}) copy-start(bf16[2,8,192,256]{3,2,1,0:T(8,128)(2,1)S(1)} %pad_maximum_fusion.refs_4_) | copy-start | bytes 4718596
  73.4 9.6 %collective-permute-start.14 = (bf16[2,8,192,256]{3,2,1,0:T(8,128)(2,1)S(1)}, bf16[2,8,192,256]{3,2,1,0:T(8,128)(2,1)}, u32[]{:S(2)}, u32[]{:S(2)}) collective-permute-start(bf16[2,8,192,256]{3,2,1,0:T(8,128)(2,1)S(1)} %pad_maximum_fusion.refs_4_), channel_id=1, source_target_pairs={{0,8},{1,9},{2,10},{3,11},{4,12},{5,13},{6,14},{7,15},{8,0},{9,1},... | collective-permute-start | bytes 4718600 | tf_op jit(solution)/shard_map/ppermute | solution.py:39
  76.8 20.1 %all-to-all-start.1 = ((bf16[8,80,512]{2,1,0:T(8,128)(2,1)}), bf16[8,80,512]{2,1,0:T(8,128)(2,1)S(1)}, u32[]{:S(2)}, u32[]{:S(2)}) async-start(bf16[8,80,512]{2,1,0:T(8,128)(2,1)} %cached_attention.1.refs_6_), calls=%async_computation.1 | async-start | bytes 1310720 | tf_op jit(solution)/shard_map/all_to_all | solution.py:528
  83.0 14.8 %copy-start.2 = (f32[1024]{0:T(1024)S(1)}, f32[1024]{0:T(1024)}, u32[]{:S(2)}) copy-start(f32[1024]{0:T(1024)} %param.19) | copy-start | bytes 12292
  97.0 0.8 copy-start.8
  103.3 20.4 %collective-permute-start.17 = (bf16[160,1024]{1,0:T(8,128)(2,1)}, bf16[160,1024]{1,0:T(8,128)(2,1)S(1)}, u32[]{:S(2)}, u32[]{:S(2)}) collective-permute-start(bf16[160,1024]{1,0:T(8,128)(2,1)} %get-tuple-element.41), channel_id=1, source_target_pairs={{0,3},{1,2},{2,1},{3,0},{4,7},{5,6},{6,5},{7,4},{8,11},{9,10},{10,... | collective-permute-start | bytes 983048 | tf_op jit(solution)/shard_map/ppermute | solution.py:39
  106.2 20.8 %collective-permute-start.15 = (bf16[160,1024]{1,0:T(8,128)(2,1)}, bf16[160,1024]{1,0:T(8,128)(2,1)S(1)}, u32[]{:S(2)}, u32[]{:S(2)}) collective-permute-start(bf16[160,1024]{1,0:T(8,128)(2,1)} %get-tuple-element.39), channel_id=1, source_target_pairs={{0,1},{1,0},{2,3},{3,2},{4,5},{5,4},{6,7},{7,6},{8,9},{9,8},{10,11... | collective-permute-start | bytes 983048 | tf_op jit(solution)/shard_map/ppermute | solution.py:39
  106.5 24.1 %collective-permute-start.16 = (bf16[160,1024]{1,0:T(8,128)(2,1)}, bf16[160,1024]{1,0:T(8,128)(2,1)S(1)}, u32[]{:S(2)}, u32[]{:S(2)}) collective-permute-start(bf16[160,1024]{1,0:T(8,128)(2,1)} %get-tuple-element.40), channel_id=1, source_target_pairs={{0,2},{1,3},{2,0},{3,1},{4,6},{5,7},{6,4},{7,5},{8,10},{9,11},{10,... | collective-permute-start | bytes 983048 | tf_op jit(solution)/shard_map/ppermute | solution.py:39
  106.5 43.3 %collective-permute-start.21 = (bf16[160,1024]{1,0:T(8,128)(2,1)S(1)}, bf16[160,1024]{1,0:T(8,128)(2,1)S(1)}, u32[]{:S(2)}, u32[]{:S(2)}) collective-permute-start(bf16[160,1024]{1,0:T(8,128)(2,1)S(1)} %get-tuple-element.46), channel_id=1, source_target_pairs={{0,4},{1,5},{2,6},{3,7},{4,0},{5,1},{6,2},{7,3},{8,12},{9,13},{10,... | collective-permute-start | bytes 983048 | tf_op jit(solution)/shard_map/ppermute | solution.py:39
  108.7 41.2 %collective-permute-start.22 = (bf16[160,1024]{1,0:T(8,128)(2,1)S(1)}, bf16[160,1024]{1,0:T(8,128)(2,1)S(1)}, u32[]{:S(2)}, u32[]{:S(2)}) collective-permute-start(bf16[160,1024]{1,0:T(8,128)(2,1)S(1)} %get-tuple-element.47), channel_id=1, source_target_pairs={{0,5},{1,4},{2,7},{3,6},{4,1},{5,0},{6,3},{7,2},{8,13},{9,12},{10,... | collective-permute-start | bytes 983048 | tf_op jit(solution)/shard_map/ppermute | solution.py:39
  123.6 7.0 %copy-start.1 = (bf16[160,1024]{1,0:T(8,128)(2,1)}, bf16[160,1024]{1,0:T(8,128)(2,1)S(1)}, u32[]{:S(2)}) copy-start(bf16[160,1024]{1,0:T(8,128)(2,1)S(1)} %collective-permute-done.17.refs_3_.refs_2_) | copy-start | bytes 983044
  125.5 43.5 %collective-permute-start.25 = (bf16[160,1024]{1,0:T(8,128)(2,1)S(1)}, bf16[160,1024]{1,0:T(8,128)(2,1)S(1)}, u32[]{:S(2)}, u32[]{:S(2)}) collective-permute-start(bf16[160,1024]{1,0:T(8,128)(2,1)S(1)} %get-tuple-element.51), channel_id=1, source_target_pairs={{0,6},{1,7},{2,4},{3,5},{4,2},{5,3},{6,0},{7,1},{8,14},{9,15},{10,... | collective-permute-start | bytes 983048 | tf_op jit(solution)/shard_map/ppermute | solution.py:39
  127.0 3.7 %copy-start.11 = (bf16[160,1024]{1,0:T(8,128)(2,1)}, bf16[160,1024]{1,0:T(8,128)(2,1)S(1)}, u32[]{:S(2)}) copy-start(bf16[160,1024]{1,0:T(8,128)(2,1)S(1)} %collective-permute-done.15.refs_1_) | copy-start | bytes 983044
  127.0 42.8 %collective-permute-start.26 = (bf16[160,1024]{1,0:T(8,128)(2,1)S(1)}, bf16[160,1024]{1,0:T(8,128)(2,1)S(1)}, u32[]{:S(2)}, u32[]{:S(2)}) collective-permute-start(bf16[160,1024]{1,0:T(8,128)(2,1)S(1)} %get-tuple-element.52), channel_id=1, source_target_pairs={{0,7},{1,6},{2,5},{3,4},{4,3},{5,2},{6,1},{7,0},{8,15},{9,14},{10,... | collective-permute-start | bytes 983048 | tf_op jit(solution)/shard_map/ppermute | solution.py:39
  130.7 0.7 copy-start.12
  163.9 30.5 %collective-permute-start.23 = (bf16[160,1024]{1,0:T(8,128)(2,1)S(1)}, bf16[160,1024]{1,0:T(8,128)(2,1)S(1)}, u32[]{:S(2)}, u32[]{:S(2)}) collective-permute-start(bf16[160,1024]{1,0:T(8,128)(2,1)S(1)} %get-tuple-element.48.refs_5_), channel_id=1, source_target_pairs={{0,4},{1,5},{2,6},{3,7},{4,0},{5,1},{6,2},{7,3},{8,12},{9,13},{10,... | collective-permute-start | bytes 983048 | tf_op jit(solution)/shard_map/ppermute | solution.py:39
  167.7 31.7 %collective-permute-start.24 = (bf16[160,1024]{1,0:T(8,128)(2,1)S(1)}, bf16[160,1024]{1,0:T(8,128)(2,1)S(1)}, u32[]{:S(2)}, u32[]{:S(2)}) collective-permute-start(bf16[160,1024]{1,0:T(8,128)(2,1)S(1)} %get-tuple-element.49), channel_id=1, source_target_pairs={{0,5},{1,4},{2,7},{3,6},{4,1},{5,0},{6,3},{7,2},{8,13},{9,12},{10,... | collective-permute-start | bytes 983048 | tf_op jit(solution)/shard_map/ppermute | solution.py:39
  167.7 16.7 %collective-permute-start.18 = (bf16[160,1024]{1,0:T(8,128)(2,1)S(1)}, bf16[160,1024]{1,0:T(8,128)(2,1)S(1)}, u32[]{:S(2)}, u32[]{:S(2)}) collective-permute-start(bf16[160,1024]{1,0:T(8,128)(2,1)S(1)} %get-tuple-element.43), channel_id=1, source_target_pairs={{0,1},{1,0},{2,3},{3,2},{4,5},{5,4},{6,7},{7,6},{8,9},{9,8},{10,11... | collective-permute-start | bytes 983048 | tf_op jit(solution)/shard_map/ppermute | solution.py:39
  169.0 16.7 %collective-permute-start.19 = (bf16[160,1024]{1,0:T(8,128)(2,1)S(1)}, bf16[160,1024]{1,0:T(8,128)(2,1)S(1)}, u32[]{:S(2)}, u32[]{:S(2)}) collective-permute-start(bf16[160,1024]{1,0:T(8,128)(2,1)S(1)} %get-tuple-element.44), channel_id=1, source_target_pairs={{0,2},{1,3},{2,0},{3,1},{4,6},{5,7},{6,4},{7,5},{8,10},{9,11},{10,... | collective-permute-start | bytes 983048 | tf_op jit(solution)/shard_map/ppermute | solution.py:39
  169.8 20.3 %collective-permute-start.20 = (bf16[160,1024]{1,0:T(8,128)(2,1)S(1)}, bf16[160,1024]{1,0:T(8,128)(2,1)S(1)}, u32[]{:S(2)}, u32[]{:S(2)}) collective-permute-start(bf16[160,1024]{1,0:T(8,128)(2,1)S(1)} %get-tuple-element.45), channel_id=1, source_target_pairs={{0,3},{1,2},{2,1},{3,0},{4,7},{5,6},{6,5},{7,4},{8,11},{9,10},{10,... | collective-permute-start | bytes 983048 | tf_op jit(solution)/shard_map/ppermute | solution.py:39
  184.4 32.9 %collective-permute-start.27 = (bf16[160,1024]{1,0:T(8,128)(2,1)S(1)}, bf16[160,1024]{1,0:T(8,128)(2,1)S(1)}, u32[]{:S(2)}, u32[]{:S(2)}) collective-permute-start(bf16[160,1024]{1,0:T(8,128)(2,1)S(1)} %get-tuple-element.53), channel_id=1, source_target_pairs={{0,6},{1,7},{2,4},{3,5},{4,2},{5,3},{6,0},{7,1},{8,14},{9,15},{10,... | collective-permute-start | bytes 983048 | tf_op jit(solution)/shard_map/ppermute | solution.py:39
  185.7 38.8 %collective-permute-start.28 = (bf16[160,1024]{1,0:T(8,128)(2,1)S(1)}, bf16[160,1024]{1,0:T(8,128)(2,1)S(1)}, u32[]{:S(2)}, u32[]{:S(2)}) collective-permute-start(bf16[160,1024]{1,0:T(8,128)(2,1)S(1)} %get-tuple-element.54), channel_id=1, source_target_pairs={{0,7},{1,6},{2,5},{3,4},{4,3},{5,2},{6,1},{7,0},{8,15},{9,14},{10,... | collective-permute-start | bytes 983048 | tf_op jit(solution)/shard_map/ppermute | solution.py:39

commit v4 on v3

--- a/solution.py
+++ b/solution.py
@@ -20,6 +20,12 @@
 
 def dot(a, b, dims=(((1,), (0,)), ((), ()))):
     return lax.dot_general(a, b, dims, preferred_element_type=F32)
+
+
+def rms_norm(values, gain):
+    values = values.astype(F32)
+    mean_square = jnp.mean(values * values, axis=-1, keepdims=True)
+    return (values * lax.rsqrt(mean_square + EPSILON) * gain).astype(BF16)
 
 
 def vmem(count):
@@ -294,16 +300,17 @@
     )(info, q, *normed, even, odd, earlier)
 
 
-def fill(out_refs, which, normed, slot_rows, placing):
+def fill(out_refs, which, values, slot_rows, placing):
     cap = out_refs[0].shape[0]
-    rows = normed.shape[0]
+    rows = values.shape[0]
     for n, s in enumerate(which):
         at_slot = lax.broadcasted_iota(jnp.int32, (cap, rows), 0)
         placing[n * cap : (n + 1) * cap, :] = (
             (at_slot == slot_rows[s : s + 1, :]).astype(F32).astype(BF16)
         )
+    rows_out = dot(placing[0 : len(which) * cap, :], values).astype(BF16)
     for n in range(len(which)):
-        out_refs[n][...] = dot(placing[n * cap : (n + 1) * cap, :], normed).astype(BF16)
+        out_refs[n][...] = rows_out[n * cap : (n + 1) * cap, :]
 
 
 def dispatch_kernel(which, *refs):
@@ -328,10 +335,11 @@
     )(normed, slot_rows, earlier)
 
 
-def merge_kernel(which, tokens, own, cached, w_o, gain, router, hits, slot_rows, *refs):
+def merge_kernel(narrow, which, tokens, own, cached, w_o, gain, router, hits, slot_rows, *refs):
     state_ref, gates_ref, normed_ref = refs[:3]
-    out_refs = refs[3 : 3 + len(which)]
-    attended, placing = refs[3 + len(which) :]
+    count = len(narrow) + len(which)
+    out_refs = refs[3 : 3 + count]
+    attended, placing = refs[3 + count :]
     for s in range(own.shape[0]):
         part = cached[s].astype(F32)
         lse = part[HD : HD + 1] + part[HD + 1 : HD + 2] + part[HD + 2 : HD + 3]
@@ -342,7 +350,9 @@
         norm = 1.0 / (w_cached + w_own * total)
         merged = part[0:HD] * (w_cached * norm) + own[s, 0:HD, :] * (w_own * norm)
         attended[s * HD : (s + 1) * HD, :] = merged.astype(BF16)
-    state = tokens[...].astype(F32) + dot(attended[...].T, w_o[...])
+    rows_attended = attended[...].T
+    fill(out_refs[: len(narrow)], narrow, rows_attended, slot_rows, placing)
+    state = tokens[...].astype(F32) + dot(rows_attended, w_o[...])
     state_ref[...] = state
     mean_square = jnp.mean(state * state, axis=-1, keepdims=True)
     normed = (state * lax.rsqrt(mean_square + EPSILON) * gain[...]).astype(BF16)
@@ -350,25 +360,26 @@
     squashed = jnp.where(hits[...] > 0, jax.nn.sigmoid(logits), 0.0)
     gates_ref[...] = squashed / jnp.sum(squashed, axis=1, keepdims=True)
     normed_ref[...] = normed
-    fill(out_refs, which, normed, slot_rows, placing)
-
-
-def merge_dispatch(tokens, own, cached, w_o, gain, router, hits, slot_rows, which, cap):
+    fill(out_refs[len(narrow) :], which, normed, slot_rows, placing)
+
+
+def merge_dispatch(tokens, own, cached, w_o, gain, router, hits, slot_rows, narrow, which, cap):
     lanes = own.shape[0]
     rows, width = tokens.shape
     return pl.pallas_call(
-        functools.partial(merge_kernel, tuple(which)),
+        functools.partial(merge_kernel, tuple(narrow), tuple(which)),
         out_shape=[
             jax.ShapeDtypeStruct((rows, width), F32),
             jax.ShapeDtypeStruct((rows, lanes), F32),
             jax.ShapeDtypeStruct((rows, width), BF16),
         ]
+        + [jax.ShapeDtypeStruct((cap, lanes * HD), BF16)] * len(narrow)
         + [jax.ShapeDtypeStruct((cap, width), BF16)] * len(which),
         in_specs=vmem(8),
-        out_specs=vmem(3 + len(which)),
+        out_specs=vmem(3 + len(narrow) + len(which)),
         scratch_shapes=[
             pltpu.VMEM((lanes * HD, rows), BF16),
-            pltpu.VMEM((len(which) * cap, rows), BF16),
+            pltpu.VMEM((max(len(narrow), len(which)) * cap, rows), BF16),
         ],
         compiler_params=params(),
         cost_estimate=pl.CostEstimate(
@@ -378,8 +389,12 @@
     )(tokens, own, cached, w_o, gain, router, hits, slot_rows)
 
 
-def expert_kernel(count, *refs):
+def expert_kernel(count, late, *refs):
     x_refs = refs[:count]
+    if late:
+        attended_refs = refs[count : count + late]
+        w_o, gain = refs[count + late : count + late + 2]
+        refs = refs[late + 2 :]
     gate_ref, up_ref, down_ref = refs[count : count + 3]
     out_refs = refs[count + 4 : 2 * count + 4]
     x_all, total = refs[2 * count + 4 :]
@@ -389,7 +404,10 @@
     @pl.when(step == 0)
     def _():
         for n in range(count):
-            x_all[n * cap : (n + 1) * cap, :] = x_refs[n][...]
+            x = x_refs[n][...]
+            if n < late:
+                x = rms_norm(x.astype(F32) + dot(attended_refs[n][...], w_o[...]), gain[...])
+            x_all[n * cap : (n + 1) * cap, :] = x
 
     x = x_all[...]
     gate = dot(x, gate_ref[0])
@@ -411,7 +429,7 @@
             out_refs[n][...] = total[n * cap : (n + 1) * cap, :].astype(BF16)
 
 
-def expert(chunks, w_in, w_out, earlier):
+def expert(chunks, w_in, w_out, earlier, late=()):
     count = len(chunks)
     cap, width = chunks[0].shape
     hidden = w_out.shape[1]
@@ -419,10 +437,11 @@
     steps = hidden // tile
     whole = pl.BlockSpec((cap, width), lambda j: (0, 0))
     return pl.pallas_call(
-        functools.partial(expert_kernel, count),
+        functools.partial(expert_kernel, count, max(0, len(late) - 2)),
         grid=(steps,),
         out_shape=[jax.ShapeDtypeStruct((cap, width), BF16)] * count,
         in_specs=[whole] * count
+        + [pl.BlockSpec(extra.shape, lambda j: (0, 0)) for extra in late]
         + [
             pl.BlockSpec((1, width, tile), lambda j: (0, 0, j)),
             pl.BlockSpec((1, width, tile), lambda j: (0, 0, j + steps)),
@@ -441,10 +460,11 @@
             transcendentals=count * cap * hidden,
         ),
         name="expert",
-    )(*chunks, w_in, w_in, w_out, earlier)
-
-
-def combine_kernel(first, count, last, *refs):
+    )(*chunks, *late, w_in, w_in, w_out, earlier)
+
+
+def combine_kernel(which, *refs):
+    count = len(which)
     base, gates, slots = refs[:3]
     parts = refs[3 : 3 + count]
     out = refs[3 + count]
@@ -452,18 +472,18 @@
     cap = parts[0].shape[0]
     total = base[...]
     for n in range(count):
-        s = first + n
+        s = which[n]
         lane = lax.broadcasted_iota(jnp.int32, (rows, cap), 1)
         pick = (lane == slots[:, s : s + 1]).astype(F32).astype(BF16)
         total = total + gates[:, s : s + 1] * dot(pick, parts[n][...])
     out[...] = total.astype(out.dtype)
 
 
-def combine(base, gates, slots, parts, first, last):
+def combine(base, gates, slots, parts, which, last):
     count = len(parts)
     rows, width = base.shape
     return pl.pallas_call(
-        functools.partial(combine_kernel, first, count, last),
+        functools.partial(combine_kernel, tuple(which)),
         out_shape=jax.ShapeDtypeStruct((rows, width), BF16 if last else F32),
         in_specs=vmem(3 + count),
         out_specs=pl.BlockSpec(memory_space=pltpu.VMEM),
@@ -503,9 +523,7 @@
     q_high = gather_high(w_t[0:HD], lanes, groups)
     q_plane = gather_plane(q_high, lanes, groups)
     q_other = send(q_plane, lanes, lanes, groups)
-    values = tokens.astype(F32)
-    mean_square = jnp.mean(values * values, axis=-1, keepdims=True)
-    normed = (values * lax.rsqrt(mean_square + EPSILON) * gain_attn).astype(BF16)
+    normed = rms_norm(tokens, gain_attn)
     q = project_queries(info, normed, q_plane, q_other)
     q_here = lax.all_to_all(q, "tensor", split_axis=0, concat_axis=0, tiled=True)
 
@@ -523,11 +541,6 @@
     rest = gather_high(rest, lanes, groups)
     rest = gather_plane(after(rest, *near[1:]), lanes, groups)
 
-    parts = cached_attention(cached_lengths, page_table, q_here, kv_cache)
-    rest_other = send(after(rest, parts), lanes, lanes, groups)
-    cached = lax.all_to_all(parts, "tensor", split_axis=0, concat_axis=0, tiled=True)
-    own, w_o = self_attention(info, q, near, rest, rest_other, parts)
-
     names = me ^ jnp.arange(lanes, dtype=jnp.int32)
     hit_rows = (routes[:, 0][None, :] == names[:, None]) | (routes[:, 1][None, :] == names[:, None])
     earlier = jnp.triu(jnp.ones((rows, rows), BF16), 1)
@@ -539,9 +552,19 @@
     cap = -(-capacity // 16) * 16
     router = jnp.take(w_router, names, axis=1)
 
-    half, quarter = lanes // 2, lanes // 4
-    near = list(range(half))
-    far = [list(range(half, half + quarter)), list(range(half + quarter, lanes))]
+    half = lanes // 2
+    near_experts = list(range(half))
+    far = [list(range(half, lanes, 2)), list(range(half + 1, lanes, 2))]
+    ahead = far[0][: max(1, len(far[0]) // 2)]
+    early = dispatch(tokens, slot_rows, ahead, cap, tokens)
+    early = lax.optimization_barrier((*early, q_here))[:-1]
+    early = [send(part, s, lanes, groups) for s, part in zip(ahead, early)]
+
+    parts = cached_attention(cached_lengths, page_table, q_here, kv_cache)
+    rest_other = send(after(rest, parts, *early), lanes, lanes, groups)
+    cached = lax.all_to_all(parts, "tensor", split_axis=0, concat_axis=0, tiled=True)
+    own, w_o = self_attention(info, q, near, rest, rest_other, parts)
+
     outcome = merge_dispatch(
         tokens,
         own,
@@ -551,23 +574,26 @@
         router,
         hits,
         slot_rows,
-        far[0] + near,
+        ahead,
+        far[0][len(ahead) :] + far[1] + near_experts,
         cap,
     )
     state, gates, normed_moe = outcome[:3]
-    buffers = dict(zip(far[0] + near, outcome[3:]))
-    arrived = {s: send(buffers[s], s, lanes, groups) if s else buffers[s] for s in buffers}
-    buffers.update(zip(far[1], dispatch(normed_moe, slot_rows, far[1], cap, arrived[near[-1]])))
-    arrived.update({s: send(buffers[s], s, lanes, groups) for s in far[1]})
+    late = [send(part, s, lanes, groups) for s, part in zip(ahead, outcome[3:])]
+    whole = far[0][len(ahead) :] + far[1] + near_experts
+    arrived = dict(zip(whole, outcome[3 + len(ahead) :]))
+    arrived.update({s: send(arrived[s], s, lanes, groups) for s in whole if s})
+    arrived.update(zip(ahead, early))
     mixed = state
     results = [gates]
-    for part in (near, far[0], far[1]):
-        results = expert([arrived[s] for s in part], w_in, w_out, results[0])
+    for part in (far[0], near_experts, far[1]):
+        more = (*late, w_o, gain_moe.reshape(1, width)) if part is far[0] else ()
+        results = expert([arrived[s] for s in part], w_in, w_out, results[0], more)
         returned = [
             results[n] if s == 0 else send(results[n], s, lanes, groups)
             for n, s in enumerate(part)
         ]
-        mixed = combine(mixed, gates, slots, returned, part[0], part is far[1])
+        mixed = combine(mixed, gates, slots, returned, part, part is far[1])
     return mixed
 
 

time: 229 us -> 224 us (0.978)
  waiting for transfers between devices: 85.9 us -> 73.6 us
  starting transfers between devices: 47.7 us -> 51.1 us
  Pallas kernels: 84.6 us -> 86.9 us
    ppermute x28 -> x29, waiting for transfers between devices: 79.7 us -> 67.3 us  [send(): return lax.ppermute(value, AXES, [(i, i ^ mask) for i in range(total)])]
    ppermute x28 -> x29, starting transfers between devices: 33.3 us -> 36.3 us  [send(): return lax.ppermute(value, AXES, [(i, i ^ mask) for i in range(total)])]
    pallas_call x1, Pallas kernels: 8.5 us -> 11 us  [cached_attention(): pl.pallas_call(functools.partial(cached_kernel, requests, span_devs, 4),...]
  transfers between devices with their start and end apart: 31 -> 32, of which waited for: 17 -> 15; matrix products, arithmetic and copies ran while one was open for 3% -> 4% of each run, Pallas kernels for 32% -> 33%
where the time goes in v4:
time: 224 us; the launch traced here: 223 us
  Pallas kernels  86.9 us (39%)
  waiting for transfers between devices  73.6 us (33%)
  starting transfers between devices  51.1 us (23%)
  other arithmetic  5.6 us (2%)
  local copies, waits for them, and re-layouts  4.31 us (2%)
    ppermute x29, waiting for transfers between devices, send(): return lax.ppermute(value, AXES, [(i, i ^ mask) for i in range(total)])  67.3 us
    pallas_call x3, Pallas kernels, expert(): pl.pallas_call(functools.partial(expert_kernel, count, max(0, len(late) -...  47.4 us
    ppermute x29, starting transfers between devices, send(): return lax.ppermute(value, AXES, [(i, i ^ mask) for i in range(total)])  36.3 us
    pallas_call x3, Pallas kernels, combine(): pl.pallas_call(functools.partial(combine_kernel, tuple(which)), out_shape...  11.5 us
    pallas_call x1, Pallas kernels, cached_attention(): pl.pallas_call(functools.partial(cached_kernel, requests, span_devs, 4),...  11 us
    pallas_call x1, Pallas kernels, self_attention(): pl.pallas_call(functools.partial(self_kernel, span_devs), out_shape=[jax....  7.76 us
    all_to_all x1, waiting for transfers between devices, body(): lax.all_to_all(parts, 'tensor', split_axis=0, concat_axis=0, tiled=True)  6.21 us
    all_to_all x1, starting transfers between devices, body(): lax.all_to_all(q, 'tensor', split_axis=0, concat_axis=0, tiled=True)  6.14 us
  transfers between devices with their start and end apart: 32, of which 15 were waited for; matrix products, arithmetic and copies ran while one was open for 4% of the time, Pallas kernels for 33%

profile of v4, /device:TPU:9, one launch (start us, length us, event | category | flops | bytes accessed | tf_op | source)
XLA Modules:
  0.0 223.0 jit_solution(14986419816776942412)
XLA Ops:
  0.0 0.8 slice_bitcast_fusion
  0.8 2.5 %collective-permute-start.1 = (bf16[64,256]{1,0:T(8,128)(2,1)S(1)}, bf16[64,256]{1,0:T(8,128)(2,1)S(1)}, u32[]{:S(2)}, u32[]{:S(2)}) collective-permute-start(bf16[64,256]{1,0:T(8,128)(2,1)S(1)} %get-tuple-element.58), channel_id=1, source_target_pairs={{0,4},{1,5},{2,6},{3,7},{4,0},{5,1},{6,2},{7,3},{8,12},{9,13},{10,... | collective-permute-start | bytes 98312 | tf_op jit(solution)/shard_map/ppermute | solution.py:45
  3.5 1.5 collective-permute-done.1
  5.0 1.6 collective-permute-done.2
  6.7 1.3 collective-permute-start.4
  8.0 1.2 collective-permute-start.5
  9.1 1.5 fusion
  10.6 0.8 slice.19
  11.5 0.3 collective-permute-start.3
  11.7 0.8 pad_maximum_fusion.8
  12.5 0.3 collective-permute-done.5
  12.8 3.5 %collective-permute-done.3 = bf16[4,64,256]{2,1,0:T(8,128)(2,1)S(1)} collective-permute-done((bf16[4,64,256]{2,1,0:T(8,128)(2,1)S(1)}, bf16[4,64,256]{2,1,0:T(8,128)(2,1)S(1)}, u32[]{:S(2)}, u32[]{:S(2)}) %collective-permute-start.3) | collective-permute-done | bytes 131104 | tf_op jit(solution)/shard_map/ppermute | solution.py:45
  16.4 2.9 %collective-permute-start.6 = (bf16[2,8,64,256]{3,2,1,0:T(8,128)(2,1)S(1)}, bf16[2,8,64,256]{3,2,1,0:T(8,128)(2,1)S(1)}, u32[]{:S(2)}, u32[]{:S(2)}) collective-permute-start(bf16[2,8,64,256]{3,2,1,0:T(8,128)(2,1)S(1)} %pad_maximum_fusion.3.even), channel_id=1, source_target_pairs={{0,8},{1,9},{2,10},{3,11},{4,12},{5,13},{6,14},{7,15},{8,0},{9,1},... | collective-permute-start | bytes 1572872 | tf_op jit(solution)/shard_map/ppermute | solution.py:45
  19.4 1.3 fusion.2.normed.refs_2_
  20.9 2.9 %project_queries.1.refs_1_ = bf16[8,64,512]{2,1,0:T(8,128)(2,1)} custom-call(s32[2]{0:T(128)S(1)} %pad_add_fusion.info.refs_0_, bf16[512,1024]{1,0:T(8,128)(2,1)} %fusion.2.normed.refs_2_, bf16[2,8,64,256]{3,2,1,0:T(8,128)(2,1)S(1)} %pad_maximum_fusion.3.even, bf16[2,8,64,256]{3,2,1,0:T(8,128)(2,1)S(1)} %collective-permute-done.6.odd), custom_call_target="tpu_custom_call" | custom-call | flops 1000000000 | bytes 2000000 | tf_op jit(solution)/shard_map/project_queries/pallas_call | solution.py:188
  23.8 3.2 %collective-permute-start.7 = (bf16[512,1024]{1,0:T(8,128)(2,1)S(1)}, bf16[512,1024]{1,0:T(8,128)(2,1)}, u32[]{:S(2)}, u32[]{:S(2)}) collective-permute-start(bf16[512,1024]{1,0:T(8,128)(2,1)S(1)} %copy-done.8), channel_id=1, source_target_pairs={{0,1},{2,3},{4,5},{6,7},{8,9},{10,11},{12,13},{14,15},{16,17},{18,... | collective-permute-start | bytes 3145736 | tf_op jit(solution)/shard_map/ppermute | solution.py:540
  26.9 6.1 %all-to-all-start = ((bf16[8,64,512]{2,1,0:T(8,128)(2,1)}), bf16[8,64,512]{2,1,0:T(8,128)(2,1)S(1)}, u32[]{:S(2)}, u32[]{:S(2)}) async-start(bf16[8,64,512]{2,1,0:T(8,128)(2,1)} %project_queries.1.refs_1_), calls=%async_computation | async-start | bytes 1048576 | tf_op jit(solution)/shard_map/all_to_all | solution.py:528
  33.1 0.2 collective-permute-start.8
  33.3 2.3 %collective-permute-start.9 = (bf16[192,256]{1,0:T(8,128)(2,1)S(1)}, bf16[192,256]{1,0:T(8,128)(2,1)}, u32[]{:S(2)}, u32[]{:S(2)}) collective-permute-start(bf16[192,256]{1,0:T(8,128)(2,1)S(1)} %pad_maximum_fusion.8), channel_id=1, source_target_pairs={{0,4},{1,5},{2,6},{3,7},{4,0},{5,1},{6,2},{7,3},{8,12},{9,13},{10,... | collective-permute-start | bytes 294920 | tf_op jit(solution)/shard_map/ppermute | solution.py:45
  35.6 0.3 collective-permute-start.10
  35.8 1.3 fusion.7
  37.2 0.4 dispatch.1
  37.6 7.0 %collective-permute-done.8 = bf16[192,256]{1,0:T(8,128)(2,1)} collective-permute-done((bf16[192,256]{1,0:T(8,128)(2,1)S(1)}, bf16[192,256]{1,0:T(8,128)(2,1)}, u32[]{:S(2)}, u32[]{:S(2)}) %collective-permute-start.8) | collective-permute-done | bytes 98336 | tf_op jit(solution)/shard_map/ppermute | solution.py:45
  44.5 6.3 %collective-permute-done.9 = bf16[192,256]{1,0:T(8,128)(2,1)} collective-permute-done((bf16[192,256]{1,0:T(8,128)(2,1)S(1)}, bf16[192,256]{1,0:T(8,128)(2,1)}, u32[]{:S(2)}, u32[]{:S(2)}) %collective-permute-start.9) | collective-permute-done | bytes 98336 | tf_op jit(solution)/shard_map/ppermute | solution.py:45
  50.8 3.6 %collective-permute-done.10 = bf16[192,256]{1,0:T(8,128)(2,1)} collective-permute-done((bf16[192,256]{1,0:T(8,128)(2,1)S(1)}, bf16[192,256]{1,0:T(8,128)(2,1)}, u32[]{:S(2)}, u32[]{:S(2)}) %collective-permute-start.10) | collective-permute-done | bytes 98336 | tf_op jit(solution)/shard_map/ppermute | solution.py:45
  54.5 1.0 pad_maximum_fusion.4
  55.6 2.1 collective-permute-start.11
  57.7 1.2 collective-permute-start.12
  59.0 11.0 %cached_attention.1.refs_6_ = bf16[8,80,512]{2,1,0:T(8,128)(2,1)} custom-call(s32[4]{0:T(128)S(1)} %copy-done.4, s32[1,128]{1,0:T(1,128)S(1)} %copy-done.5, bf16[8,64,512]{2,1,0:T(8,128)(2,1)S(1)} %all-to-all-done.q_ref, bf16[128,128,128]{2,1,0:T(8,128)(2,1)} %kv_ref.1), custom_call_target="tpu_custom_call" | custom-call | flops 8000000000 | bytes 6000000 | tf_op jit(solution)/shard_map/cached_attention/pallas_call | solution.py:152
  70.1 5.2 %collective-permute-done.13 = bf16[4,192,256]{2,1,0:T(8,128)(2,1)S(1)} collective-permute-done((bf16[4,192,256]{2,1,0:T(8,128)(2,1)S(1)}, bf16[4,192,256]{2,1,0:T(8,128)(2,1)S(1)}, u32[]{:S(2)}, u32[]{:S(2)}) %collective-permute-start.13) | collective-permute-done | bytes 393248 | tf_op jit(solution)/shard_map/ppermute | solution.py:45
  75.6 2.4 %collective-permute-start.15 = (bf16[2,8,192,256]{3,2,1,0:T(8,128)(2,1)S(1)}, bf16[2,8,192,256]{3,2,1,0:T(8,128)(2,1)}, u32[]{:S(2)}, u32[]{:S(2)}) collective-permute-start(bf16[2,8,192,256]{3,2,1,0:T(8,128)(2,1)S(1)} %pad_maximum_fusion.refs_4_), channel_id=1, source_target_pairs={{0,8},{1,9},{2,10},{3,11},{4,12},{5,13},{6,14},{7,15},{8,0},{9,1},... | collective-permute-start | bytes 4718600 | tf_op jit(solution)/shard_map/ppermute | solution.py:45
  78.1 5.4 %all-to-all-start.1 = ((bf16[8,80,512]{2,1,0:T(8,128)(2,1)}), bf16[8,80,512]{2,1,0:T(8,128)(2,1)S(1)}, u32[]{:S(2)}, u32[]{:S(2)}) async-start(bf16[8,80,512]{2,1,0:T(8,128)(2,1)} %cached_attention.1.refs_6_), calls=%async_computation.1 | async-start | bytes 1310720 | tf_op jit(solution)/shard_map/all_to_all | solution.py:565
  83.5 0.6 gather_fusion
  84.2 0.2 copy.29
  84.4 0.2 fusion.8.hits
  84.6 7.8 %self_attention.1 = (f32[8,88,512]{2,1,0:T(8,128)}, bf16[512,1024]{1,0:T(8,128)(2,1)}) custom-call(s32[2]{0:T(128)S(1)} %pad_add_fusion.info.refs_0_, bf16[8,64,512]{2,1,0:T(8,128)(2,1)} %project_queries.1.refs_1_, bf16[512,1024]{1,0:T(8,128)(2,1)} %fusion.2.normed.refs_2_, bf16[512,1024]{1,0:T(8,128)(2,1)} %collective-permute-done.7.refs_3_, ...), custom_call_target="tpu_custom_call" | custom-call | flops 4000000000 | bytes 5000000 | tf_op jit(solution)/shard_map/self_attention/pallas_call | solution.py:281
  92.4 6.2 %all-to-all-done.1.cached = bf16[8,80,512]{2,1,0:T(8,128)(2,1)S(1)} async-done(((bf16[8,80,512]{2,1,0:T(8,128)(2,1)}), bf16[8,80,512]{2,1,0:T(8,128)(2,1)S(1)}, u32[]{:S(2)}, u32[]{:S(2)}) %all-to-all-start.1) | async-done | bytes 655392 | tf_op jit(solution)/shard_map/all_to_all | solution.py:565
  98.6 0.8 copy-done.9
  99.4 6.0 %merge_and_dispatch.1 = (f32[512,1024]{1,0:T(8,128)}, f32[512,8]{1,0:T(8,128)S(1)}, bf16[512,1024]{1,0:T(8,128)(2,1)}, bf16[160,512]{1,0:T(8,128)(2,1)S(1)}, bf1...) custom-call(bf16[512,1024]{1,0:T(8,128)(2,1)} %tokens.1, ...), custom_call_target="tpu_custom_call" | custom-call | flops 4000000000 | bytes 10000000 | tf_op jit(solution)/shard_map/merge_and_dispatch/pallas_call | solution.py:369
  105.4 1.0 collective-permute-start.16
  106.4 3.2 %collective-permute-start.17 = (bf16[160,512]{1,0:T(8,128)(2,1)S(1)}, bf16[160,512]{1,0:T(8,128)(2,1)S(1)}, u32[]{:S(2)}, u32[]{:S(2)}) collective-permute-start(bf16[160,512]{1,0:T(8,128)(2,1)S(1)} %get-tuple-element.40), channel_id=1, source_target_pairs={{0,4},{1,5},{2,6},{3,7},{4,0},{5,1},{6,2},{7,3},{8,12},{9,13},{10,... | collective-permute-start | bytes 491528 | tf_op jit(solution)/shard_map/ppermute | solution.py:45
  109.6 1.1 collective-permute-start.20
  110.7 1.5 collective-permute-start.22
  112.2 14.7 %collective-permute-done.17.refs_2_ = bf16[160,512]{1,0:T(8,128)(2,1)S(1)} collective-permute-done((bf16[160,512]{1,0:T(8,128)(2,1)S(1)}, bf16[160,512]{1,0:T(8,128)(2,1)S(1)}, u32[]{:S(2)}, u32[]{:S(2)}) %collective-permute-start.17) | collective-permute-done | bytes 163872 | tf_op jit(solution)/shard_map/ppermute | solution.py:45
  127.0 2.6 %collective-permute-start.26 = (bf16[160,1024]{1,0:T(8,128)(2,1)S(1)}, bf16[160,1024]{1,0:T(8,128)(2,1)S(1)}, u32[]{:S(2)}, u32[]{:S(2)}) collective-permute-start(bf16[160,1024]{1,0:T(8,128)(2,1)S(1)} %get-tuple-element.51), channel_id=1, source_target_pairs={{0,5},{1,4},{2,7},{3,6},{4,1},{5,0},{6,3},{7,2},{8,13},{9,12},{10,... | collective-permute-start | bytes 983048 | tf_op jit(solution)/shard_map/ppermute | solution.py:45
  129.5 0.5 collective-permute-start.27
  130.1 15.0 %expert.3 = (bf16[160,1024]{1,0:T(8,128)(2,1)S(1)}, bf16[160,1024]{1,0:T(8,128)(2,1)S(1)}) custom-call(bf16[160,1024]{1,0:T(8,128)(2,1)S(1)} %collective-permute-done.14.refs_0_, bf16[160,1024]{1,0:T(8,128)(2,1)S(1)} %collective-permute-done.16.refs_1_, bf16[160,512]{1,0:T(8,128)(2,1)S(1)} %collective-permute-done.17.refs_2_, ...), custom_call_target="tpu_custom_call" | custom-call | flops 5536481280 | bytes 17301504 | tf_op jit(solution)/shard_map/expert/pallas_call | solution.py:439
  145.1 2.2 %collective-permute-start.18 = (bf16[160,1024]{1,0:T(8,128)(2,1)S(1)}, bf16[160,1024]{1,0:T(8,128)(2,1)S(1)}, u32[]{:S(2)}, u32[]{:S(2)}) collective-permute-start(bf16[160,1024]{1,0:T(8,128)(2,1)S(1)} %get-tuple-element.41.refs_7_), channel_id=1, source_target_pairs={{0,4},{1,5},{2,6},{3,7},{4,0},{5,1},{6,2},{7,3},{8,12},{9,13},{10,... | collective-permute-start | bytes 983048 | tf_op jit(solution)/shard_map/ppermute | solution.py:45
  147.4 0.7 copy-done.13
  148.2 18.3 %expert.4 = (bf16[160,1024]{1,0:T(8,128)(2,1)S(1)}, bf16[160,1024]{1,0:T(8,128)(2,1)S(1)}, bf16[160,1024]{1,0:T(8,128)(2,1)S(1)}, bf16[160,1024]{1,0:T(8,128)(2,1)S(1)}) custom-call(bf16[160,1024]{1,0:T(8,128)(2,1)S(1)} %copy-done.6, bf16[160,1024]{1,0:T(8,128)(2,1)S(1)} %collective-permute-done.20.refs_1_, bf16[160,1024]{1,0:T(8,128)(2,1)} %copy-done.13, ...), custom_call_target="tpu_custom_call" | custom-call | flops 11072962560 | bytes 17301504 | tf_op jit(solution)/shard_map/expert/pallas_call | solution.py:439
  166.5 0.5 collective-permute-start.23
  167.0 1.0 collective-permute-start.24
  168.0 1.2 collective-permute-start.25
  169.2 0.4 collective-permute-start.19
  169.6 14.1 %expert.5 = (bf16[160,1024]{1,0:T(8,128)(2,1)S(1)}, bf16[160,1024]{1,0:T(8,128)(2,1)S(1)}) custom-call(bf16[160,1024]{1,0:T(8,128)(2,1)S(1)} %collective-permute-done.26.refs_0_, bf16[160,1024]{1,0:T(8,128)(2,1)S(1)} %collective-permute-done.27.refs_1_, bf16[1,1024,5632]{2,1,0:T(8,128)(2,1)} %refs_3_.1, bf16[1,1024,5632]{2,1,0:T(8,128)(2,1)} %refs_3_.1, ...), custom_call_target="tpu_custom_call" | custom-call | flops 5536481280 | bytes 17301504 | tf_op jit(solution)/shard_map/expert/pallas_call | solution.py:439
  183.7 3.0 %collective-permute-start.28 = (bf16[160,1024]{1,0:T(8,128)(2,1)S(1)}, bf16[160,1024]{1,0:T(8,128)(2,1)S(1)}, u32[]{:S(2)}, u32[]{:S(2)}) collective-permute-start(bf16[160,1024]{1,0:T(8,128)(2,1)S(1)} %get-tuple-element.53), channel_id=1, source_target_pairs={{0,5},{1,4},{2,7},{3,6},{4,1},{5,0},{6,3},{7,2},{8,13},{9,12},{10,... | collective-permute-start | bytes 983048 | tf_op jit(solution)/shard_map/ppermute | solution.py:45
  186.6 1.3 collective-permute-start.29
  187.9 0.2 bitcast_select_fusion.refs_2_
  188.1 3.7 %combine.3.refs_0_ = f32[512,1024]{1,0:T(8,128)} custom-call(f32[512,1024]{1,0:T(8,128)} %get-tuple-element.37.refs_0_, f32[512,8]{1,0:T(8,128)S(1)} %get-tuple-element.38.refs_8_.refs_1_, s32[512,8]{1,0:T(8,128)S(1)} %bitcast_select_fusion.refs_2_, bf16[160,1024]{1,0:T(8,128)(2,1)S(1)} %collective-permute-done.18.refs_3_, ...), custom_call_target="tpu_custom_call" | custom-call | flops 335544320 | bytes 6000000 | tf_op jit(solution)/shard_map/combine/pallas_call | solution.py:485
  191.9 2.9 %collective-permute-done.25.refs_6_ = bf16[160,1024]{1,0:T(8,128)(2,1)S(1)} collective-permute-done((bf16[160,1024]{1,0:T(8,128)(2,1)S(1)}, bf16[160,1024]{1,0:T(8,128)(2,1)S(1)}, u32[]{:S(2)}, u32[]{:S(2)}) %collective-permute-start.25) | collective-permute-done | bytes 327712 | tf_op jit(solution)/shard_map/ppermute | solution.py:45
  194.8 4.4 %combine.4.refs_0_ = f32[512,1024]{1,0:T(8,128)} custom-call(f32[512,1024]{1,0:T(8,128)} %combine.3.refs_0_, f32[512,8]{1,0:T(8,128)S(1)} %get-tuple-element.38.refs_8_.refs_1_, s32[512,8]{1,0:T(8,128)S(1)} %bitcast_select_fusion.refs_2_, bf16[160,1024]{1,0:T(8,128)(2,1)S(1)} %get-tuple-element.47.refs_3_.refs_5_, ...), custom_call_target="tpu_custom_call" | custom-call | flops 671088640 | bytes 6000000 | tf_op jit(solution)/shard_map/combine/pallas_call | solution.py:485
  199.2 11.6 %collective-permute-done.28.refs_3_ = bf16[160,1024]{1,0:T(8,128)(2,1)S(1)} collective-permute-done((bf16[160,1024]{1,0:T(8,128)(2,1)S(1)}, bf16[160,1024]{1,0:T(8,128)(2,1)S(1)}, u32[]{:S(2)}, u32[]{:S(2)}) %collective-permute-start.28) | collective-permute-done | bytes 327712 | tf_op jit(solution)/shard_map/ppermute | solution.py:45
  210.8 8.8 %collective-permute-done.29.refs_4_ = bf16[160,1024]{1,0:T(8,128)(2,1)S(1)} collective-permute-done((bf16[160,1024]{1,0:T(8,128)(2,1)S(1)}, bf16[160,1024]{1,0:T(8,128)(2,1)S(1)}, u32[]{:S(2)}, u32[]{:S(2)}) %collective-permute-start.29) | collective-permute-done | bytes 327712 | tf_op jit(solution)/shard_map/ppermute | solution.py:45
  219.6 3.4 %combine.5 = bf16[512,1024]{1,0:T(8,128)(2,1)} custom-call(f32[512,1024]{1,0:T(8,128)} %combine.4.refs_0_, f32[512,8]{1,0:T(8,128)S(1)} %get-tuple-element.38.refs_8_.refs_1_, s32[512,8]{1,0:T(8,128)S(1)} %bitcast_select_fusion.refs_2_, bf16[160,1024]{1,0:T(8,128)(2,1)S(1)} %collective-permute-done.28.refs_3_, ...), custom_call_target="tpu_custom_call" | custom-call | flops 335544320 | bytes 6000000 | tf_op jit(solution)/shard_map/combine/pallas_call | solution.py:485
  (72 shorter events, 1.6 us)
Async XLA Ops:
  0.0 83.5 %copy-start = (bf16[1024,8]{0,1:T(8,128)(2,1)S(1)}, bf16[1024,8]{0,1:T(8,128)(2,1)}, u32[]{:S(2)}) copy-start(bf16[1024,8]{0,1:T(8,128)(2,1)} %param.20) | copy-start | bytes 49156
  0.8 2.8 %collective-permute-start = (bf16[64,256]{1,0:T(8,128)(2,1)S(1)}, bf16[64,256]{1,0:T(8,128)(2,1)S(1)}, u32[]{:S(2)}, u32[]{:S(2)}) collective-permute-start(bf16[64,256]{1,0:T(8,128)(2,1)S(1)} %get-tuple-element.58), channel_id=1, source_target_pairs={{0,2},{1,3},{2,0},{3,1},{4,6},{5,7},{6,4},{7,5},{8,10},{9,11},{10,... | collective-permute-start | bytes 98312 | tf_op jit(solution)/shard_map/ppermute | solution.py:45
  0.8 4.2 %collective-permute-start.1 = (bf16[64,256]{1,0:T(8,128)(2,1)S(1)}, bf16[64,256]{1,0:T(8,128)(2,1)S(1)}, u32[]{:S(2)}, u32[]{:S(2)}) collective-permute-start(bf16[64,256]{1,0:T(8,128)(2,1)S(1)} %get-tuple-element.58), channel_id=1, source_target_pairs={{0,4},{1,5},{2,6},{3,7},{4,0},{5,1},{6,2},{7,3},{8,12},{9,13},{10,... | collective-permute-start | bytes 98312 | tf_op jit(solution)/shard_map/ppermute | solution.py:45
  3.3 3.4 %collective-permute-start.2 = (bf16[64,256]{1,0:T(8,128)(2,1)S(1)}, bf16[64,256]{1,0:T(8,128)(2,1)S(1)}, u32[]{:S(2)}, u32[]{:S(2)}) collective-permute-start(bf16[64,256]{1,0:T(8,128)(2,1)S(1)} %get-tuple-element.58), channel_id=1, source_target_pairs={{0,6},{1,7},{2,4},{3,5},{4,2},{5,3},{6,0},{7,1},{8,14},{9,15},{10,... | collective-permute-start | bytes 98312 | tf_op jit(solution)/shard_map/ppermute | solution.py:45
  6.6 12.8 %copy-start.1 = (bf16[512,1024]{1,0:T(8,128)(2,1)S(1)}, bf16[512,1024]{1,0:T(8,128)(2,1)}, u32[]{:S(2)}) copy-start(bf16[512,1024]{1,0:T(8,128)(2,1)} %tokens.1) | copy-start | bytes 3145732
  6.7 12.8 %copy-start.11 = (f32[1024]{0:T(1024)S(1)}, f32[1024]{0:T(1024)}, u32[]{:S(2)}) copy-start(f32[1024]{0:T(1024)} %param.13) | copy-start | bytes 12292
  6.7 5.8 %collective-permute-start.4 = (bf16[4,64,256]{2,1,0:T(8,128)(2,1)S(1)}, bf16[4,64,256]{2,1,0:T(8,128)(2,1)S(1)}, u32[]{:S(2)}, u32[]{:S(2)}) collective-permute-start(bf16[4,64,256]{2,1,0:T(8,128)(2,1)S(1)} %get-tuple-element.56), channel_id=1, source_target_pairs={{0,16},{1,17},{2,18},{3,19},{4,20},{5,21},{6,22},{7,23},{8,24},{9,... | collective-permute-start | bytes 393224 | tf_op jit(solution)/shard_map/ppermute | solution.py:45
  8.0 4.8 %collective-permute-start.5 = (bf16[4,64,256]{2,1,0:T(8,128)(2,1)S(1)}, bf16[4,64,256]{2,1,0:T(8,128)(2,1)S(1)}, u32[]{:S(2)}, u32[]{:S(2)}) collective-permute-start(bf16[4,64,256]{2,1,0:T(8,128)(2,1)S(1)} %get-tuple-element.56), channel_id=1, source_target_pairs={{0,17},{1,16},{2,19},{3,18},{4,21},{5,20},{6,23},{7,22},{8,25},{9,... | collective-permute-start | bytes 393224 | tf_op jit(solution)/shard_map/ppermute | solution.py:45
  11.5 4.8 %collective-permute-start.3 = (bf16[4,64,256]{2,1,0:T(8,128)(2,1)S(1)}, bf16[4,64,256]{2,1,0:T(8,128)(2,1)S(1)}, u32[]{:S(2)}, u32[]{:S(2)}) collective-permute-start(bf16[4,64,256]{2,1,0:T(8,128)(2,1)S(1)} %get-tuple-element.56), channel_id=1, source_target_pairs={{0,1},{1,0},{2,3},{3,2},{4,5},{5,4},{6,7},{7,6},{8,9},{9,8},{10,11... | collective-permute-start | bytes 393224 | tf_op jit(solution)/shard_map/ppermute | solution.py:45
  16.4 4.4 %collective-permute-start.6 = (bf16[2,8,64,256]{3,2,1,0:T(8,128)(2,1)S(1)}, bf16[2,8,64,256]{3,2,1,0:T(8,128)(2,1)S(1)}, u32[]{:S(2)}, u32[]{:S(2)}) collective-permute-start(bf16[2,8,64,256]{3,2,1,0:T(8,128)(2,1)S(1)} %pad_maximum_fusion.3.even), channel_id=1, source_target_pairs={{0,8},{1,9},{2,10},{3,11},{4,12},{5,13},{6,14},{7,15},{8,0},{9,1},... | collective-permute-start | bytes 1572872 | tf_op jit(solution)/shard_map/ppermute | solution.py:45
  20.7 3.1 %copy-start.8 = (bf16[512,1024]{1,0:T(8,128)(2,1)S(1)}, bf16[512,1024]{1,0:T(8,128)(2,1)}, u32[]{:S(2)}) copy-start(bf16[512,1024]{1,0:T(8,128)(2,1)} %fusion.2.normed.refs_2_) | copy-start | bytes 3145732
  20.7 12.4 %copy-start.12 = (s32[512,2]{0,1:T(2,128)S(1)}, s32[512,2]{0,1:T(2,128)}, u32[]{:S(2)}) copy-start(s32[512,2]{0,1:T(2,128)} %param.21) | copy-start | bytes 12292
  23.8 31.8 %collective-permute-start.7 = (bf16[512,1024]{1,0:T(8,128)(2,1)S(1)}, bf16[512,1024]{1,0:T(8,128)(2,1)}, u32[]{:S(2)}, u32[]{:S(2)}) collective-permute-start(bf16[512,1024]{1,0:T(8,128)(2,1)S(1)} %copy-done.8), channel_id=1, source_target_pairs={{0,1},{2,3},{4,5},{6,7},{8,9},{10,11},{12,13},{14,15},{16,17},{18,... | collective-permute-start | bytes 3145736 | tf_op jit(solution)/shard_map/ppermute | solution.py:540
  26.9 28.6 %all-to-all-start = ((bf16[8,64,512]{2,1,0:T(8,128)(2,1)}), bf16[8,64,512]{2,1,0:T(8,128)(2,1)S(1)}, u32[]{:S(2)}, u32[]{:S(2)}) async-start(bf16[8,64,512]{2,1,0:T(8,128)(2,1)} %project_queries.1.refs_1_), calls=%async_computation | async-start | bytes 1048576 | tf_op jit(solution)/shard_map/all_to_all | solution.py:528
  33.1 11.4 %collective-permute-start.8 = (bf16[192,256]{1,0:T(8,128)(2,1)S(1)}, bf16[192,256]{1,0:T(8,128)(2,1)}, u32[]{:S(2)}, u32[]{:S(2)}) collective-permute-start(bf16[192,256]{1,0:T(8,128)(2,1)S(1)} %pad_maximum_fusion.8), channel_id=1, source_target_pairs={{0,2},{1,3},{2,0},{3,1},{4,6},{5,7},{6,4},{7,5},{8,10},{9,11},{10,... | collective-permute-start | bytes 294920 | tf_op jit(solution)/shard_map/ppermute | solution.py:45
  33.3 17.5 %collective-permute-start.9 = (bf16[192,256]{1,0:T(8,128)(2,1)S(1)}, bf16[192,256]{1,0:T(8,128)(2,1)}, u32[]{:S(2)}, u32[]{:S(2)}) collective-permute-start(bf16[192,256]{1,0:T(8,128)(2,1)S(1)} %pad_maximum_fusion.8), channel_id=1, source_target_pairs={{0,4},{1,5},{2,6},{3,7},{4,0},{5,1},{6,2},{7,3},{8,12},{9,13},{10,... | collective-permute-start | bytes 294920 | tf_op jit(solution)/shard_map/ppermute | solution.py:45
  35.6 18.9 %collective-permute-start.10 = (bf16[192,256]{1,0:T(8,128)(2,1)S(1)}, bf16[192,256]{1,0:T(8,128)(2,1)}, u32[]{:S(2)}, u32[]{:S(2)}) collective-permute-start(bf16[192,256]{1,0:T(8,128)(2,1)S(1)} %pad_maximum_fusion.8), channel_id=1, source_target_pairs={{0,6},{1,7},{2,4},{3,5},{4,2},{5,3},{6,0},{7,1},{8,14},{9,15},{10,... | collective-permute-start | bytes 294920 | tf_op jit(solution)/shard_map/ppermute | solution.py:45
  37.1 21.9 %copy-start.4 = (s32[4]{0:T(128)S(1)}, s32[4]{0:T(128)}, u32[]{:S(2)}) copy-start(s32[4]{0:T(128)} %lengths.1) | copy-start | bytes 52
  37.1 21.9 %copy-start.5 = (s32[1,128]{1,0:T(1,128)S(1)}, s32[1,128]{1,0:T(1,128)}, u32[]{:S(2)}) copy-start(s32[1,128]{1,0:T(1,128)} %table.1) | copy-start | bytes 1540
  55.5 20.1 %collective-permute-start.14 = (bf16[160,1024]{1,0:T(8,128)(2,1)S(1)}, bf16[160,1024]{1,0:T(8,128)(2,1)S(1)}, u32[]{:S(2)}, u32[]{:S(2)}) collective-permute-start(bf16[160,1024]{1,0:T(8,128)(2,1)S(1)} %dispatch.1), channel_id=1, source_target_pairs={{0,4},{1,5},{2,6},{3,7},{4,0},{5,1},{6,2},{7,3},{8,12},{9,13},{10,... | collective-permute-start | bytes 983048 | tf_op jit(solution)/shard_map/ppermute | solution.py:45
  55.6 14.4 %collective-permute-start.11 = (bf16[4,192,256]{2,1,0:T(8,128)(2,1)S(1)}, bf16[4,192,256]{2,1,0:T(8,128)(2,1)S(1)}, u32[]{:S(2)}, u32[]{:S(2)}) collective-permute-start(bf16[4,192,256]{2,1,0:T(8,128)(2,1)S(1)} %pad_maximum_fusion.4), channel_id=1, source_target_pairs={{0,1},{1,0},{2,3},{3,2},{4,5},{5,4},{6,7},{7,6},{8,9},{9,8},{10,11... | collective-permute-start | bytes 1179656 | tf_op jit(solution)/shard_map/ppermute | solution.py:45
  57.7 12.4 %collective-permute-start.12 = (bf16[4,192,256]{2,1,0:T(8,128)(2,1)S(1)}, bf16[4,192,256]{2,1,0:T(8,128)(2,1)S(1)}, u32[]{:S(2)}, u32[]{:S(2)}) collective-permute-start(bf16[4,192,256]{2,1,0:T(8,128)(2,1)S(1)} %pad_maximum_fusion.4), channel_id=1, source_target_pairs={{0,16},{1,17},{2,18},{3,19},{4,20},{5,21},{6,22},{7,23},{8,24},{9,... | collective-permute-start | bytes 1179656 | tf_op jit(solution)/shard_map/ppermute | solution.py:45
  59.0 16.3 %collective-permute-start.13 = (bf16[4,192,256]{2,1,0:T(8,128)(2,1)S(1)}, bf16[4,192,256]{2,1,0:T(8,128)(2,1)S(1)}, u32[]{:S(2)}, u32[]{:S(2)}) collective-permute-start(bf16[4,192,256]{2,1,0:T(8,128)(2,1)S(1)} %pad_maximum_fusion.4), channel_id=1, source_target_pairs={{0,17},{1,16},{2,19},{3,18},{4,21},{5,20},{6,23},{7,22},{8,25},{9,... | collective-permute-start | bytes 1179656 | tf_op jit(solution)/shard_map/ppermute | solution.py:45
  75.6 9.0 %copy-start.7 = (bf16[2,8,192,256]{3,2,1,0:T(8,128)(2,1)}, bf16[2,8,192,256]{3,2,1,0:T(8,128)(2,1)S(1)}, u32[]{:S(2)}) copy-start(bf16[2,8,192,256]{3,2,1,0:T(8,128)(2,1)S(1)} %pad_maximum_fusion.refs_4_) | copy-start | bytes 4718596
  75.6 9.0 %collective-permute-start.15 = (bf16[2,8,192,256]{3,2,1,0:T(8,128)(2,1)S(1)}, bf16[2,8,192,256]{3,2,1,0:T(8,128)(2,1)}, u32[]{:S(2)}, u32[]{:S(2)}) collective-permute-start(bf16[2,8,192,256]{3,2,1,0:T(8,128)(2,1)S(1)} %pad_maximum_fusion.refs_4_), channel_id=1, source_target_pairs={{0,8},{1,9},{2,10},{3,11},{4,12},{5,13},{6,14},{7,15},{8,0},{9,1},... | collective-permute-start | bytes 4718600 | tf_op jit(solution)/shard_map/ppermute | solution.py:45
  78.1 20.5 %all-to-all-start.1 = ((bf16[8,80,512]{2,1,0:T(8,128)(2,1)}), bf16[8,80,512]{2,1,0:T(8,128)(2,1)S(1)}, u32[]{:S(2)}, u32[]{:S(2)}) async-start(bf16[8,80,512]{2,1,0:T(8,128)(2,1)} %cached_attention.1.refs_6_), calls=%async_computation.1 | async-start | bytes 1310720 | tf_op jit(solution)/shard_map/all_to_all | solution.py:565
  84.6 14.8 %copy-start.2 = (f32[1024]{0:T(1024)S(1)}, f32[1024]{0:T(1024)}, u32[]{:S(2)}) copy-start(f32[1024]{0:T(1024)} %param.19) | copy-start | bytes 12292
  98.6 0.8 copy-start.9
  105.4 24.1 %collective-permute-start.16 = (bf16[160,1024]{1,0:T(8,128)(2,1)S(1)}, bf16[160,1024]{1,0:T(8,128)(2,1)S(1)}, u32[]{:S(2)}, u32[]{:S(2)}) collective-permute-start(bf16[160,1024]{1,0:T(8,128)(2,1)S(1)} %get-tuple-element.39), channel_id=1, source_target_pairs={{0,6},{1,7},{2,4},{3,5},{4,2},{5,3},{6,0},{7,1},{8,14},{9,15},{10,... | collective-permute-start | bytes 983048 | tf_op jit(solution)/shard_map/ppermute | solution.py:45
  106.4 20.6 %collective-permute-start.17 = (bf16[160,512]{1,0:T(8,128)(2,1)S(1)}, bf16[160,512]{1,0:T(8,128)(2,1)S(1)}, u32[]{:S(2)}, u32[]{:S(2)}) collective-permute-start(bf16[160,512]{1,0:T(8,128)(2,1)S(1)} %get-tuple-element.40), channel_id=1, source_target_pairs={{0,4},{1,5},{2,6},{3,7},{4,0},{5,1},{6,2},{7,3},{8,12},{9,13},{10,... | collective-permute-start | bytes 491528 | tf_op jit(solution)/shard_map/ppermute | solution.py:45
  109.6 35.5 %collective-permute-start.20 = (bf16[160,1024]{1,0:T(8,128)(2,1)}, bf16[160,1024]{1,0:T(8,128)(2,1)S(1)}, u32[]{:S(2)}, u32[]{:S(2)}) collective-permute-start(bf16[160,1024]{1,0:T(8,128)(2,1)} %get-tuple-element.44), channel_id=1, source_target_pairs={{0,1},{1,0},{2,3},{3,2},{4,5},{5,4},{6,7},{7,6},{8,9},{9,8},{10,11... | collective-permute-start | bytes 983048 | tf_op jit(solution)/shard_map/ppermute | solution.py:45
  110.7 36.6 %collective-permute-start.21 = (bf16[160,1024]{1,0:T(8,128)(2,1)}, bf16[160,1024]{1,0:T(8,128)(2,1)S(1)}, u32[]{:S(2)}, u32[]{:S(2)}) collective-permute-start(bf16[160,1024]{1,0:T(8,128)(2,1)} %get-tuple-element.45), channel_id=1, source_target_pairs={{0,2},{1,3},{2,0},{3,1},{4,6},{5,7},{6,4},{7,5},{8,10},{9,11},{10,... | collective-permute-start | bytes 983048 | tf_op jit(solution)/shard_map/ppermute | solution.py:45
  110.7 36.6 %collective-permute-start.22 = (bf16[160,1024]{1,0:T(8,128)(2,1)}, bf16[160,1024]{1,0:T(8,128)(2,1)S(1)}, u32[]{:S(2)}, u32[]{:S(2)}) collective-permute-start(bf16[160,1024]{1,0:T(8,128)(2,1)} %get-tuple-element.46), channel_id=1, source_target_pairs={{0,3},{1,2},{2,1},{3,0},{4,7},{5,6},{6,5},{7,4},{8,11},{9,10},{10,... | collective-permute-start | bytes 983048 | tf_op jit(solution)/shard_map/ppermute | solution.py:45
  127.0 41.1 %collective-permute-start.26 = (bf16[160,1024]{1,0:T(8,128)(2,1)S(1)}, bf16[160,1024]{1,0:T(8,128)(2,1)S(1)}, u32[]{:S(2)}, u32[]{:S(2)}) collective-permute-start(bf16[160,1024]{1,0:T(8,128)(2,1)S(1)} %get-tuple-element.51), channel_id=1, source_target_pairs={{0,5},{1,4},{2,7},{3,6},{4,1},{5,0},{6,3},{7,2},{8,13},{9,12},{10,... | collective-permute-start | bytes 983048 | tf_op jit(solution)/shard_map/ppermute | solution.py:45
  129.5 39.7 %collective-permute-start.27 = (bf16[160,1024]{1,0:T(8,128)(2,1)S(1)}, bf16[160,1024]{1,0:T(8,128)(2,1)S(1)}, u32[]{:S(2)}, u32[]{:S(2)}) collective-permute-start(bf16[160,1024]{1,0:T(8,128)(2,1)S(1)} %get-tuple-element.52), channel_id=1, source_target_pairs={{0,7},{1,6},{2,5},{3,4},{4,3},{5,2},{6,1},{7,0},{8,15},{9,14},{10,... | collective-permute-start | bytes 983048 | tf_op jit(solution)/shard_map/ppermute | solution.py:45
  130.1 18.1 %copy-start.6 = (bf16[160,1024]{1,0:T(8,128)(2,1)S(1)}, bf16[160,1024]{1,0:T(8,128)(2,1)}, u32[]{:S(2)}) copy-start(bf16[160,1024]{1,0:T(8,128)(2,1)} %get-tuple-element.43.refs_0_) | copy-start | bytes 983044
  145.1 2.3 %copy-start.3 = (bf16[160,1024]{1,0:T(8,128)(2,1)}, bf16[160,1024]{1,0:T(8,128)(2,1)S(1)}, u32[]{:S(2)}) copy-start(bf16[160,1024]{1,0:T(8,128)(2,1)S(1)} %get-tuple-element.41.refs_7_) | copy-start | bytes 983044
  145.1 38.6 %collective-permute-start.18 = (bf16[160,1024]{1,0:T(8,128)(2,1)S(1)}, bf16[160,1024]{1,0:T(8,128)(2,1)S(1)}, u32[]{:S(2)}, u32[]{:S(2)}) collective-permute-start(bf16[160,1024]{1,0:T(8,128)(2,1)S(1)} %get-tuple-element.41.refs_7_), channel_id=1, source_target_pairs={{0,4},{1,5},{2,6},{3,7},{4,0},{5,1},{6,2},{7,3},{8,12},{9,13},{10,... | collective-permute-start | bytes 983048 | tf_op jit(solution)/shard_map/ppermute | solution.py:45
  147.3 0.7 copy-start.13
  147.3 0.8 copy-start.14
  166.5 25.4 %collective-permute-start.23 = (bf16[160,1024]{1,0:T(8,128)(2,1)S(1)}, bf16[160,1024]{1,0:T(8,128)(2,1)S(1)}, u32[]{:S(2)}, u32[]{:S(2)}) collective-permute-start(bf16[160,1024]{1,0:T(8,128)(2,1)S(1)} %get-tuple-element.48), channel_id=1, source_target_pairs={{0,1},{1,0},{2,3},{3,2},{4,5},{5,4},{6,7},{7,6},{8,9},{9,8},{10,11... | collective-permute-start | bytes 983048 | tf_op jit(solution)/shard_map/ppermute | solution.py:45
  167.0 24.9 %collective-permute-start.24 = (bf16[160,1024]{1,0:T(8,128)(2,1)S(1)}, bf16[160,1024]{1,0:T(8,128)(2,1)S(1)}, u32[]{:S(2)}, u32[]{:S(2)}) collective-permute-start(bf16[160,1024]{1,0:T(8,128)(2,1)S(1)} %get-tuple-element.49), channel_id=1, source_target_pairs={{0,2},{1,3},{2,0},{3,1},{4,6},{5,7},{6,4},{7,5},{8,10},{9,11},{10,... | collective-permute-start | bytes 983048 | tf_op jit(solution)/shard_map/ppermute | solution.py:45
  168.0 26.8 %collective-permute-start.25 = (bf16[160,1024]{1,0:T(8,128)(2,1)S(1)}, bf16[160,1024]{1,0:T(8,128)(2,1)S(1)}, u32[]{:S(2)}, u32[]{:S(2)}) collective-permute-start(bf16[160,1024]{1,0:T(8,128)(2,1)S(1)} %get-tuple-element.50), channel_id=1, source_target_pairs={{0,3},{1,2},{2,1},{3,0},{4,7},{5,6},{6,5},{7,4},{8,11},{9,10},{10,... | collective-permute-start | bytes 983048 | tf_op jit(solution)/shard_map/ppermute | solution.py:45
  169.2 17.4 %collective-permute-start.19 = (bf16[160,1024]{1,0:T(8,128)(2,1)S(1)}, bf16[160,1024]{1,0:T(8,128)(2,1)S(1)}, u32[]{:S(2)}, u32[]{:S(2)}) collective-permute-start(bf16[160,1024]{1,0:T(8,128)(2,1)S(1)} %get-tuple-element.42), channel_id=1, source_target_pairs={{0,6},{1,7},{2,4},{3,5},{4,2},{5,3},{6,0},{7,1},{8,14},{9,15},{10,... | collective-permute-start | bytes 983048 | tf_op jit(solution)/shard_map/ppermute | solution.py:45
  169.6 18.3 %copy-start.10 = (s32[8,512]{0,1:T(8,128)S(1)}, s32[8,512]{0,1:T(8,128)}, u32[]{:S(2)}) copy-start(s32[8,512]{0,1:T(8,128)} %get-tuple-element.62) | copy-start | bytes 49156
  183.7 27.1 %collective-permute-start.28 = (bf16[160,1024]{1,0:T(8,128)(2,1)S(1)}, bf16[160,1024]{1,0:T(8,128)(2,1)S(1)}, u32[]{:S(2)}, u32[]{:S(2)}) collective-permute-start(bf16[160,1024]{1,0:T(8,128)(2,1)S(1)} %get-tuple-element.53), channel_id=1, source_target_pairs={{0,5},{1,4},{2,7},{3,6},{4,1},{5,0},{6,3},{7,2},{8,13},{9,12},{10,... | collective-permute-start | bytes 983048 | tf_op jit(solution)/shard_map/ppermute | solution.py:45
  186.6 33.0 %collective-permute-start.29 = (bf16[160,1024]{1,0:T(8,128)(2,1)S(1)}, bf16[160,1024]{1,0:T(8,128)(2,1)S(1)}, u32[]{:S(2)}, u32[]{:S(2)}) collective-permute-start(bf16[160,1024]{1,0:T(8,128)(2,1)S(1)} %get-tuple-element.54), channel_id=1, source_target_pairs={{0,7},{1,6},{2,5},{3,4},{4,3},{5,2},{6,1},{7,0},{8,15},{9,14},{10,... | collective-permute-start | bytes 983048 | tf_op jit(solution)/shard_map/ppermute | solution.py:45

commit v5 on v4

--- a/solution.py
+++ b/solution.py
@@ -161,7 +161,7 @@
         ],
         compiler_params=params(),
         cost_estimate=pl.CostEstimate(
-            flops=8 * 10**9, bytes_accessed=6 * 10**6, transcendentals=8 * 10**6
+            flops=24 * 10**9, bytes_accessed=6 * 10**6, transcendentals=8 * 10**6
         ),
         name="cached_attention",
     )(lengths, table, q, kv_cache)
@@ -529,7 +529,7 @@
 
     near = [normed]
     rest = jnp.concatenate([w_t[HD : 3 * HD], w_attn_out.T], axis=0)
-    ready, rest = lax.optimization_barrier((normed, rest, q))[:2]
+    ready, rest = after(normed, q_plane), after(rest, q)
     for i in range(1, span_devs):
         pairs = [
             (b * lanes + t, b * lanes + (t ^ i))
@@ -539,7 +539,7 @@
         ]
         near.append(lax.ppermute(ready, AXES, pairs))
     rest = gather_high(rest, lanes, groups)
-    rest = gather_plane(after(rest, *near[1:]), lanes, groups)
+    rest = gather_plane(after(rest, q_here, *near[1:]), lanes, groups)
 
     names = me ^ jnp.arange(lanes, dtype=jnp.int32)
     hit_rows = (routes[:, 0][None, :] == names[:, None]) | (routes[:, 1][None, :] == names[:, None])

time: 224 us -> 219 us (0.978)
  Pallas kernels: 86.9 us -> 84.4 us
    pallas_call x1, Pallas kernels: 11 us -> 8.5 us  [cached_attention(): pl.pallas_call(functools.partial(cached_kernel, requests, span_devs, 4),...]
  transfers between devices with their start and end apart: 32 -> 32, of which waited for: 15 -> 14; matrix products, arithmetic and copies ran while one was open for 4% -> 3% of each run, Pallas kernels for 33% -> 34%
where the time goes in v5:
time: 219 us; the launch traced here: 218 us
  Pallas kernels  84.4 us (39%)
  waiting for transfers between devices  74.8 us (34%)
  starting transfers between devices  50.2 us (23%)
  other arithmetic  3.87 us (2%)
  local copies, waits for them, and re-layouts  3.47 us (2%)
    ppermute x29, waiting for transfers between devices, send(): return lax.ppermute(value, AXES, [(i, i ^ mask) for i in range(total)])  68.6 us
    pallas_call x3, Pallas kernels, expert(): pl.pallas_call(functools.partial(expert_kernel, count, max(0, len(late) -...  47.4 us
    ppermute x29, starting transfers between devices, send(): return lax.ppermute(value, AXES, [(i, i ^ mask) for i in range(total)])  35.9 us
    pallas_call x3, Pallas kernels, combine(): pl.pallas_call(functools.partial(combine_kernel, tuple(which)), out_shape...  11.6 us
    pallas_call x1, Pallas kernels, cached_attention(): pl.pallas_call(functools.partial(cached_kernel, requests, span_devs, 4),...  8.5 us
    pallas_call x1, Pallas kernels, self_attention(): pl.pallas_call(functools.partial(self_kernel, span_devs), out_shape=[jax....  7.78 us
    all_to_all x1, waiting for transfers between devices, body(): lax.all_to_all(parts, 'tensor', split_axis=0, concat_axis=0, tiled=True)  6.2 us
    all_to_all x1, starting transfers between devices, body(): lax.all_to_all(q, 'tensor', split_axis=0, concat_axis=0, tiled=True)  6.11 us
  transfers between devices with their start and end apart: 32, of which 14 were waited for; matrix products, arithmetic and copies ran while one was open for 3% of the time, Pallas kernels for 34%

profile of v5, /device:TPU:9, one launch (start us, length us, event | category | flops | bytes accessed | tf_op | source)
XLA Modules:
  0.0 218.4 jit_solution(9188825677842622816)
XLA Ops:
  0.0 0.8 slice_bitcast_fusion
  0.8 2.5 %collective-permute-start.1 = (bf16[64,256]{1,0:T(8,128)(2,1)S(1)}, bf16[64,256]{1,0:T(8,128)(2,1)S(1)}, u32[]{:S(2)}, u32[]{:S(2)}) collective-permute-start(bf16[64,256]{1,0:T(8,128)(2,1)S(1)} %get-tuple-element.58), channel_id=1, source_target_pairs={{0,4},{1,5},{2,6},{3,7},{4,0},{5,1},{6,2},{7,3},{8,12},{9,13},{10,... | collective-permute-start | bytes 98312 | tf_op jit(solution)/shard_map/ppermute | solution.py:45
  3.3 0.2 collective-permute-start.2
  3.5 1.5 collective-permute-done.1
  5.0 1.6 collective-permute-done.2
  6.7 1.3 collective-permute-start.4
  8.0 1.2 collective-permute-start.5
  9.1 0.3 collective-permute-start.3
  9.4 1.5 fusion
  10.9 1.9 collective-permute-done.5
  12.8 0.6 collective-permute-done.3
  13.6 3.4 %collective-permute-start.6 = (bf16[2,8,64,256]{3,2,1,0:T(8,128)(2,1)S(1)}, bf16[2,8,64,256]{3,2,1,0:T(8,128)(2,1)S(1)}, u32[]{:S(2)}, u32[]{:S(2)}) collective-permute-start(bf16[2,8,64,256]{3,2,1,0:T(8,128)(2,1)S(1)} %pad_maximum_fusion.3.even), channel_id=1, source_target_pairs={{0,8},{1,9},{2,10},{3,11},{4,12},{5,13},{6,14},{7,15},{8,0},{9,1},... | collective-permute-start | bytes 1572872 | tf_op jit(solution)/shard_map/ppermute | solution.py:45
  17.0 0.3 fusion.2.normed.refs_2_
  17.3 4.1 %collective-permute-start.7 = (bf16[512,1024]{1,0:T(8,128)(2,1)S(1)}, bf16[512,1024]{1,0:T(8,128)(2,1)}, u32[]{:S(2)}, u32[]{:S(2)}) collective-permute-start(bf16[512,1024]{1,0:T(8,128)(2,1)S(1)} %fusion.2.normed.refs_2_), channel_id=1, source_target_pairs={{0,1},{2,3},{4,5},{6,7},{8,9},{10,11},{12,13},{14,15},{16,17},{18,... | collective-permute-start | bytes 3145736 | tf_op jit(solution)/shard_map/ppermute | solution.py:540
  21.5 2.9 %project_queries.1.refs_1_ = bf16[8,64,512]{2,1,0:T(8,128)(2,1)} custom-call(s32[2]{0:T(128)S(1)} %pad_add_fusion.info.refs_0_, bf16[512,1024]{1,0:T(8,128)(2,1)} %copy-done.8, bf16[2,8,64,256]{3,2,1,0:T(8,128)(2,1)S(1)} %pad_maximum_fusion.3.even, bf16[2,8,64,256]{3,2,1,0:T(8,128)(2,1)S(1)} %collective-permute-done.6.odd), custom_call_target="tpu_custom_call" | custom-call | flops 1000000000 | bytes 2000000 | tf_op jit(solution)/shard_map/project_queries/pallas_call | solution.py:188
  24.4 6.1 %all-to-all-start = ((bf16[8,64,512]{2,1,0:T(8,128)(2,1)}), bf16[8,64,512]{2,1,0:T(8,128)(2,1)S(1)}, u32[]{:S(2)}, u32[]{:S(2)}) async-start(bf16[8,64,512]{2,1,0:T(8,128)(2,1)} %project_queries.1.refs_1_), calls=%async_computation | async-start | bytes 1048576 | tf_op jit(solution)/shard_map/all_to_all | solution.py:528
  30.6 0.2 collective-permute-start.8
  30.8 2.3 %collective-permute-start.9 = (bf16[192,256]{1,0:T(8,128)(2,1)S(1)}, bf16[192,256]{1,0:T(8,128)(2,1)}, u32[]{:S(2)}, u32[]{:S(2)}) collective-permute-start(bf16[192,256]{1,0:T(8,128)(2,1)S(1)} %pad_maximum_fusion.8), channel_id=1, source_target_pairs={{0,4},{1,5},{2,6},{3,7},{4,0},{5,1},{6,2},{7,3},{8,12},{9,13},{10,... | collective-permute-start | bytes 294920 | tf_op jit(solution)/shard_map/ppermute | solution.py:45
  33.0 0.3 collective-permute-start.10
  33.3 1.3 fusion.7
  34.7 0.3 dispatch.1
  35.0 7.2 %collective-permute-done.8 = bf16[192,256]{1,0:T(8,128)(2,1)} collective-permute-done((bf16[192,256]{1,0:T(8,128)(2,1)S(1)}, bf16[192,256]{1,0:T(8,128)(2,1)}, u32[]{:S(2)}, u32[]{:S(2)}) %collective-permute-start.8) | collective-permute-done | bytes 98336 | tf_op jit(solution)/shard_map/ppermute | solution.py:45
  42.3 6.2 %collective-permute-done.9 = bf16[192,256]{1,0:T(8,128)(2,1)} collective-permute-done((bf16[192,256]{1,0:T(8,128)(2,1)S(1)}, bf16[192,256]{1,0:T(8,128)(2,1)}, u32[]{:S(2)}, u32[]{:S(2)}) %collective-permute-start.9) | collective-permute-done | bytes 98336 | tf_op jit(solution)/shard_map/ppermute | solution.py:45
  48.5 3.7 %collective-permute-done.10 = bf16[192,256]{1,0:T(8,128)(2,1)} collective-permute-done((bf16[192,256]{1,0:T(8,128)(2,1)S(1)}, bf16[192,256]{1,0:T(8,128)(2,1)}, u32[]{:S(2)}, u32[]{:S(2)}) %collective-permute-start.10) | collective-permute-done | bytes 98336 | tf_op jit(solution)/shard_map/ppermute | solution.py:45
  52.2 1.0 pad_maximum_fusion.4
  53.2 1.3 collective-permute-start.11
  54.5 1.2 collective-permute-start.12
  55.7 0.2 collective-permute-start.13
  56.0 8.5 %cached_attention.1.refs_6_ = bf16[8,80,512]{2,1,0:T(8,128)(2,1)} custom-call(s32[4]{0:T(128)S(1)} %copy-done.4, s32[1,128]{1,0:T(1,128)S(1)} %copy-done.5, bf16[8,64,512]{2,1,0:T(8,128)(2,1)S(1)} %all-to-all-done.q_ref, bf16[128,128,128]{2,1,0:T(8,128)(2,1)} %kv_ref.1), custom_call_target="tpu_custom_call" | custom-call | flops 24000000000 | bytes 6000000 | tf_op jit(solution)/shard_map/cached_attention/pallas_call | solution.py:152
  64.6 7.6 %collective-permute-done.13 = bf16[4,192,256]{2,1,0:T(8,128)(2,1)S(1)} collective-permute-done((bf16[4,192,256]{2,1,0:T(8,128)(2,1)S(1)}, bf16[4,192,256]{2,1,0:T(8,128)(2,1)S(1)}, u32[]{:S(2)}, u32[]{:S(2)}) %collective-permute-start.13) | collective-permute-done | bytes 393248 | tf_op jit(solution)/shard_map/ppermute | solution.py:45
  72.5 2.3 %collective-permute-start.15 = (bf16[2,8,192,256]{3,2,1,0:T(8,128)(2,1)S(1)}, bf16[2,8,192,256]{3,2,1,0:T(8,128)(2,1)}, u32[]{:S(2)}, u32[]{:S(2)}) collective-permute-start(bf16[2,8,192,256]{3,2,1,0:T(8,128)(2,1)S(1)} %pad_maximum_fusion.refs_4_), channel_id=1, source_target_pairs={{0,8},{1,9},{2,10},{3,11},{4,12},{5,13},{6,14},{7,15},{8,0},{9,1},... | collective-permute-start | bytes 4718600 | tf_op jit(solution)/shard_map/ppermute | solution.py:45
  74.8 4.0 %all-to-all-start.1 = ((bf16[8,80,512]{2,1,0:T(8,128)(2,1)}), bf16[8,80,512]{2,1,0:T(8,128)(2,1)S(1)}, u32[]{:S(2)}, u32[]{:S(2)}) async-start(bf16[8,80,512]{2,1,0:T(8,128)(2,1)} %cached_attention.1.refs_6_), calls=%async_computation.1 | async-start | bytes 1310720 | tf_op jit(solution)/shard_map/all_to_all | solution.py:565
  78.9 0.6 gather_fusion
  79.6 0.2 copy.29
  79.7 0.2 fusion.8.hits
  80.0 7.8 %self_attention.1 = (f32[8,88,512]{2,1,0:T(8,128)}, bf16[512,1024]{1,0:T(8,128)(2,1)}) custom-call(s32[2]{0:T(128)S(1)} %pad_add_fusion.info.refs_0_, bf16[8,64,512]{2,1,0:T(8,128)(2,1)} %project_queries.1.refs_1_, bf16[512,1024]{1,0:T(8,128)(2,1)} %copy-done.8, bf16[512,1024]{1,0:T(8,128)(2,1)} %collective-permute-done.7.refs_3_, ...), custom_call_target="tpu_custom_call" | custom-call | flops 4000000000 | bytes 5000000 | tf_op jit(solution)/shard_map/self_attention/pallas_call | solution.py:281
  87.8 6.2 %all-to-all-done.1.cached = bf16[8,80,512]{2,1,0:T(8,128)(2,1)S(1)} async-done(((bf16[8,80,512]{2,1,0:T(8,128)(2,1)}), bf16[8,80,512]{2,1,0:T(8,128)(2,1)S(1)}, u32[]{:S(2)}, u32[]{:S(2)}) %all-to-all-start.1) | async-done | bytes 655392 | tf_op jit(solution)/shard_map/all_to_all | solution.py:565
  94.0 0.8 copy-done.9
  94.8 6.0 %merge_and_dispatch.1 = (f32[512,1024]{1,0:T(8,128)}, f32[512,8]{1,0:T(8,128)S(1)}, bf16[512,1024]{1,0:T(8,128)(2,1)}, bf16[160,512]{1,0:T(8,128)(2,1)S(1)}, bf1...) custom-call(bf16[512,1024]{1,0:T(8,128)(2,1)} %tokens.1, ...), custom_call_target="tpu_custom_call" | custom-call | flops 4000000000 | bytes 10000000 | tf_op jit(solution)/shard_map/merge_and_dispatch/pallas_call | solution.py:369
  100.8 1.0 collective-permute-start.16
  101.8 3.2 %collective-permute-start.17 = (bf16[160,512]{1,0:T(8,128)(2,1)S(1)}, bf16[160,512]{1,0:T(8,128)(2,1)S(1)}, u32[]{:S(2)}, u32[]{:S(2)}) collective-permute-start(bf16[160,512]{1,0:T(8,128)(2,1)S(1)} %get-tuple-element.40), channel_id=1, source_target_pairs={{0,4},{1,5},{2,6},{3,7},{4,0},{5,1},{6,2},{7,3},{8,12},{9,13},{10,... | collective-permute-start | bytes 491528 | tf_op jit(solution)/shard_map/ppermute | solution.py:45
  104.9 1.1 collective-permute-start.20
  106.1 1.5 collective-permute-start.22
  107.6 14.7 %collective-permute-done.17.refs_2_ = bf16[160,512]{1,0:T(8,128)(2,1)S(1)} collective-permute-done((bf16[160,512]{1,0:T(8,128)(2,1)S(1)}, bf16[160,512]{1,0:T(8,128)(2,1)S(1)}, u32[]{:S(2)}, u32[]{:S(2)}) %collective-permute-start.17) | collective-permute-done | bytes 163872 | tf_op jit(solution)/shard_map/ppermute | solution.py:45
  122.3 2.6 %collective-permute-start.26 = (bf16[160,1024]{1,0:T(8,128)(2,1)S(1)}, bf16[160,1024]{1,0:T(8,128)(2,1)S(1)}, u32[]{:S(2)}, u32[]{:S(2)}) collective-permute-start(bf16[160,1024]{1,0:T(8,128)(2,1)S(1)} %get-tuple-element.51), channel_id=1, source_target_pairs={{0,5},{1,4},{2,7},{3,6},{4,1},{5,0},{6,3},{7,2},{8,13},{9,12},{10,... | collective-permute-start | bytes 983048 | tf_op jit(solution)/shard_map/ppermute | solution.py:45
  124.9 0.5 collective-permute-start.27
  125.4 15.0 %expert.3 = (bf16[160,1024]{1,0:T(8,128)(2,1)S(1)}, bf16[160,1024]{1,0:T(8,128)(2,1)S(1)}) custom-call(bf16[160,1024]{1,0:T(8,128)(2,1)S(1)} %collective-permute-done.14.refs_0_, bf16[160,1024]{1,0:T(8,128)(2,1)S(1)} %collective-permute-done.16.refs_1_, bf16[160,512]{1,0:T(8,128)(2,1)S(1)} %collective-permute-done.17.refs_2_, ...), custom_call_target="tpu_custom_call" | custom-call | flops 5536481280 | bytes 17301504 | tf_op jit(solution)/shard_map/expert/pallas_call | solution.py:439
  140.5 2.2 %collective-permute-start.18 = (bf16[160,1024]{1,0:T(8,128)(2,1)S(1)}, bf16[160,1024]{1,0:T(8,128)(2,1)S(1)}, u32[]{:S(2)}, u32[]{:S(2)}) collective-permute-start(bf16[160,1024]{1,0:T(8,128)(2,1)S(1)} %get-tuple-element.41.refs_7_), channel_id=1, source_target_pairs={{0,4},{1,5},{2,6},{3,7},{4,0},{5,1},{6,2},{7,3},{8,12},{9,13},{10,... | collective-permute-start | bytes 983048 | tf_op jit(solution)/shard_map/ppermute | solution.py:45
  142.7 0.7 copy-done.15
  143.5 18.3 %expert.4 = (bf16[160,1024]{1,0:T(8,128)(2,1)S(1)}, bf16[160,1024]{1,0:T(8,128)(2,1)S(1)}, bf16[160,1024]{1,0:T(8,128)(2,1)S(1)}, bf16[160,1024]{1,0:T(8,128)(2,1)S(1)}) custom-call(bf16[160,1024]{1,0:T(8,128)(2,1)S(1)} %copy-done.6, bf16[160,1024]{1,0:T(8,128)(2,1)S(1)} %collective-permute-done.20.refs_1_, bf16[160,1024]{1,0:T(8,128)(2,1)} %copy-done.15, ...), custom_call_target="tpu_custom_call" | custom-call | flops 11072962560 | bytes 17301504 | tf_op jit(solution)/shard_map/expert/pallas_call | solution.py:439
  161.9 0.5 collective-permute-start.23
  162.4 1.0 collective-permute-start.24
  163.4 1.2 collective-permute-start.25
  164.6 0.4 collective-permute-start.19
  165.0 14.1 %expert.5 = (bf16[160,1024]{1,0:T(8,128)(2,1)S(1)}, bf16[160,1024]{1,0:T(8,128)(2,1)S(1)}) custom-call(bf16[160,1024]{1,0:T(8,128)(2,1)S(1)} %collective-permute-done.26.refs_0_, bf16[160,1024]{1,0:T(8,128)(2,1)S(1)} %collective-permute-done.27.refs_1_, bf16[1,1024,5632]{2,1,0:T(8,128)(2,1)} %refs_3_.1, bf16[1,1024,5632]{2,1,0:T(8,128)(2,1)} %refs_3_.1, ...), custom_call_target="tpu_custom_call" | custom-call | flops 5536481280 | bytes 17301504 | tf_op jit(solution)/shard_map/expert/pallas_call | solution.py:439
  179.0 3.0 %collective-permute-start.28 = (bf16[160,1024]{1,0:T(8,128)(2,1)S(1)}, bf16[160,1024]{1,0:T(8,128)(2,1)S(1)}, u32[]{:S(2)}, u32[]{:S(2)}) collective-permute-start(bf16[160,1024]{1,0:T(8,128)(2,1)S(1)} %get-tuple-element.53), channel_id=1, source_target_pairs={{0,5},{1,4},{2,7},{3,6},{4,1},{5,0},{6,3},{7,2},{8,13},{9,12},{10,... | collective-permute-start | bytes 983048 | tf_op jit(solution)/shard_map/ppermute | solution.py:45
  182.0 1.3 collective-permute-start.29
  183.3 0.2 bitcast_select_fusion.refs_2_
  183.5 3.8 %combine.3.refs_0_ = f32[512,1024]{1,0:T(8,128)} custom-call(f32[512,1024]{1,0:T(8,128)} %get-tuple-element.37.refs_0_, f32[512,8]{1,0:T(8,128)S(1)} %get-tuple-element.38.refs_8_.refs_1_, s32[512,8]{1,0:T(8,128)S(1)} %bitcast_select_fusion.refs_2_, bf16[160,1024]{1,0:T(8,128)(2,1)S(1)} %collective-permute-done.18.refs_3_, ...), custom_call_target="tpu_custom_call" | custom-call | flops 335544320 | bytes 6000000 | tf_op jit(solution)/shard_map/combine/pallas_call | solution.py:485
  187.2 2.9 %collective-permute-done.25.refs_6_ = bf16[160,1024]{1,0:T(8,128)(2,1)S(1)} collective-permute-done((bf16[160,1024]{1,0:T(8,128)(2,1)S(1)}, bf16[160,1024]{1,0:T(8,128)(2,1)S(1)}, u32[]{:S(2)}, u32[]{:S(2)}) %collective-permute-start.25) | collective-permute-done | bytes 327712 | tf_op jit(solution)/shard_map/ppermute | solution.py:45
  190.2 4.4 %combine.4.refs_0_ = f32[512,1024]{1,0:T(8,128)} custom-call(f32[512,1024]{1,0:T(8,128)} %combine.3.refs_0_, f32[512,8]{1,0:T(8,128)S(1)} %get-tuple-element.38.refs_8_.refs_1_, s32[512,8]{1,0:T(8,128)S(1)} %bitcast_select_fusion.refs_2_, bf16[160,1024]{1,0:T(8,128)(2,1)S(1)} %get-tuple-element.47.refs_3_.refs_5_, ...), custom_call_target="tpu_custom_call" | custom-call | flops 671088640 | bytes 6000000 | tf_op jit(solution)/shard_map/combine/pallas_call | solution.py:485
  194.6 11.6 %collective-permute-done.28.refs_3_ = bf16[160,1024]{1,0:T(8,128)(2,1)S(1)} collective-permute-done((bf16[160,1024]{1,0:T(8,128)(2,1)S(1)}, bf16[160,1024]{1,0:T(8,128)(2,1)S(1)}, u32[]{:S(2)}, u32[]{:S(2)}) %collective-permute-start.28) | collective-permute-done | bytes 327712 | tf_op jit(solution)/shard_map/ppermute | solution.py:45
  206.1 8.8 %collective-permute-done.29.refs_4_ = bf16[160,1024]{1,0:T(8,128)(2,1)S(1)} collective-permute-done((bf16[160,1024]{1,0:T(8,128)(2,1)S(1)}, bf16[160,1024]{1,0:T(8,128)(2,1)S(1)}, u32[]{:S(2)}, u32[]{:S(2)}) %collective-permute-start.29) | collective-permute-done | bytes 327712 | tf_op jit(solution)/shard_map/ppermute | solution.py:45
  215.0 3.4 %combine.5 = bf16[512,1024]{1,0:T(8,128)(2,1)} custom-call(f32[512,1024]{1,0:T(8,128)} %combine.4.refs_0_, f32[512,8]{1,0:T(8,128)S(1)} %get-tuple-element.38.refs_8_.refs_1_, s32[512,8]{1,0:T(8,128)S(1)} %bitcast_select_fusion.refs_2_, bf16[160,1024]{1,0:T(8,128)(2,1)S(1)} %collective-permute-done.28.refs_3_, ...), custom_call_target="tpu_custom_call" | custom-call | flops 335544320 | bytes 6000000 | tf_op jit(solution)/shard_map/combine/pallas_call | solution.py:485
  (76 shorter events, 1.2 us)
Async XLA Ops:
  0.0 78.9 %copy-start = (bf16[1024,8]{0,1:T(8,128)(2,1)S(1)}, bf16[1024,8]{0,1:T(8,128)(2,1)}, u32[]{:S(2)}) copy-start(bf16[1024,8]{0,1:T(8,128)(2,1)} %param.20) | copy-start | bytes 49156
  0.8 2.8 %collective-permute-start = (bf16[64,256]{1,0:T(8,128)(2,1)S(1)}, bf16[64,256]{1,0:T(8,128)(2,1)S(1)}, u32[]{:S(2)}, u32[]{:S(2)}) collective-permute-start(bf16[64,256]{1,0:T(8,128)(2,1)S(1)} %get-tuple-element.58), channel_id=1, source_target_pairs={{0,2},{1,3},{2,0},{3,1},{4,6},{5,7},{6,4},{7,5},{8,10},{9,11},{10,... | collective-permute-start | bytes 98312 | tf_op jit(solution)/shard_map/ppermute | solution.py:45
  0.8 4.2 %collective-permute-start.1 = (bf16[64,256]{1,0:T(8,128)(2,1)S(1)}, bf16[64,256]{1,0:T(8,128)(2,1)S(1)}, u32[]{:S(2)}, u32[]{:S(2)}) collective-permute-start(bf16[64,256]{1,0:T(8,128)(2,1)S(1)} %get-tuple-element.58), channel_id=1, source_target_pairs={{0,4},{1,5},{2,6},{3,7},{4,0},{5,1},{6,2},{7,3},{8,12},{9,13},{10,... | collective-permute-start | bytes 98312 | tf_op jit(solution)/shard_map/ppermute | solution.py:45
  3.3 3.4 %collective-permute-start.2 = (bf16[64,256]{1,0:T(8,128)(2,1)S(1)}, bf16[64,256]{1,0:T(8,128)(2,1)S(1)}, u32[]{:S(2)}, u32[]{:S(2)}) collective-permute-start(bf16[64,256]{1,0:T(8,128)(2,1)S(1)} %get-tuple-element.58), channel_id=1, source_target_pairs={{0,6},{1,7},{2,4},{3,5},{4,2},{5,3},{6,0},{7,1},{8,14},{9,15},{10,... | collective-permute-start | bytes 98312 | tf_op jit(solution)/shard_map/ppermute | solution.py:45
  6.6 10.3 %copy-start.1 = (bf16[512,1024]{1,0:T(8,128)(2,1)S(1)}, bf16[512,1024]{1,0:T(8,128)(2,1)}, u32[]{:S(2)}) copy-start(bf16[512,1024]{1,0:T(8,128)(2,1)} %tokens.1) | copy-start | bytes 3145732
  6.7 10.3 %copy-start.13 = (f32[1024]{0:T(1024)S(1)}, f32[1024]{0:T(1024)}, u32[]{:S(2)}) copy-start(f32[1024]{0:T(1024)} %param.13) | copy-start | bytes 12292
  6.7 4.2 %collective-permute-start.4 = (bf16[4,64,256]{2,1,0:T(8,128)(2,1)S(1)}, bf16[4,64,256]{2,1,0:T(8,128)(2,1)S(1)}, u32[]{:S(2)}, u32[]{:S(2)}) collective-permute-start(bf16[4,64,256]{2,1,0:T(8,128)(2,1)S(1)} %get-tuple-element.56), channel_id=1, source_target_pairs={{0,16},{1,17},{2,18},{3,19},{4,20},{5,21},{6,22},{7,23},{8,24},{9,... | collective-permute-start | bytes 393224 | tf_op jit(solution)/shard_map/ppermute | solution.py:45
  8.0 4.8 %collective-permute-start.5 = (bf16[4,64,256]{2,1,0:T(8,128)(2,1)S(1)}, bf16[4,64,256]{2,1,0:T(8,128)(2,1)S(1)}, u32[]{:S(2)}, u32[]{:S(2)}) collective-permute-start(bf16[4,64,256]{2,1,0:T(8,128)(2,1)S(1)} %get-tuple-element.56), channel_id=1, source_target_pairs={{0,17},{1,16},{2,19},{3,18},{4,21},{5,20},{6,23},{7,22},{8,25},{9,... | collective-permute-start | bytes 393224 | tf_op jit(solution)/shard_map/ppermute | solution.py:45
  9.1 4.4 %collective-permute-start.3 = (bf16[4,64,256]{2,1,0:T(8,128)(2,1)S(1)}, bf16[4,64,256]{2,1,0:T(8,128)(2,1)S(1)}, u32[]{:S(2)}, u32[]{:S(2)}) collective-permute-start(bf16[4,64,256]{2,1,0:T(8,128)(2,1)S(1)} %get-tuple-element.56), channel_id=1, source_target_pairs={{0,1},{1,0},{2,3},{3,2},{4,5},{5,4},{6,7},{7,6},{8,9},{9,8},{10,11... | collective-permute-start | bytes 393224 | tf_op jit(solution)/shard_map/ppermute | solution.py:45
  13.6 7.9 %collective-permute-start.6 = (bf16[2,8,64,256]{3,2,1,0:T(8,128)(2,1)S(1)}, bf16[2,8,64,256]{3,2,1,0:T(8,128)(2,1)S(1)}, u32[]{:S(2)}, u32[]{:S(2)}) collective-permute-start(bf16[2,8,64,256]{3,2,1,0:T(8,128)(2,1)S(1)} %pad_maximum_fusion.3.even), channel_id=1, source_target_pairs={{0,8},{1,9},{2,10},{3,11},{4,12},{5,13},{6,14},{7,15},{8,0},{9,1},... | collective-permute-start | bytes 1572872 | tf_op jit(solution)/shard_map/ppermute | solution.py:45
  17.3 4.2 %copy-start.8 = (bf16[512,1024]{1,0:T(8,128)(2,1)}, bf16[512,1024]{1,0:T(8,128)(2,1)S(1)}, u32[]{:S(2)}) copy-start(bf16[512,1024]{1,0:T(8,128)(2,1)S(1)} %fusion.2.normed.refs_2_) | copy-start | bytes 3145732
  17.3 35.9 %collective-permute-start.7 = (bf16[512,1024]{1,0:T(8,128)(2,1)S(1)}, bf16[512,1024]{1,0:T(8,128)(2,1)}, u32[]{:S(2)}, u32[]{:S(2)}) collective-permute-start(bf16[512,1024]{1,0:T(8,128)(2,1)S(1)} %fusion.2.normed.refs_2_), channel_id=1, source_target_pairs={{0,1},{2,3},{4,5},{6,7},{8,9},{10,11},{12,13},{14,15},{16,17},{18,... | collective-permute-start | bytes 3145736 | tf_op jit(solution)/shard_map/ppermute | solution.py:540
  21.5 9.0 %copy-start.11 = (bf16[256,192]{0,1:T(8,128)(2,1)S(1)}, bf16[256,192]{0,1:T(8,128)(2,1)}, u32[]{:S(2)}) copy-start(bf16[256,192]{0,1:T(8,128)(2,1)} %param.14) | copy-start | bytes 294916
  21.5 9.0 %copy-start.12 = (bf16[256,64]{0,1:T(8,128)(2,1)S(1)}, bf16[256,64]{0,1:T(8,128)(2,1)}, u32[]{:S(2)}) copy-start(bf16[256,64]{0,1:T(8,128)(2,1)} %param.15) | copy-start | bytes 98308
  21.5 9.1 %copy-start.14 = (s32[512,2]{0,1:T(2,128)S(1)}, s32[512,2]{0,1:T(2,128)}, u32[]{:S(2)}) copy-start(s32[512,2]{0,1:T(2,128)} %param.21) | copy-start | bytes 12292
  24.4 28.8 %all-to-all-start = ((bf16[8,64,512]{2,1,0:T(8,128)(2,1)}), bf16[8,64,512]{2,1,0:T(8,128)(2,1)S(1)}, u32[]{:S(2)}, u32[]{:S(2)}) async-start(bf16[8,64,512]{2,1,0:T(8,128)(2,1)} %project_queries.1.refs_1_), calls=%async_computation | async-start | bytes 1048576 | tf_op jit(solution)/shard_map/all_to_all | solution.py:528
  30.6 11.7 %collective-permute-start.8 = (bf16[192,256]{1,0:T(8,128)(2,1)S(1)}, bf16[192,256]{1,0:T(8,128)(2,1)}, u32[]{:S(2)}, u32[]{:S(2)}) collective-permute-start(bf16[192,256]{1,0:T(8,128)(2,1)S(1)} %pad_maximum_fusion.8), channel_id=1, source_target_pairs={{0,2},{1,3},{2,0},{3,1},{4,6},{5,7},{6,4},{7,5},{8,10},{9,11},{10,... | collective-permute-start | bytes 294920 | tf_op jit(solution)/shard_map/ppermute | solution.py:45
  30.8 17.7 %collective-permute-start.9 = (bf16[192,256]{1,0:T(8,128)(2,1)S(1)}, bf16[192,256]{1,0:T(8,128)(2,1)}, u32[]{:S(2)}, u32[]{:S(2)}) collective-permute-start(bf16[192,256]{1,0:T(8,128)(2,1)S(1)} %pad_maximum_fusion.8), channel_id=1, source_target_pairs={{0,4},{1,5},{2,6},{3,7},{4,0},{5,1},{6,2},{7,3},{8,12},{9,13},{10,... | collective-permute-start | bytes 294920 | tf_op jit(solution)/shard_map/ppermute | solution.py:45
  33.0 19.1 %collective-permute-start.10 = (bf16[192,256]{1,0:T(8,128)(2,1)S(1)}, bf16[192,256]{1,0:T(8,128)(2,1)}, u32[]{:S(2)}, u32[]{:S(2)}) collective-permute-start(bf16[192,256]{1,0:T(8,128)(2,1)S(1)} %pad_maximum_fusion.8), channel_id=1, source_target_pairs={{0,6},{1,7},{2,4},{3,5},{4,2},{5,3},{6,0},{7,1},{8,14},{9,15},{10,... | collective-permute-start | bytes 294920 | tf_op jit(solution)/shard_map/ppermute | solution.py:45
  34.6 21.4 %copy-start.4 = (s32[4]{0:T(128)S(1)}, s32[4]{0:T(128)}, u32[]{:S(2)}) copy-start(s32[4]{0:T(128)} %lengths.1) | copy-start | bytes 52
  34.6 21.4 %copy-start.5 = (s32[1,128]{1,0:T(1,128)S(1)}, s32[1,128]{1,0:T(1,128)}, u32[]{:S(2)}) copy-start(s32[1,128]{1,0:T(1,128)} %table.1) | copy-start | bytes 1540
  53.2 11.2 %collective-permute-start.11 = (bf16[4,192,256]{2,1,0:T(8,128)(2,1)S(1)}, bf16[4,192,256]{2,1,0:T(8,128)(2,1)S(1)}, u32[]{:S(2)}, u32[]{:S(2)}) collective-permute-start(bf16[4,192,256]{2,1,0:T(8,128)(2,1)S(1)} %pad_maximum_fusion.4), channel_id=1, source_target_pairs={{0,1},{1,0},{2,3},{3,2},{4,5},{5,4},{6,7},{7,6},{8,9},{9,8},{10,11... | collective-permute-start | bytes 1179656 | tf_op jit(solution)/shard_map/ppermute | solution.py:45
  54.5 10.1 %collective-permute-start.12 = (bf16[4,192,256]{2,1,0:T(8,128)(2,1)S(1)}, bf16[4,192,256]{2,1,0:T(8,128)(2,1)S(1)}, u32[]{:S(2)}, u32[]{:S(2)}) collective-permute-start(bf16[4,192,256]{2,1,0:T(8,128)(2,1)S(1)} %pad_maximum_fusion.4), channel_id=1, source_target_pairs={{0,16},{1,17},{2,18},{3,19},{4,20},{5,21},{6,22},{7,23},{8,24},{9,... | collective-permute-start | bytes 1179656 | tf_op jit(solution)/shard_map/ppermute | solution.py:45
  55.7 16.5 %collective-permute-start.13 = (bf16[4,192,256]{2,1,0:T(8,128)(2,1)S(1)}, bf16[4,192,256]{2,1,0:T(8,128)(2,1)S(1)}, u32[]{:S(2)}, u32[]{:S(2)}) collective-permute-start(bf16[4,192,256]{2,1,0:T(8,128)(2,1)S(1)} %pad_maximum_fusion.4), channel_id=1, source_target_pairs={{0,17},{1,16},{2,19},{3,18},{4,21},{5,20},{6,23},{7,22},{8,25},{9,... | collective-permute-start | bytes 1179656 | tf_op jit(solution)/shard_map/ppermute | solution.py:45
  56.0 16.6 %collective-permute-start.14 = (bf16[160,1024]{1,0:T(8,128)(2,1)S(1)}, bf16[160,1024]{1,0:T(8,128)(2,1)S(1)}, u32[]{:S(2)}, u32[]{:S(2)}) collective-permute-start(bf16[160,1024]{1,0:T(8,128)(2,1)S(1)} %dispatch.1), channel_id=1, source_target_pairs={{0,4},{1,5},{2,6},{3,7},{4,0},{5,1},{6,2},{7,3},{8,12},{9,13},{10,... | collective-permute-start | bytes 983048 | tf_op jit(solution)/shard_map/ppermute | solution.py:45
  72.5 7.5 %copy-start.7 = (bf16[2,8,192,256]{3,2,1,0:T(8,128)(2,1)}, bf16[2,8,192,256]{3,2,1,0:T(8,128)(2,1)S(1)}, u32[]{:S(2)}) copy-start(bf16[2,8,192,256]{3,2,1,0:T(8,128)(2,1)S(1)} %pad_maximum_fusion.refs_4_) | copy-start | bytes 4718596
  72.5 7.5 %collective-permute-start.15 = (bf16[2,8,192,256]{3,2,1,0:T(8,128)(2,1)S(1)}, bf16[2,8,192,256]{3,2,1,0:T(8,128)(2,1)}, u32[]{:S(2)}, u32[]{:S(2)}) collective-permute-start(bf16[2,8,192,256]{3,2,1,0:T(8,128)(2,1)S(1)} %pad_maximum_fusion.refs_4_), channel_id=1, source_target_pairs={{0,8},{1,9},{2,10},{3,11},{4,12},{5,13},{6,14},{7,15},{8,0},{9,1},... | collective-permute-start | bytes 4718600 | tf_op jit(solution)/shard_map/ppermute | solution.py:45
  74.8 19.1 %all-to-all-start.1 = ((bf16[8,80,512]{2,1,0:T(8,128)(2,1)}), bf16[8,80,512]{2,1,0:T(8,128)(2,1)S(1)}, u32[]{:S(2)}, u32[]{:S(2)}) async-start(bf16[8,80,512]{2,1,0:T(8,128)(2,1)} %cached_attention.1.refs_6_), calls=%async_computation.1 | async-start | bytes 1310720 | tf_op jit(solution)/shard_map/all_to_all | solution.py:565
  80.0 14.8 %copy-start.2 = (f32[1024]{0:T(1024)S(1)}, f32[1024]{0:T(1024)}, u32[]{:S(2)}) copy-start(f32[1024]{0:T(1024)} %param.19) | copy-start | bytes 12292
  94.0 0.8 copy-start.9
  100.8 24.1 %collective-permute-start.16 = (bf16[160,1024]{1,0:T(8,128)(2,1)S(1)}, bf16[160,1024]{1,0:T(8,128)(2,1)S(1)}, u32[]{:S(2)}, u32[]{:S(2)}) collective-permute-start(bf16[160,1024]{1,0:T(8,128)(2,1)S(1)} %get-tuple-element.39), channel_id=1, source_target_pairs={{0,6},{1,7},{2,4},{3,5},{4,2},{5,3},{6,0},{7,1},{8,14},{9,15},{10,... | collective-permute-start | bytes 983048 | tf_op jit(solution)/shard_map/ppermute | solution.py:45
  101.8 20.6 %collective-permute-start.17 = (bf16[160,512]{1,0:T(8,128)(2,1)S(1)}, bf16[160,512]{1,0:T(8,128)(2,1)S(1)}, u32[]{:S(2)}, u32[]{:S(2)}) collective-permute-start(bf16[160,512]{1,0:T(8,128)(2,1)S(1)} %get-tuple-element.40), channel_id=1, source_target_pairs={{0,4},{1,5},{2,6},{3,7},{4,0},{5,1},{6,2},{7,3},{8,12},{9,13},{10,... | collective-permute-start | bytes 491528 | tf_op jit(solution)/shard_map/ppermute | solution.py:45
  104.9 35.5 %collective-permute-start.20 = (bf16[160,1024]{1,0:T(8,128)(2,1)}, bf16[160,1024]{1,0:T(8,128)(2,1)S(1)}, u32[]{:S(2)}, u32[]{:S(2)}) collective-permute-start(bf16[160,1024]{1,0:T(8,128)(2,1)} %get-tuple-element.44), channel_id=1, source_target_pairs={{0,1},{1,0},{2,3},{3,2},{4,5},{5,4},{6,7},{7,6},{8,9},{9,8},{10,11... | collective-permute-start | bytes 983048 | tf_op jit(solution)/shard_map/ppermute | solution.py:45
  106.1 36.6 %collective-permute-start.21 = (bf16[160,1024]{1,0:T(8,128)(2,1)}, bf16[160,1024]{1,0:T(8,128)(2,1)S(1)}, u32[]{:S(2)}, u32[]{:S(2)}) collective-permute-start(bf16[160,1024]{1,0:T(8,128)(2,1)} %get-tuple-element.45), channel_id=1, source_target_pairs={{0,2},{1,3},{2,0},{3,1},{4,6},{5,7},{6,4},{7,5},{8,10},{9,11},{10,... | collective-permute-start | bytes 983048 | tf_op jit(solution)/shard_map/ppermute | solution.py:45
  106.1 36.6 %collective-permute-start.22 = (bf16[160,1024]{1,0:T(8,128)(2,1)}, bf16[160,1024]{1,0:T(8,128)(2,1)S(1)}, u32[]{:S(2)}, u32[]{:S(2)}) collective-permute-start(bf16[160,1024]{1,0:T(8,128)(2,1)} %get-tuple-element.46), channel_id=1, source_target_pairs={{0,3},{1,2},{2,1},{3,0},{4,7},{5,6},{6,5},{7,4},{8,11},{9,10},{10,... | collective-permute-start | bytes 983048 | tf_op jit(solution)/shard_map/ppermute | solution.py:45
  122.3 41.1 %collective-permute-start.26 = (bf16[160,1024]{1,0:T(8,128)(2,1)S(1)}, bf16[160,1024]{1,0:T(8,128)(2,1)S(1)}, u32[]{:S(2)}, u32[]{:S(2)}) collective-permute-start(bf16[160,1024]{1,0:T(8,128)(2,1)S(1)} %get-tuple-element.51), channel_id=1, source_target_pairs={{0,5},{1,4},{2,7},{3,6},{4,1},{5,0},{6,3},{7,2},{8,13},{9,12},{10,... | collective-permute-start | bytes 983048 | tf_op jit(solution)/shard_map/ppermute | solution.py:45
  124.9 39.7 %collective-permute-start.27 = (bf16[160,1024]{1,0:T(8,128)(2,1)S(1)}, bf16[160,1024]{1,0:T(8,128)(2,1)S(1)}, u32[]{:S(2)}, u32[]{:S(2)}) collective-permute-start(bf16[160,1024]{1,0:T(8,128)(2,1)S(1)} %get-tuple-element.52), channel_id=1, source_target_pairs={{0,7},{1,6},{2,5},{3,4},{4,3},{5,2},{6,1},{7,0},{8,15},{9,14},{10,... | collective-permute-start | bytes 983048 | tf_op jit(solution)/shard_map/ppermute | solution.py:45
  125.4 18.1 %copy-start.6 = (bf16[160,1024]{1,0:T(8,128)(2,1)S(1)}, bf16[160,1024]{1,0:T(8,128)(2,1)}, u32[]{:S(2)}) copy-start(bf16[160,1024]{1,0:T(8,128)(2,1)} %get-tuple-element.43.refs_0_) | copy-start | bytes 983044
  140.4 2.3 %copy-start.3 = (bf16[160,1024]{1,0:T(8,128)(2,1)}, bf16[160,1024]{1,0:T(8,128)(2,1)S(1)}, u32[]{:S(2)}) copy-start(bf16[160,1024]{1,0:T(8,128)(2,1)S(1)} %get-tuple-element.41.refs_7_) | copy-start | bytes 983044
  140.5 38.6 %collective-permute-start.18 = (bf16[160,1024]{1,0:T(8,128)(2,1)S(1)}, bf16[160,1024]{1,0:T(8,128)(2,1)S(1)}, u32[]{:S(2)}, u32[]{:S(2)}) collective-permute-start(bf16[160,1024]{1,0:T(8,128)(2,1)S(1)} %get-tuple-element.41.refs_7_), channel_id=1, source_target_pairs={{0,4},{1,5},{2,6},{3,7},{4,0},{5,1},{6,2},{7,3},{8,12},{9,13},{10,... | collective-permute-start | bytes 983048 | tf_op jit(solution)/shard_map/ppermute | solution.py:45
  142.7 0.7 copy-start.15
  142.7 0.8 copy-start.16
  161.9 25.4 %collective-permute-start.23 = (bf16[160,1024]{1,0:T(8,128)(2,1)S(1)}, bf16[160,1024]{1,0:T(8,128)(2,1)S(1)}, u32[]{:S(2)}, u32[]{:S(2)}) collective-permute-start(bf16[160,1024]{1,0:T(8,128)(2,1)S(1)} %get-tuple-element.48), channel_id=1, source_target_pairs={{0,1},{1,0},{2,3},{3,2},{4,5},{5,4},{6,7},{7,6},{8,9},{9,8},{10,11... | collective-permute-start | bytes 983048 | tf_op jit(solution)/shard_map/ppermute | solution.py:45
  162.4 24.9 %collective-permute-start.24 = (bf16[160,1024]{1,0:T(8,128)(2,1)S(1)}, bf16[160,1024]{1,0:T(8,128)(2,1)S(1)}, u32[]{:S(2)}, u32[]{:S(2)}) collective-permute-start(bf16[160,1024]{1,0:T(8,128)(2,1)S(1)} %get-tuple-element.49), channel_id=1, source_target_pairs={{0,2},{1,3},{2,0},{3,1},{4,6},{5,7},{6,4},{7,5},{8,10},{9,11},{10,... | collective-permute-start | bytes 983048 | tf_op jit(solution)/shard_map/ppermute | solution.py:45
  163.4 26.8 %collective-permute-start.25 = (bf16[160,1024]{1,0:T(8,128)(2,1)S(1)}, bf16[160,1024]{1,0:T(8,128)(2,1)S(1)}, u32[]{:S(2)}, u32[]{:S(2)}) collective-permute-start(bf16[160,1024]{1,0:T(8,128)(2,1)S(1)} %get-tuple-element.50), channel_id=1, source_target_pairs={{0,3},{1,2},{2,1},{3,0},{4,7},{5,6},{6,5},{7,4},{8,11},{9,10},{10,... | collective-permute-start | bytes 983048 | tf_op jit(solution)/shard_map/ppermute | solution.py:45
  164.6 17.4 %collective-permute-start.19 = (bf16[160,1024]{1,0:T(8,128)(2,1)S(1)}, bf16[160,1024]{1,0:T(8,128)(2,1)S(1)}, u32[]{:S(2)}, u32[]{:S(2)}) collective-permute-start(bf16[160,1024]{1,0:T(8,128)(2,1)S(1)} %get-tuple-element.42), channel_id=1, source_target_pairs={{0,6},{1,7},{2,4},{3,5},{4,2},{5,3},{6,0},{7,1},{8,14},{9,15},{10,... | collective-permute-start | bytes 983048 | tf_op jit(solution)/shard_map/ppermute | solution.py:45
  165.0 18.3 %copy-start.10 = (s32[8,512]{0,1:T(8,128)S(1)}, s32[8,512]{0,1:T(8,128)}, u32[]{:S(2)}) copy-start(s32[8,512]{0,1:T(8,128)} %get-tuple-element.62) | copy-start | bytes 49156
  179.0 27.1 %collective-permute-start.28 = (bf16[160,1024]{1,0:T(8,128)(2,1)S(1)}, bf16[160,1024]{1,0:T(8,128)(2,1)S(1)}, u32[]{:S(2)}, u32[]{:S(2)}) collective-permute-start(bf16[160,1024]{1,0:T(8,128)(2,1)S(1)} %get-tuple-element.53), channel_id=1, source_target_pairs={{0,5},{1,4},{2,7},{3,6},{4,1},{5,0},{6,3},{7,2},{8,13},{9,12},{10,... | collective-permute-start | bytes 983048 | tf_op jit(solution)/shard_map/ppermute | solution.py:45
  182.0 33.0 %collective-permute-start.29 = (bf16[160,1024]{1,0:T(8,128)(2,1)S(1)}, bf16[160,1024]{1,0:T(8,128)(2,1)S(1)}, u32[]{:S(2)}, u32[]{:S(2)}) collective-permute-start(bf16[160,1024]{1,0:T(8,128)(2,1)S(1)} %get-tuple-element.54), channel_id=1, source_target_pairs={{0,7},{1,6},{2,5},{3,4},{4,3},{5,2},{6,1},{7,0},{8,15},{9,14},{10,... | collective-permute-start | bytes 983048 | tf_op jit(solution)/shard_map/ppermute | solution.py:45
